TPU v7x, 32 devices: a whole 2x2x4 slice. The times are simulated.
32 devices in a mesh: px: 8 (over z, y), py: 4 (over x, core).
Axes of the slice: x: 2, y: 2, z: 4, core: 2. Of those that a mesh axis runs over, the one named last changes fastest.
Arguments:
- estimate: float32 [512, 512, 128], P('px', 'py'), may hold values from 0.2 to 5
- observed: float32 [512, 512, 128], P('px', 'py'), may hold values from 0.2 to 5
- psf: float32 [32, 32, 32], replicated, as said below
Outputs:
- updated: float32 [512, 512, 128], P('px', 'py')
Inputs may be any that keep to these rules, and one draw needn't show every extreme that they name: `psf`: every entry is positive.
All inputs are finite; a program needn't handle non-finite values.
Results may differ from a plain program's by a relative error of at most 0.00009.
Values sent between devices are 32-bit elements; how exact they have to be, the bound alone decides.
A program may use at most 192 MiB of HBM per device.

v0:
```python
import math

import jax
import jax.numpy as jnp
from jax import lax
from jax.sharding import PartitionSpec as P

NX = 512
NY = 512


penalty_weight = 0.1
smoothing = 0.1


def with_halo(block, sides, width):
    for axis, dim in sides:
        count = lax.axis_size(axis)
        forward = [(i, i + 1) for i in range(count - 1)]
        backward = [(target, source) for source, target in forward]
        low = lax.ppermute(
            lax.slice_in_dim(block, block.shape[dim] - width, None, axis=dim), axis, forward
        )
        high = lax.ppermute(lax.slice_in_dim(block, 0, width, axis=dim), axis, backward)
        block = jnp.concatenate([low, block, high], axis=dim)
    return block


def product(pattern, left, right):
    return jnp.einsum(pattern, left, right, precision=lax.Precision.HIGHEST)


def tables(length):
    indices = jnp.arange(length)
    turns = jnp.remainder(indices[:, None] * indices[None, :], length).astype(jnp.float32) * (
        2.0 * math.pi / length
    )
    return (jnp.cos(turns), jnp.sin(turns))


def offset_tables(offsets, frequency, length):
    turns = jnp.remainder(offsets[:, None] * frequency[None, :], length).astype(jnp.float32) * (
        2.0 * math.pi / length
    )
    return (jnp.cos(turns), jnp.sin(turns))


def complex_apply(real_part, imag_part, cosine, sines, pattern, forward):
    real_cos = product(pattern, real_part, cosine)
    real_sin = product(pattern, real_part, sines)
    imag_cos = product(pattern, imag_part, cosine)
    imag_sin = product(pattern, imag_part, sines)
    if forward:
        return (real_cos + imag_sin, imag_cos - real_sin)
    return (real_cos - imag_sin, imag_cos + real_sin)


def transfer_function(
    kernel, first_index, second_index, depth_share, first_share, second_whole, first_whole, depth
):
    length = kernel.shape[0]
    offsets = jnp.arange(length) - length // 2
    depth_freq = first_index * depth_share + jnp.arange(depth_share)
    first_freq = second_index * first_share + jnp.arange(first_share)
    second_freq = jnp.arange(second_whole)
    cosine, sines = offset_tables(offsets, depth_freq, depth)
    real_part = product("baz,zk->bak", kernel, cosine)
    imag_part = -product("baz,zk->bak", kernel, sines)
    cosine, sines = offset_tables(offsets, first_freq, first_whole)
    real_part, imag_part = complex_apply(real_part, imag_part, cosine, sines, "baz,aj->bzj", True)
    cosine, sines = offset_tables(offsets, second_freq, second_whole)
    real_part, imag_part = complex_apply(real_part, imag_part, cosine, sines, "bzj,bm->zjm", True)
    factor = 1.0 / (first_whole * second_whole * depth)
    return (real_part * factor, imag_part * factor)


def outward_one(spectrum, handler):
    result = handler(lax.all_to_all(spectrum, "py", split_axis=2, concat_axis=3, tiled=True))
    return result


def outward_two(spectrum):
    result = lax.all_to_all(spectrum, "px", split_axis=2, concat_axis=3, tiled=True)
    return result


def homeward_two(spectrum, handler):
    result = handler(lax.all_to_all(spectrum, "px", split_axis=3, concat_axis=2, tiled=True))
    return result


def homeward_one(spectrum, handler):
    result = handler(lax.all_to_all(spectrum, "py", split_axis=3, concat_axis=2, tiled=True))
    return result


def along_first(segment):
    cosine, sines = tables(segment.shape[3])
    real_part, imag_part = complex_apply(segment[0], segment[1], cosine, sines, "bza,ak->zkb", True)
    return jnp.stack([real_part, imag_part])


def inverse_first(segment):
    cosine, sines = tables(segment.shape[2])
    real_part, imag_part = complex_apply(
        segment[0], segment[1], cosine, sines, "zab,ak->bzk", False
    )
    return jnp.stack([real_part, imag_part])


def to_real(segment):
    cosine, sines = tables(segment.shape[2])
    return product("bza,zk->bak", segment[0], cosine) - product("bza,zk->bak", segment[1], sines)


def convolve(volume, transfer_real, transfer_imag, adjoint):
    cosine, sines = tables(volume.shape[2])
    spectrum = jnp.stack(
        [product("baz,zk->bka", volume, cosine), -product("baz,zk->bka", volume, sines)]
    )
    spectrum = outward_one(spectrum, along_first)
    spectrum = outward_two(spectrum)
    cosine_second, sines_second = tables(spectrum.shape[3])
    real_part, imag_part = complex_apply(
        spectrum[0], spectrum[1], cosine_second, sines_second, "zab,bk->zak", True
    )
    signed_imag = -transfer_imag if adjoint else transfer_imag
    weighted_real = real_part * transfer_real - imag_part * signed_imag
    weighted_imag = real_part * signed_imag + imag_part * transfer_real
    real_part, imag_part = complex_apply(
        weighted_real, weighted_imag, cosine_second, sines_second, "zab,bk->zak", False
    )
    spectrum = homeward_two(jnp.stack([real_part, imag_part]), inverse_first)
    return homeward_one(spectrum, to_real)


def backward_depth(flux):
    return flux - jnp.concatenate([jnp.zeros_like(flux[:, :, :1]), flux[:, :, :-1]], 2)


def normalized(slope_rows, slope_cols, slope_depth):
    factor = lax.rsqrt(
        slope_rows * slope_rows
        + slope_cols * slope_cols
        + slope_depth * slope_depth
        + smoothing * smoothing
    )
    return (slope_rows * factor, slope_cols * factor, slope_depth * factor)


def variation(volume):
    row_count = volume.shape[0]
    col_count = volume.shape[1]
    padded = with_halo(volume, (("px", 0), ("py", 1)), 1)
    region = padded[:-1, :-1]
    slope_rows = padded[1:, :-1] - region
    slope_cols = padded[:-1, 1:] - region
    row_global = lax.axis_index("px") * row_count - 1 + jnp.arange(row_count + 1)
    col_global = lax.axis_index("py") * col_count - 1 + jnp.arange(col_count + 1)
    row_valid = ((row_global >= 0) & (row_global <= NX - 2))[:, None, None]
    col_valid = ((col_global >= 0) & (col_global <= NY - 2))[None, :, None]
    slope_rows = jnp.where(row_valid, slope_rows, 0.0)
    slope_cols = jnp.where(col_valid, slope_cols, 0.0)
    slope_depth = jnp.concatenate(
        [region[:, :, 1:] - region[:, :, :-1], jnp.zeros_like(region[:, :, :1])], 2
    )
    flux_rows, flux_cols, flux_depth = normalized(slope_rows, slope_cols, slope_depth)
    divergence = (
        flux_rows[1:, 1:]
        - flux_rows[:-1, 1:]
        + (flux_cols[1:, 1:] - flux_cols[1:, :-1])
        + backward_depth(flux_depth[1:, 1:])
    )
    return divergence


def shards(estimate, observed, psf):
    first_index = lax.axis_index("py")
    second_index = lax.axis_index("px")
    first_size = lax.axis_size("py")
    second_size = lax.axis_size("px")
    second_local, first_local, depth = estimate.shape
    first_whole = first_local * first_size
    second_whole = second_local * second_size
    transfer_real, transfer_imag = transfer_function(
        psf,
        first_index,
        second_index,
        depth // first_size,
        first_whole // second_size,
        second_whole,
        first_whole,
        depth,
    )
    blurred = convolve(estimate, transfer_real, transfer_imag, False)
    quotient = observed / blurred
    correction = convolve(quotient, transfer_real, transfer_imag, True)
    divergence = variation(estimate)
    return estimate * correction / (1.0 - penalty_weight * divergence)


def solution(mesh):
    placed = (P("px", "py", None), P("px", "py", None), P())
    return jax.shard_map(
        shards, mesh=mesh, in_specs=placed, out_specs=P("px", "py", None), check_vma=False
    )
```

profile of v0, /device:TPU:1, one launch (start us, length us, event | category | flops | bytes accessed | tf_op | source)
XLA Modules:
  0.0 2399.5 jit_solution(811326743580848369)
XLA Ops:
  16.9 107.3 %all_to_all.120 = f32[2,64,128,128]{3,1,0,2:T(8,128)} all-to-all(f32[2,64,128,128]{3,1,0,2:T(8,128)S(1)} %copy.82), channel_id=1, replica_groups=mesh['px'=8,'py'=4] {'py'}, dimensions={2} | all-to-all | bytes 16777216 | tf_op jit(solution)/shard_map/all_to_all | solution.py:78
  211.7 16.3 copy.84
  228.0 15.5 reshape.88
  277.4 154.1 %all-to-all-done.1 = f32[8,1,262144]{2,1,0:T(1,128)} async-done(((f32[8,1,262144]{2,1,0:T(1,128)}), f32[8,1,262144]{2,1,0:T(1,128)}, u32[]{:S(2)}, u32[]{:S(2)}) %all-to-all-start.1) | async-done | bytes 8388640 | tf_op jit(solution)/shard_map/all_to_all | solution.py:83
  432.1 26.5 %reduce = f32[8,262144]{1,0:T(8,128)} reduce(f32[8,1,262144]{2,1,0:T(1,128)} %all-to-all-done.1, f32[]{:T(128)} %broadcast.379), dimensions={1}, to_apply=%all_to_all.91.reduce_sub_computation | reduce | bytes 16777220 | tf_op jit(solution)/shard_map/all_to_all | solution.py:83
  458.6 15.6 reshape.89
  552.5 18.0 multiply_subtract_fusion.1
  619.7 16.3 copy.90
  636.0 15.5 reshape.90
  651.5 187.2 %all_to_all.121 = f32[8,1,262144]{2,1,0:T(1,128)} all-to-all(f32[8,1,262144]{2,1,0:T(1,128)} %reshape.90), channel_id=1, replica_groups=mesh['px'=8,'py'=4] {'px'}, dimensions={0} | all-to-all | bytes 16777216 | tf_op jit(solution)/shard_map/all_to_all | solution.py:88
  838.7 26.3 %reduce.1 = f32[8,262144]{1,0:T(8,128)} reduce(f32[8,1,262144]{2,1,0:T(1,128)} %all_to_all.121, f32[]{:T(128)} %broadcast.379), dimensions={1}, to_apply=%all_to_all.94.reduce_sub_computation | reduce | bytes 16777220 | tf_op jit(solution)/shard_map/all_to_all | solution.py:88
  865.0 15.6 reshape.91
  880.6 15.7 copy.142
  976.3 16.3 copy.92
  1007.0 102.4 %all_to_all.122 = f32[4,1,524288]{2,1,0:T(1,128)} all-to-all(f32[4,1,524288]{2,1,0:T(1,128)} %reshape.92), channel_id=1, replica_groups=mesh['px'=8,'py'=4] {'py'}, dimensions={0} | all-to-all | bytes 16777216 | tf_op jit(solution)/shard_map/all_to_all | solution.py:93
  1109.4 28.3 %reduce.2 = f32[4,524288]{1,0:T(4,128)} reduce(f32[4,1,524288]{2,1,0:T(1,128)} %all_to_all.122, f32[]{:T(128)} %broadcast.379), dimensions={1}, to_apply=%all_to_all.97.reduce_sub_computation | reduce | bytes 16777220 | tf_op jit(solution)/shard_map/all_to_all | solution.py:93
  1137.6 16.8 reshape.93
  1206.1 96.9 %all_to_all.123 = f32[2,64,128,128]{3,1,0,2:T(8,128)} all-to-all(f32[2,64,128,128]{3,1,0,2:T(8,128)S(1)} %copy.100), channel_id=1, replica_groups=mesh['px'=8,'py'=4] {'py'}, dimensions={2} | all-to-all | bytes 16777216 | tf_op jit(solution)/shard_map/all_to_all | solution.py:78
  1390.4 16.3 copy.102
  1422.2 188.1 %all_to_all.124 = f32[8,1,262144]{2,1,0:T(1,128)} all-to-all(f32[8,1,262144]{2,1,0:T(1,128)} %reshape.94), channel_id=1, replica_groups=mesh['px'=8,'py'=4] {'px'}, dimensions={0} | all-to-all | bytes 16777216 | tf_op jit(solution)/shard_map/all_to_all | solution.py:83
  1610.2 26.3 %reduce.3 = f32[8,262144]{1,0:T(8,128)} reduce(f32[8,1,262144]{2,1,0:T(1,128)} %all_to_all.124, f32[]{:T(128)} %broadcast.379), dimensions={1}, to_apply=%all_to_all.103.reduce_sub_computation | reduce | bytes 16777220 | tf_op jit(solution)/shard_map/all_to_all | solution.py:83
  1636.5 15.6 reshape.95
  1730.4 17.9 multiply_subtract_fusion
  1797.6 16.3 copy.104
  1829.4 188.5 %all_to_all.125 = f32[8,1,262144]{2,1,0:T(1,128)} all-to-all(f32[8,1,262144]{2,1,0:T(1,128)} %reshape.96), channel_id=1, replica_groups=mesh['px'=8,'py'=4] {'px'}, dimensions={0} | all-to-all | bytes 16777216 | tf_op jit(solution)/shard_map/all_to_all | solution.py:88
  2018.0 26.3 %reduce.4 = f32[8,262144]{1,0:T(8,128)} reduce(f32[8,1,262144]{2,1,0:T(1,128)} %all_to_all.125, f32[]{:T(128)} %broadcast.379), dimensions={1}, to_apply=%all_to_all.106.reduce_sub_computation | reduce | bytes 16777220 | tf_op jit(solution)/shard_map/all_to_all | solution.py:88
  2044.3 15.6 reshape.97
  2155.5 16.3 copy.106
  2209.5 75.4 %collective-permute-done.2 = f32[66,1,128]{2,1,0:T(1,128)S(1)} collective-permute-done((f32[66,1,128]{2,1,0:T(1,128)S(1)}, f32[66,1,128]{2,1,0:T(1,128)S(1)}, u32[]{:S(2)}, u32[]{:S(2)}) %collective-permute-start.2) | collective-permute-done | bytes 33824 | tf_op jit(solution)/shard_map/ppermute | solution.py:21
  2303.9 28.7 %reduce.5 = f32[4,524288]{1,0:T(4,128)} reduce(f32[4,1,524288]{2,1,0:T(1,128)} %all-to-all-done.7, f32[]{:T(128)} %broadcast.379), dimensions={1}, to_apply=%all_to_all.109.reduce_sub_computation | reduce | bytes 16777220 | tf_op jit(solution)/shard_map/all_to_all | solution.py:93
  2332.5 16.8 reshape.99
  2382.6 16.7 fusion.11
  (187 shorter events, 843.0 us)
Async XLA Ops:
  0.0 250.1 %copy-start = (f32[32,32,32]{2,1,0:T(8,128)S(1)}, f32[32,32,32]{2,1,0:T(8,128)}, u32[]{:S(2)}) copy-start(f32[32,32,32]{2,1,0:T(8,128)} %param.5) | copy-start | bytes 393220
  172.3 12.7 copy-start.6
  172.3 12.7 copy-start.21
  185.0 11.1 copy-start.4
  243.5 188.1 %all-to-all-start.1 = ((f32[8,1,262144]{2,1,0:T(1,128)}), f32[8,1,262144]{2,1,0:T(1,128)}, u32[]{:S(2)}, u32[]{:S(2)}) async-start(f32[8,1,262144]{2,1,0:T(1,128)} %reshape.88), calls=%async_computation.1 | async-start | bytes 16777216 | tf_op jit(solution)/shard_map/all_to_all | solution.py:83
  525.6 14.5 copy-start.14
  525.6 14.5 copy-start.27
  540.1 12.4 copy-start.8
  540.1 12.4 copy-start.10
  540.1 12.4 copy-start.13
  910.1 14.5 copy-start.16
  944.2 12.9 copy-start.17
  957.2 11.3 copy-start.25
  1350.8 12.7 copy-start.7
  1350.8 12.7 copy-start.22
  1363.4 11.2 copy-start.5
  1703.3 14.9 copy-start.15
  1703.3 14.9 copy-start.28
  1718.2 12.3 copy-start.9
  1718.2 12.3 copy-start.11
  1718.2 12.3 copy-start.12
  2089.1 14.5 copy-start.18
  2123.5 12.9 copy-start.19
  2136.4 11.1 copy-start.26
  2186.2 117.6 %all-to-all-start.7 = ((f32[4,1,524288]{2,1,0:T(1,128)}), f32[4,1,524288]{2,1,0:T(1,128)}, u32[]{:S(2)}, u32[]{:S(2)}) async-start(f32[4,1,524288]{2,1,0:T(1,128)} %reshape.98), calls=%async_computation.7 | async-start | bytes 16777216 | tf_op jit(solution)/shard_map/all_to_all | solution.py:93
  2194.8 4.1 collective-permute-start
  2197.5 5.4 collective-permute-start.1
  2203.0 81.9 %collective-permute-start.2 = (f32[66,1,128]{2,1,0:T(1,128)S(1)}, f32[66,1,128]{2,1,0:T(1,128)S(1)}, u32[]{:S(2)}, u32[]{:S(2)}) collective-permute-start(f32[66,1,128]{2,1,0:T(1,128)S(1)} %get-tuple-element.31), channel_id=1, source_target_pairs={{0,1},{1,2},{2,3},{4,5},{5,6},{6,7},{8,9},{9,10},{10,11},{12,13},{... | collective-permute-start | bytes 101384 | tf_op jit(solution)/shard_map/ppermute | solution.py:21
  2207.6 79.1 %collective-permute-start.3 = (f32[66,1,128]{2,1,0:T(1,128)S(1)}, f32[66,1,128]{2,1,0:T(1,128)S(1)}, u32[]{:S(2)}, u32[]{:S(2)}) collective-permute-start(f32[66,1,128]{2,1,0:T(1,128)S(1)} %get-tuple-element.30), channel_id=1, source_target_pairs={{1,0},{2,1},{3,2},{5,4},{6,5},{7,6},{9,8},{10,9},{11,10},{13,12},{... | collective-permute-start | bytes 101384 | tf_op jit(solution)/shard_map/ppermute | solution.py:24
  2369.6 11.9 slice-start
  2370.2 11.4 slice-start.1
  2382.6 16.7 copy-start.1
  (7 other events, 27.5 us)
where the time goes:
time: 2410 us; the launch traced here: 2400 us
  blocking collectives  870 us (36%)
  local copies, waits for them, and re-layouts  565 us (23%)
  matrix products  495 us (21%)
  waiting for transfers between devices  231 us (10%)
  other arithmetic  212 us (9%)
  starting transfers between devices  24.7 us (1%)
    dot_general x42, matrix products, product(): return jnp.einsum(pattern, left, right, precision=lax.Precision.HIGHEST)  393 us
    all_to_all x2, blocking collectives, homeward_two(): lax.all_to_all(spectrum, 'px', split_axis=3, concat_axis=2, tiled=True)  376 us
    all_to_all x2, blocking collectives, outward_one(): lax.all_to_all(spectrum, 'py', split_axis=2, concat_axis=3, tiled=True)  204 us
    unnamed x80, local copies, waits for them, and re-layouts  196 us
    all_to_all x1, blocking collectives, outward_two(): lax.all_to_all(spectrum, 'px', split_axis=2, concat_axis=3, tiled=True)  188 us
    all_to_all x1, waiting for transfers between devices, outward_two(): lax.all_to_all(spectrum, 'px', split_axis=2, concat_axis=3, tiled=True)  154 us
    all_to_all x1, blocking collectives, homeward_one(): lax.all_to_all(spectrum, 'py', split_axis=3, concat_axis=2, tiled=True)  102 us
    unnamed x8, matrix products  102 us
  transfers between devices with their start and end apart: 6, of which 4 were waited for; matrix products, arithmetic and copies ran while one was open for 2% of the time, Pallas kernels for 0%

commit v1 on v0

v1 whole, which is shorter than its diff:
```python
import functools
import math

import jax
import jax.numpy as jnp
import ml_dtypes
import numpy as np
from jax import lax
from jax.experimental import pallas as pl
from jax.experimental.pallas import tpu as pltpu
from jax.sharding import PartitionSpec as P

penalty_weight = 0.1
smoothing = 0.1

LANES = 128
ROWS = 8
VMEM_LIMIT = 48 * 1024 * 1024


def halves(table):
    table = np.asarray(table, np.float64).astype(np.float32)
    high = table.astype(ml_dtypes.bfloat16)
    low = (table - high.astype(np.float32)).astype(ml_dtypes.bfloat16)
    return np.stack([high, low])


def waves(left, right, length):
    turns = np.remainder(np.outer(left, right), length) * (2.0 * math.pi / length)
    return np.cos(turns), np.sin(turns)


def up16(count):
    return -(-count // 16) * 16


def split(value):
    high = value.astype(jnp.bfloat16)
    low = (value - high.astype(jnp.float32)).astype(jnp.bfloat16)
    return high, low


def dot(left, right, dims):
    return lax.dot_general(left, right, (dims, ((), ())), preferred_element_type=jnp.float32)


def by_table(value, table, dims=((1,), (0,))):
    high, low = split(value)
    return dot(high, table[0], dims) + (dot(low, table[0], dims) + dot(high, table[1], dims))


def table_by(table, value, dims=((1,), (0,))):
    high, low = split(value)
    return dot(table[0], high, dims) + (dot(table[0], low, dims) + dot(table[1], high, dims))


class Plan:
    def __init__(self, rows, cols, depth, edge):
        half = edge // 2
        self.rows, self.cols, self.depth, self.edge, self.half = rows, cols, depth, edge, half
        self.row_whole = rows + edge
        self.col_whole = cols + edge
        self.modes = depth // 2 + 1
        self.mode_pad = up16(self.modes)
        modes = np.arange(self.modes)

        cosine, sine = waves(modes, np.arange(depth), depth)
        table = np.zeros((2 * self.mode_pad, depth))
        table[: self.modes] = cosine
        table[self.mode_pad : self.mode_pad + self.modes] = -sine
        self.depth_out = halves(table)
        weight = np.where((modes == 0) | (2 * modes == depth), 1.0, 2.0)
        weight = weight / (depth * self.row_whole * self.col_whole)
        table = np.zeros((self.mode_pad, 2 * depth))
        table[: self.modes, :depth] = cosine * weight[:, None]
        table[: self.modes, depth:] = -sine * weight[:, None]
        self.depth_home = halves(table)

        freq = np.arange(self.row_whole)
        place = np.concatenate([np.arange(rows + half), np.arange(-half, 0)])
        cosine, sine = waves(place, freq, self.row_whole)
        self.rows_out = halves(self.lane_table(cosine, -sine, LANES, LANES))
        cosine, sine = waves(freq, np.arange(rows), self.row_whole)
        self.rows_home = halves(self.lane_table(cosine, sine, LANES, rows))
        offset = np.arange(edge) - half
        cosine, sine = waves(offset, freq, self.row_whole)
        self.rows_psf = halves(self.lane_table(cosine, -sine, LANES, LANES))

        freq = np.arange(self.col_whole)
        place = np.concatenate([np.arange(cols + half), np.arange(-half, 0)])
        self.cols_out = halves(np.concatenate(waves(freq, place, self.col_whole)))
        self.cols_home = halves(np.concatenate(waves(np.arange(cols), freq, self.col_whole)))
        self.cols_psf = halves(np.concatenate(waves(freq, offset, self.col_whole)))

    @staticmethod
    def lane_table(real_part, imag_part, left, right):
        table = np.zeros((2 * left, 2 * right))
        height, width = real_part.shape
        table[:height, :width] = real_part
        table[:height, right : right + width] = imag_part
        table[left : left + height, :width] = -imag_part
        table[left : left + height, right : right + width] = real_part
        return table


def whole_spec(array):
    return pl.BlockSpec(array.shape, lambda i: (0,) * array.ndim)


def params():
    return pltpu.CompilerParams(
        dimension_semantics=("arbitrary",), vmem_limit_bytes=VMEM_LIMIT
    )


def cost(flops, moved):
    return pl.CostEstimate(flops=int(flops), bytes_accessed=int(moved), transcendentals=0)


def depth_out_kernel(plan, volume_ref, table_ref, out_ref):
    pad = jnp.zeros((LANES - plan.row_whole, plan.depth), jnp.float32)
    for j in range(ROWS):
        slab = volume_ref[:, j, :]
        if plan.row_whole < LANES:
            slab = jnp.concatenate([slab, pad], 0)
        result = table_by(table_ref, slab, ((1,), (1,)))
        out_ref[:, j, :LANES] = result[: plan.modes]
        out_ref[:, j, LANES:] = result[plan.mode_pad : plan.mode_pad + plan.modes]


def depth_out(plan, volume):
    return pl.pallas_call(
        functools.partial(depth_out_kernel, plan),
        grid=(plan.col_whole // ROWS,),
        in_specs=[
            pl.BlockSpec((plan.row_whole, ROWS, plan.depth), lambda i: (0, i, 0)),
            whole_spec(plan.depth_out),
        ],
        out_specs=pl.BlockSpec((plan.modes, ROWS, 2 * LANES), lambda i: (0, i, 0)),
        out_shape=jax.ShapeDtypeStruct((plan.modes, plan.col_whole, 2 * LANES), jnp.float32),
        compiler_params=params(),
        cost_estimate=cost(3e9, 2e7),
        name="depth_out",
    )(volume, plan.depth_out)


def turned(table, value, forward):
    both = table_by(table, value)
    half = both.shape[0] // 2
    cos_real, cos_imag = both[:half, :LANES], both[:half, LANES:]
    sin_real, sin_imag = both[half:, :LANES], both[half:, LANES:]
    if forward:
        return cos_real + sin_imag, cos_imag - sin_real
    return cos_real - sin_imag, cos_imag + sin_real


def transfer_kernel(psf_ref, rows_ref, cols_ref, out_ref):
    for j in range(out_ref.shape[0]):
        value = by_table(psf_ref[j], rows_ref)
        real_part, imag_part = turned(cols_ref, value, True)
        out_ref[j, :, :LANES] = real_part
        out_ref[j, :, LANES:] = imag_part


def step_of(modes):
    return max(size for size in range(1, 6) if modes % size == 0)


def transfer(plan, psf):
    edge = plan.edge
    offset = np.arange(edge) - plan.half
    cosine, sine = waves(offset, np.arange(plan.modes), plan.depth)
    parts = [
        jnp.einsum(
            "abc,ck->kba",
            psf,
            jnp.asarray(table, jnp.float32),
            precision=lax.Precision.HIGHEST,
        )
        for table in (cosine, -sine)
    ]
    parts = [jnp.pad(part, ((0, 0), (0, 0), (0, LANES - edge))) for part in parts]
    modes = jnp.concatenate(parts, 2)
    step = step_of(plan.modes)
    return pl.pallas_call(
        transfer_kernel,
        grid=(plan.modes // step,),
        in_specs=[
            pl.BlockSpec((step, edge, 2 * LANES), lambda i: (i, 0, 0)),
            whole_spec(plan.rows_psf),
            whole_spec(plan.cols_psf),
        ],
        out_specs=pl.BlockSpec((step, plan.col_whole, 2 * LANES), lambda i: (i, 0, 0)),
        out_shape=jax.ShapeDtypeStruct((plan.modes, plan.col_whole, 2 * LANES), jnp.float32),
        compiler_params=params(),
        cost_estimate=cost(9e9, 1.4e7),
        name="transfer",
    )(modes, plan.rows_psf, plan.cols_psf)


def filter_kernel(adjoint, modes_ref, transfer_ref, rows_out, cols_out, cols_home, rows_home, out_ref):
    for j in range(out_ref.shape[0]):
        value = by_table(modes_ref[j], rows_out)
        real_part, imag_part = turned(cols_out, value, True)
        gain_real = transfer_ref[j, :, :LANES]
        gain_imag = transfer_ref[j, :, LANES:]
        if adjoint:
            gain_imag = -gain_imag
        value = jnp.concatenate(
            [
                real_part * gain_real - imag_part * gain_imag,
                real_part * gain_imag + imag_part * gain_real,
            ],
            1,
        )
        value = jnp.concatenate(turned(cols_home, value, False), 1)
        out_ref[j] = by_table(value, rows_home)


def filtered(plan, modes, gains, adjoint):
    step = step_of(plan.modes)
    block = pl.BlockSpec((step, plan.col_whole, 2 * LANES), lambda i: (i, 0, 0))
    tables = [plan.rows_out, plan.cols_out, plan.cols_home, plan.rows_home]
    return pl.pallas_call(
        functools.partial(filter_kernel, adjoint),
        grid=(plan.modes // step,),
        in_specs=[block, block] + [whole_spec(table) for table in tables],
        out_specs=pl.BlockSpec((step, plan.cols, 2 * plan.rows), lambda i: (i, 0, 0)),
        out_shape=jax.ShapeDtypeStruct((plan.modes, plan.cols, 2 * plan.rows), jnp.float32),
        compiler_params=params(),
        cost_estimate=cost(2.2e10, 2.5e7),
        name="filtered",
    )(modes, gains, *tables)


def depth_home_kernel(plan, divide, modes_ref, other_ref, table_ref, out_ref):
    pad = jnp.zeros((plan.mode_pad - plan.modes, 2 * plan.rows), jnp.float32)
    for j in range(ROWS):
        slab = jnp.concatenate([modes_ref[:, j, :], pad], 0).T
        both = by_table(slab, table_ref)
        result = both[: plan.rows, : plan.depth] + both[plan.rows :, plan.depth :]
        other = other_ref[:, j, :]
        out_ref[:, j, :] = other / result if divide else other * result


def depth_home(plan, modes, other, divide):
    block = pl.BlockSpec((plan.rows, ROWS, plan.depth), lambda i: (0, i, 0))
    return pl.pallas_call(
        functools.partial(depth_home_kernel, plan, divide),
        grid=(plan.cols // ROWS,),
        in_specs=[
            pl.BlockSpec((plan.modes, ROWS, 2 * plan.rows), lambda i: (0, i, 0)),
            block,
            whole_spec(plan.depth_home),
        ],
        out_specs=block,
        out_shape=jax.ShapeDtypeStruct((plan.rows, plan.cols, plan.depth), jnp.float32),
        compiler_params=params(),
        cost_estimate=cost(3e9, 1.3e7),
        name="depth_home",
    )(modes, other, plan.depth_home)


def with_halo(block, width):
    row_count = lax.axis_size("px")
    col_count = lax.axis_size("py")
    devices = [(i, j) for i in range(row_count) for j in range(col_count)]

    def part(size, side):
        return {0: slice(None), 1: slice(0, width), -1: slice(size - width, size)}[side]

    def fetch(row_side, col_side):
        piece = block[part(block.shape[0], row_side), part(block.shape[1], col_side)]
        if row_side == 0 and col_side == 0:
            return piece
        pairs = [
            (
                ((i + row_side) % row_count) * col_count + (j + col_side) % col_count,
                i * col_count + j,
            )
            for i, j in devices
        ]
        return lax.ppermute(piece, ("px", "py"), pairs)

    sides = (0, 1, -1)
    return jnp.concatenate(
        [jnp.concatenate([fetch(row, col) for col in sides], 1) for row in sides], 0
    )


def variation(padded, row_count, col_count, row_whole, col_whole):
    region = padded[:-1, :-1]
    row_global = lax.axis_index("px") * row_count - 1 + jnp.arange(row_count + 1)
    col_global = lax.axis_index("py") * col_count - 1 + jnp.arange(col_count + 1)
    row_valid = ((row_global >= 0) & (row_global <= row_whole - 2))[:, None, None]
    col_valid = ((col_global >= 0) & (col_global <= col_whole - 2))[None, :, None]
    slope_rows = jnp.where(row_valid, padded[1:, :-1] - region, 0.0)
    slope_cols = jnp.where(col_valid, padded[:-1, 1:] - region, 0.0)
    slope_depth = jnp.concatenate(
        [region[:, :, 1:] - region[:, :, :-1], jnp.zeros_like(region[:, :, :1])], 2
    )
    factor = lax.rsqrt(
        slope_rows * slope_rows
        + slope_cols * slope_cols
        + slope_depth * slope_depth
        + smoothing * smoothing
    )
    flux_rows = slope_rows * factor
    flux_cols = slope_cols * factor
    flux_depth = (slope_depth * factor)[1:, 1:]
    before = jnp.concatenate([jnp.zeros_like(flux_depth[:, :, :1]), flux_depth[:, :, :-1]], 2)
    return (
        flux_rows[1:, 1:]
        - flux_rows[:-1, 1:]
        + (flux_cols[1:, 1:] - flux_cols[1:, :-1])
        + (flux_depth - before)
    )


def ring(padded, rows, cols):
    padded = jnp.concatenate([padded[-1:], padded[: rows + 1]], 0)
    return jnp.concatenate([padded[:, -1:], padded[:, : cols + 1]], 1)


def shards(estimate, observed, psf):
    rows, cols, depth = estimate.shape
    plan = Plan(rows, cols, depth, psf.shape[0])
    gains = transfer(plan, psf)
    padded = with_halo(estimate, plan.half)
    modes = filtered(plan, depth_out(plan, padded), gains, False)
    quotient = depth_home(plan, modes, observed, True)
    divergence = variation(
        ring(padded, rows, cols),
        rows,
        cols,
        rows * lax.axis_size("px"),
        cols * lax.axis_size("py"),
    )
    weight = estimate / (1.0 - penalty_weight * divergence)
    modes = filtered(plan, depth_out(plan, with_halo(quotient, plan.half)), gains, True)
    return depth_home(plan, modes, weight, False)


def solution(mesh):
    placed = (P("px", "py", None), P("px", "py", None), P())
    return jax.shard_map(
        shards, mesh=mesh, in_specs=placed, out_specs=P("px", "py", None), check_vma=False
    )
```

time: 2410 us -> 360 us (0.15)
  blocking collectives: 870 us -> 0 us
  local copies, waits for them, and re-layouts: 565 us -> 29.5 us
  matrix products: 495 us -> 1.91 us
  Pallas kernels: 0 us -> 225 us
  waiting for transfers between devices: 231 us -> 23.4 us
  other arithmetic: 212 us -> 43.8 us
    all_to_all x6 -> x0, blocking collectives: 870 us -> none  [the longest x2 376 us: homeward_two(): lax.all_to_all(spectrum, 'px', split_axis=3, concat_axis=2, tiled=True)]
    dot_general x42 -> x2, matrix products: 393 us -> 1.91 us  [transfer(): jnp.einsum('abc,ck->kba', psf, jnp.asarray(table, jnp.float32), precision...]
    pallas_call x0 -> x7, Pallas kernels: none -> 225 us  [the longest x2 132 us: filtered(): pl.pallas_call(functools.partial(filter_kernel, adjoint), grid=(plan.mode...]
    unnamed x80 -> x50, local copies, waits for them, and re-layouts: 196 us -> 12.1 us
    all_to_all x6 -> x0, other arithmetic: 162 us -> none  [the longest x2 56.9 us: homeward_one(): lax.all_to_all(spectrum, 'py', split_axis=3, concat_axis=2, tiled=True)]
    all_to_all x2 -> x0, waiting for transfers between devices: 154 us -> none  [the longest x1 154 us: outward_two(): lax.all_to_all(spectrum, 'px', split_axis=2, concat_axis=3, tiled=True)]
    all_to_all x9 -> x0, local copies, waits for them, and re-layouts: 120 us -> none  [the longest x3 31.3 us: outward_two(): lax.all_to_all(spectrum, 'px', split_axis=2, concat_axis=3, tiled=True)]
    another operation x8 -> x0, local copies, waits for them, and re-layouts: 108 us -> none  [the longest x2 32.6 us: along_first(): return jnp.stack([real_part, imag_part])]
  transfers between devices with their start and end apart: 6 -> 16, of which waited for: 4 -> 5; matrix products, arithmetic and copies ran while one was open for 2% -> 13% of each run, Pallas kernels for 0% -> 5%
where the time goes in v1:
time: 360 us; the launch traced here: 358 us
  Pallas kernels  225 us (62%)
  other arithmetic  43.8 us (12%)
  starting transfers between devices  34.2 us (10%)
  local copies, waits for them, and re-layouts  29.5 us (8%)
  waiting for transfers between devices  23.4 us (6%)
    pallas_call x2, Pallas kernels, filtered(): pl.pallas_call(functools.partial(filter_kernel, adjoint), grid=(plan.mode...  132 us
    pallas_call x2, Pallas kernels, depth_out(): pl.pallas_call(functools.partial(depth_out_kernel, plan), grid=(plan.col_...  42.5 us
    ppermute x16, starting transfers between devices, fetch(): return lax.ppermute(piece, ('px', 'py'), pairs)  34.2 us
    pallas_call x2, Pallas kernels, depth_home(): pl.pallas_call(functools.partial(depth_home_kernel, plan, divide), grid=(...  31.3 us
    ppermute x16, waiting for transfers between devices, fetch(): return lax.ppermute(piece, ('px', 'py'), pairs)  23.4 us
    pallas_call x1, Pallas kernels, transfer(): pl.pallas_call(transfer_kernel, grid=(plan.modes // step,), in_specs=[pl....  19.5 us
    concatenate x2, other arithmetic, with_halo(): jnp.concatenate([jnp.concatenate([fetch(row, col) for col in sides], 1) f...  18.4 us
    unnamed x50, local copies, waits for them, and re-layouts  12.1 us
  transfers between devices with their start and end apart: 16, of which 5 were waited for; matrix products, arithmetic and copies ran while one was open for 13% of the time, Pallas kernels for 5%

profile of v1, /device:TPU:1, one launch (start us, length us, event | category | flops | bytes accessed | tf_op | source)
XLA Modules:
  0.0 358.1 jit_solution(7284075856483875019)
XLA Ops:
  0.0 3.1 fusion.16
  3.1 2.1 collective-permute-start.5
  7.1 2.1 collective-permute-start.6
  9.1 2.9 collective-permute-start.2
  12.1 2.2 fusion.14
  19.0 2.0 copy.14
  21.3 19.5 %transfer.1.transfer_ref = f32[65,160,256]{2,1,0:T(8,128)} custom-call(f32[65,32,256]{2,1,0:T(8,128)S(1)} %select_maximum_fusion.psf_ref, bf16[2,256,256]{2,1,0:T(8,128)(2,1)S(1)} %copy-done.11, bf16[2,320,32]{2,1,0:T(8,128)(2,1)S(1)} %copy-done.12), custom_call_target="tpu_custom_call" | custom-call | flops 8999999488 | bytes 14000000 | tf_op jit(solution)/shard_map/transfer/pallas_call | solution.py:185
  40.9 2.6 constant_dynamic-update-slice_fusion.2
  44.7 4.5 %collective-permute-start.3 = (f32[16,16,128]{2,1,0:T(8,128)S(1)}, f32[16,16,128]{2,1,0:T(8,128)S(1)}, u32[]{:S(2)}, u32[]{:S(2)}) collective-permute-start(f32[16,16,128]{2,1,0:T(8,128)S(1)} %get-tuple-element.21), channel_id=1, source_target_pairs={{5,0},{6,1},{7,2},{4,3},{9,4},{10,5},{11,6},{8,7},{13,8},{14,9},{1... | collective-permute-start | bytes 393224 | tf_op jit(solution)/shard_map/ppermute | solution.py:283
  50.3 5.2 %collective-permute-done.5 = f32[16,128,128]{2,1,0:T(8,128)} collective-permute-done((f32[16,128,128]{2,1,0:T(8,128)}, f32[16,128,128]{2,1,0:T(8,128)}, u32[]{:S(2)}, u32[]{:S(2)}) %collective-permute-start.5) | collective-permute-done | bytes 1048608 | tf_op jit(solution)/shard_map/ppermute | solution.py:283
  55.4 8.7 %collective-permute-start.4 = (f32[16,16,128]{2,1,0:T(8,128)S(1)}, f32[16,16,128]{2,1,0:T(8,128)S(1)}, u32[]{:S(2)}, u32[]{:S(2)}) collective-permute-start(f32[16,16,128]{2,1,0:T(8,128)S(1)} %get-tuple-element.19), channel_id=1, source_target_pairs={{7,0},{4,1},{5,2},{6,3},{11,4},{8,5},{9,6},{10,7},{15,8},{12,9},{1... | collective-permute-start | bytes 393224 | tf_op jit(solution)/shard_map/ppermute | solution.py:283
  67.0 3.4 pad_maximum_fusion.volume_ref
  70.4 21.3 %depth_out.2.modes_ref = f32[65,160,256]{2,1,0:T(8,128)} custom-call(f32[96,160,128]{2,1,0:T(8,128)} %pad_maximum_fusion.volume_ref, bf16[2,160,128]{2,1,0:T(8,128)(2,1)S(1)} %copy-done.7), custom_call_target="tpu_custom_call" | custom-call | flops 3000000000 | bytes 20000000 | tf_op jit(solution)/shard_map/depth_out/pallas_call | solution.py:132
  91.8 65.8 %filtered.2.modes_ref = f32[65,128,128]{2,1,0:T(8,128)S(1)} custom-call(f32[65,160,256]{2,1,0:T(8,128)} %depth_out.2.modes_ref, f32[65,160,256]{2,1,0:T(8,128)} %transfer.1.transfer_ref, bf16[2,256,256]{2,1,0:T(8,128)(2,1)S(1)} %copy-done.9, bf16[2,320,160]{2,1,0:T(8,128)(2,1)S(1)} %copy-done.8, bf16[2,256,160]{2,1,0:T(8,128)(2,1)S(1)} %copy-done.10, ...), custom_call_target="tpu_custom_call" | custom-call | flops 22000001024 | bytes 25000000 | tf_op jit(solution)/shard_map/filtered/pallas_call | solution.py:224
  157.5 2.0 copy-done.5
  159.6 15.6 %depth_home.2 = f32[64,128,128]{2,1,0:T(8,128)S(1)} custom-call(f32[65,128,128]{2,1,0:T(8,128)} %copy-done.5, f32[64,128,128]{2,1,0:T(8,128)} %other_ref.1, bf16[2,80,256]{2,1,0:T(8,128)(2,1)S(1)} %copy-done.6), custom_call_target="tpu_custom_call" | custom-call | flops 3000000000 | bytes 13000000 | tf_op jit(solution)/shard_map/depth_home/pallas_call | solution.py:248
  178.3 5.3 %collective-permute-start.12 = (f32[16,16,128]{2,1,0:T(8,128)S(1)}, f32[16,16,128]{2,1,0:T(8,128)S(1)}, u32[]{:S(2)}, u32[]{:S(2)}) collective-permute-start(f32[16,16,128]{2,1,0:T(8,128)S(1)} %get-tuple-element.16), channel_id=1, source_target_pairs={{7,0},{4,1},{5,2},{6,3},{11,4},{8,5},{9,6},{10,7},{15,8},{12,9},{1... | collective-permute-start | bytes 393224 | tf_op jit(solution)/shard_map/ppermute | solution.py:283
  188.9 4.8 %fusion.9 = (f32[65,129,128]{2,1,0:T(8,128)}, f32[65,129,128]{2,1,0:T(8,128)}) fusion(f32[66,130,128]{2,1,0:T(8,128)S(1)} %fusion.1, pred[65]{0:T(512)(128)(4,1)S(1)} %compare_and_fusion.1, f32[65,129,127]{2,1,0:T(8,128)S(1)} %slice_subtract_fusion, f32[66,160,128]{2,1,0:T(8,128)S(1)} %fusion, pred[129]{0:T(512)(128)(4,1)S(1)} %compare_and_fusion), kind=kLoop, calls=%fused_computation.25 | loop fusion | flops 11806080 | bytes 25725374 | tf_op jit(solution)/shard_map/mul | solution.py:308
  193.7 10.6 %fusion.10 = (f32[65,129,128]{2,1,0:T(8,128)}, f32[65,129,128]{2,1,0:T(8,128)}) fusion(f32[65,129,128]{2,1,0:T(8,128)} %get-tuple-element.6, f32[66,130,128]{2,1,0:T(8,128)} %copy-done.14, f32[66,160,128]{2,1,0:T(8,128)} %copy-done.15, pred[129]{0:T(512)(128)(4,1)S(1)} %compare_and_fusion, f32[65,129,127]{2,1,0:T(8,128)} %copy-done.16), kind=kLoop, calls=%fused_computation.26 | loop fusion | flops 4293120 | bytes 25725308 | tf_op jit(solution)/shard_map/mul | solution.py:309
  204.3 3.0 slice.149
  207.4 2.4 collective-permute-start.10
  209.8 2.6 collective-permute-start.9
  212.4 2.9 collective-permute-done.12
  215.3 7.7 %fusion.7.other_ref = f32[64,128,128]{2,1,0:T(8,128)S(1)} fusion(f32[64,128,128]{2,1,0:T(8,128)} %param.13, f32[65,129,128]{2,1,0:T(8,128)} %get-tuple-element.8, f32[65,129,128]{2,1,0:T(8,128)} %get-tuple-element.7, f32[65,129,128]{2,1,0:T(8,128)S(1)} %bitcast.9, f32[64,128,127]{2,1,0:T(8,128)S(1)} %slice.149), kind=kLoop, calls=%fused_computation.18 | loop fusion | flops 8388608 | bytes 33521664 | tf_op jit(solution)/shard_map/div | solution.py:339
  223.1 2.3 collective-permute-done.8
  225.4 8.7 %collective-permute-done.13 = f32[16,128,128]{2,1,0:T(8,128)} collective-permute-done((f32[16,128,128]{2,1,0:T(8,128)}, f32[16,128,128]{2,1,0:T(8,128)}, u32[]{:S(2)}, u32[]{:S(2)}) %collective-permute-start.13) | collective-permute-done | bytes 1048608 | tf_op jit(solution)/shard_map/ppermute | solution.py:283
  234.1 4.3 %collective-permute-done.10 = f32[16,128,128]{2,1,0:T(8,128)S(1)} collective-permute-done((f32[16,128,128]{2,1,0:T(8,128)S(1)}, f32[16,128,128]{2,1,0:T(8,128)S(1)}, u32[]{:S(2)}, u32[]{:S(2)}) %collective-permute-start.10) | collective-permute-done | bytes 1048608 | tf_op jit(solution)/shard_map/ppermute | solution.py:283
  238.4 15.0 %maximum_maximum_fusion.volume_ref = f32[96,160,128]{2,1,0:T(8,128)} fusion(f32[16,16,128]{2,1,0:T(8,128)S(1)} %collective-permute-done.15, f32[16,16,128]{2,1,0:T(8,128)S(1)} %collective-permute-done.14, f32[16,128,128]{2,1,0:T(8,128)} %collective-permute-done.13, f32[16,16,128]{2,1,0:T(8,128)S(1)} %collective-permute-done.12, ...), kind=kLoop, calls=%fused_computation.1 | loop fusion | flops 15728640 | bytes 15728640 | tf_op jit(solution)/shard_map/concatenate | solution.py:286
  253.4 21.2 %depth_out.3.modes_ref = f32[65,160,256]{2,1,0:T(8,128)} custom-call(f32[96,160,128]{2,1,0:T(8,128)} %maximum_maximum_fusion.volume_ref, bf16[2,160,128]{2,1,0:T(8,128)(2,1)S(1)} %copy-done.7), custom_call_target="tpu_custom_call" | custom-call | flops 3000000000 | bytes 20000000 | tf_op jit(solution)/shard_map/depth_out/pallas_call | solution.py:132
  274.6 65.8 %filtered.3.modes_ref = f32[65,128,128]{2,1,0:T(8,128)S(1)} custom-call(f32[65,160,256]{2,1,0:T(8,128)} %depth_out.3.modes_ref, f32[65,160,256]{2,1,0:T(8,128)} %transfer.1.transfer_ref, bf16[2,256,256]{2,1,0:T(8,128)(2,1)S(1)} %copy-done.9, bf16[2,320,160]{2,1,0:T(8,128)(2,1)S(1)} %copy-done.8, bf16[2,256,160]{2,1,0:T(8,128)(2,1)S(1)} %copy-done.10, ...), custom_call_target="tpu_custom_call" | custom-call | flops 22000001024 | bytes 25000000 | tf_op jit(solution)/shard_map/filtered/pallas_call | solution.py:224
  340.4 2.0 copy-done.4
  342.4 15.7 %depth_home.3 = f32[64,128,128]{2,1,0:T(8,128)} custom-call(f32[65,128,128]{2,1,0:T(8,128)} %copy-done.4, f32[64,128,128]{2,1,0:T(8,128)S(1)} %fusion.7.other_ref, bf16[2,80,256]{2,1,0:T(8,128)(2,1)S(1)} %copy-done.6), custom_call_target="tpu_custom_call" | custom-call | flops 3000000000 | bytes 13000000 | tf_op jit(solution)/shard_map/depth_home/pallas_call | solution.py:248
  (85 shorter events, 20.2 us)
Async XLA Ops:
  0.0 16.1 %copy-start = (f32[32,32,32]{2,1,0:T(8,128)S(1)}, f32[32,32,32]{2,1,0:T(8,128)}, u32[]{:S(2)}) copy-start(f32[32,32,32]{2,1,0:T(8,128)} %param.15) | copy-start | bytes 393220
  0.0 16.1 %copy-start.18 = (f32[32,65,1]{1,0,2:T(8,128)S(1)}, f32[32,65,1]{1,0,2:T(8,128)}, u32[]{:S(2)}) copy-start(f32[32,65,1]{1,0,2:T(8,128)} %constant.74) | copy-start | bytes 24964
  0.0 17.6 %copy-start.19 = (f32[32,65,1]{1,0,2:T(8,128)S(1)}, f32[32,65,1]{1,0,2:T(8,128)}, u32[]{:S(2)}) copy-start(f32[32,65,1]{1,0,2:T(8,128)} %constant.73) | copy-start | bytes 24964
  3.1 52.3 %collective-permute-start.5 = (f32[16,128,128]{2,1,0:T(8,128)}, f32[16,128,128]{2,1,0:T(8,128)}, u32[]{:S(2)}, u32[]{:S(2)}) collective-permute-start(f32[16,128,128]{2,1,0:T(8,128)} %get-tuple-element.24), channel_id=1, source_target_pairs={{28,0},{29,1},{30,2},{31,3},{0,4},{1,5},{2,6},{3,7},{4,8},{5,9},{6... | collective-permute-start | bytes 3145736 | tf_op jit(solution)/shard_map/ppermute | solution.py:283
  7.1 59.8 %collective-permute-start.6 = (f32[16,16,128]{2,1,0:T(8,128)}, f32[16,16,128]{2,1,0:T(8,128)S(1)}, u32[]{:S(2)}, u32[]{:S(2)}) collective-permute-start(f32[16,16,128]{2,1,0:T(8,128)} %get-tuple-element.20), channel_id=1, source_target_pairs={{29,0},{30,1},{31,2},{28,3},{1,4},{2,5},{3,6},{0,7},{5,8},{6,9},{7... | collective-permute-start | bytes 393224 | tf_op jit(solution)/shard_map/ppermute | solution.py:283
  9.1 56.4 %collective-permute-start.2 = (f32[16,128,128]{2,1,0:T(8,128)}, f32[16,128,128]{2,1,0:T(8,128)}, u32[]{:S(2)}, u32[]{:S(2)}) collective-permute-start(f32[16,128,128]{2,1,0:T(8,128)} %get-tuple-element.23), channel_id=1, source_target_pairs={{4,0},{5,1},{6,2},{7,3},{8,4},{9,5},{10,6},{11,7},{12,8},{13,9},{1... | collective-permute-start | bytes 3145736 | tf_op jit(solution)/shard_map/ppermute | solution.py:283
  14.3 29.2 %collective-permute-start = (f32[64,16,128]{2,1,0:T(8,128)}, f32[64,16,128]{2,1,0:T(8,128)}, u32[]{:S(2)}, u32[]{:S(2)}) collective-permute-start(f32[64,16,128]{2,1,0:T(8,128)} %get-tuple-element.18), channel_id=1, source_target_pairs={{1,0},{2,1},{3,2},{0,3},{5,4},{6,5},{7,6},{4,7},{9,8},{10,9},{11,1... | collective-permute-start | bytes 1572872 | tf_op jit(solution)/shard_map/ppermute | solution.py:283
  15.1 6.2 %copy-start.11 = (bf16[2,256,256]{2,1,0:T(8,128)(2,1)S(1)}, bf16[2,256,256]{2,1,0:T(8,128)(2,1)}, u32[]{:S(2)}) copy-start(bf16[2,256,256]{2,1,0:T(8,128)(2,1)} %constant.57.clone.rows_ref) | copy-start | bytes 786436
  15.1 6.2 %copy-start.12 = (bf16[2,320,32]{2,1,0:T(8,128)(2,1)S(1)}, bf16[2,320,32]{2,1,0:T(8,128)(2,1)}, u32[]{:S(2)}) copy-start(bf16[2,320,32]{2,1,0:T(8,128)(2,1)} %constant.58.clone.cols_ref) | copy-start | bytes 122884
  15.1 29.6 %collective-permute-start.1 = (f32[64,16,128]{2,1,0:T(8,128)}, f32[64,16,128]{2,1,0:T(8,128)}, u32[]{:S(2)}, u32[]{:S(2)}) collective-permute-start(f32[64,16,128]{2,1,0:T(8,128)} %get-tuple-element.17), channel_id=1, source_target_pairs={{3,0},{0,1},{1,2},{2,3},{7,4},{4,5},{5,6},{6,7},{11,8},{8,9},{9,10... | collective-permute-start | bytes 1572872 | tf_op jit(solution)/shard_map/ppermute | solution.py:283
  43.5 23.4 %collective-permute-start.7 = (f32[16,16,128]{2,1,0:T(8,128)S(1)}, f32[16,16,128]{2,1,0:T(8,128)S(1)}, u32[]{:S(2)}, u32[]{:S(2)}) collective-permute-start(f32[16,16,128]{2,1,0:T(8,128)S(1)} %copy-done.17), channel_id=1, source_target_pairs={{31,0},{28,1},{29,2},{30,3},{3,4},{0,5},{1,6},{2,7},{7,8},{4,9},{5... | collective-permute-start | bytes 393224 | tf_op jit(solution)/shard_map/ppermute | solution.py:283
  44.7 22.2 %collective-permute-start.3 = (f32[16,16,128]{2,1,0:T(8,128)S(1)}, f32[16,16,128]{2,1,0:T(8,128)S(1)}, u32[]{:S(2)}, u32[]{:S(2)}) collective-permute-start(f32[16,16,128]{2,1,0:T(8,128)S(1)} %get-tuple-element.21), channel_id=1, source_target_pairs={{5,0},{6,1},{7,2},{4,3},{9,4},{10,5},{11,6},{8,7},{13,8},{14,9},{1... | collective-permute-start | bytes 393224 | tf_op jit(solution)/shard_map/ppermute | solution.py:283
  55.4 11.5 %collective-permute-start.4 = (f32[16,16,128]{2,1,0:T(8,128)S(1)}, f32[16,16,128]{2,1,0:T(8,128)S(1)}, u32[]{:S(2)}, u32[]{:S(2)}) collective-permute-start(f32[16,16,128]{2,1,0:T(8,128)S(1)} %get-tuple-element.19), channel_id=1, source_target_pairs={{7,0},{4,1},{5,2},{6,3},{11,4},{8,5},{9,6},{10,7},{15,8},{12,9},{1... | collective-permute-start | bytes 393224 | tf_op jit(solution)/shard_map/ppermute | solution.py:283
  70.4 21.3 %copy-start.8 = (bf16[2,320,160]{2,1,0:T(8,128)(2,1)S(1)}, bf16[2,320,160]{2,1,0:T(8,128)(2,1)}, u32[]{:S(2)}) copy-start(bf16[2,320,160]{2,1,0:T(8,128)(2,1)} %constant.61.clone.cols_out) | copy-start | bytes 614404
  70.4 21.3 %copy-start.9 = (bf16[2,256,256]{2,1,0:T(8,128)(2,1)S(1)}, bf16[2,256,256]{2,1,0:T(8,128)(2,1)}, u32[]{:S(2)}) copy-start(bf16[2,256,256]{2,1,0:T(8,128)(2,1)} %constant.60.clone.rows_out) | copy-start | bytes 786436
  70.4 21.3 %copy-start.10 = (bf16[2,256,160]{2,1,0:T(8,128)(2,1)S(1)}, bf16[2,256,160]{2,1,0:T(8,128)(2,1)}, u32[]{:S(2)}) copy-start(bf16[2,256,160]{2,1,0:T(8,128)(2,1)} %constant.62.clone.cols_home) | copy-start | bytes 491524
  70.4 21.3 %copy-start.13 = (bf16[2,256,128]{2,1,0:T(8,128)(2,1)S(1)}, bf16[2,256,128]{2,1,0:T(8,128)(2,1)}, u32[]{:S(2)}) copy-start(bf16[2,256,128]{2,1,0:T(8,128)(2,1)} %constant.63.clone.rows_home) | copy-start | bytes 393220
  91.8 67.8 %copy-start.6 = (bf16[2,80,256]{2,1,0:T(8,128)(2,1)S(1)}, bf16[2,80,256]{2,1,0:T(8,128)(2,1)}, u32[]{:S(2)}) copy-start(bf16[2,80,256]{2,1,0:T(8,128)(2,1)} %constant.64.clone.table_ref) | copy-start | bytes 245764
  175.2 10.0 %copy-start.2 = (f32[64,128,128]{2,1,0:T(8,128)}, f32[64,128,128]{2,1,0:T(8,128)S(1)}, u32[]{:S(2)}) copy-start(f32[64,128,128]{2,1,0:T(8,128)S(1)} %depth_home.2) | copy-start | bytes 12582916
  177.8 29.5 %collective-permute-start.15 = (f32[16,16,128]{2,1,0:T(8,128)S(1)}, f32[16,16,128]{2,1,0:T(8,128)S(1)}, u32[]{:S(2)}, u32[]{:S(2)}) collective-permute-start(f32[16,16,128]{2,1,0:T(8,128)S(1)} %get-tuple-element.14), channel_id=1, source_target_pairs={{31,0},{28,1},{29,2},{30,3},{3,4},{0,5},{1,6},{2,7},{7,8},{4,9},{5... | collective-permute-start | bytes 393224 | tf_op jit(solution)/shard_map/ppermute | solution.py:283
  178.3 31.5 %collective-permute-start.14 = (f32[16,16,128]{2,1,0:T(8,128)S(1)}, f32[16,16,128]{2,1,0:T(8,128)S(1)}, u32[]{:S(2)}, u32[]{:S(2)}) collective-permute-start(f32[16,16,128]{2,1,0:T(8,128)S(1)} %get-tuple-element.15), channel_id=1, source_target_pairs={{29,0},{30,1},{31,2},{28,3},{1,4},{2,5},{3,6},{0,7},{5,8},{6,9},{7... | collective-permute-start | bytes 393224 | tf_op jit(solution)/shard_map/ppermute | solution.py:283
  178.3 55.8 %collective-permute-start.13 = (f32[16,128,128]{2,1,0:T(8,128)}, f32[16,128,128]{2,1,0:T(8,128)}, u32[]{:S(2)}, u32[]{:S(2)}) collective-permute-start(f32[16,128,128]{2,1,0:T(8,128)} %get-tuple-element.12), channel_id=1, source_target_pairs={{28,0},{29,1},{30,2},{31,3},{0,4},{1,5},{2,6},{3,7},{4,8},{5,9},{6... | collective-permute-start | bytes 3145736 | tf_op jit(solution)/shard_map/ppermute | solution.py:283
  178.3 37.0 %collective-permute-start.12 = (f32[16,16,128]{2,1,0:T(8,128)S(1)}, f32[16,16,128]{2,1,0:T(8,128)S(1)}, u32[]{:S(2)}, u32[]{:S(2)}) collective-permute-start(f32[16,16,128]{2,1,0:T(8,128)S(1)} %get-tuple-element.16), channel_id=1, source_target_pairs={{7,0},{4,1},{5,2},{6,3},{11,4},{8,5},{9,6},{10,7},{15,8},{12,9},{1... | collective-permute-start | bytes 393224 | tf_op jit(solution)/shard_map/ppermute | solution.py:283
  183.6 39.4 %collective-permute-start.11 = (f32[16,16,128]{2,1,0:T(8,128)S(1)}, f32[16,16,128]{2,1,0:T(8,128)S(1)}, u32[]{:S(2)}, u32[]{:S(2)}) collective-permute-start(f32[16,16,128]{2,1,0:T(8,128)S(1)} %get-tuple-element.13), channel_id=1, source_target_pairs={{5,0},{6,1},{7,2},{4,3},{9,4},{10,5},{11,6},{8,7},{13,8},{14,9},{1... | collective-permute-start | bytes 393224 | tf_op jit(solution)/shard_map/ppermute | solution.py:283
  188.9 4.8 %copy-start.16 = (f32[65,129,127]{2,1,0:T(8,128)}, f32[65,129,127]{2,1,0:T(8,128)S(1)}, u32[]{:S(2)}) copy-start(f32[65,129,127]{2,1,0:T(8,128)S(1)} %slice_subtract_fusion) | copy-start | bytes 12778744
  204.3 11.0 %slice-start = ((s8[4526080]{0:T(1024)(128)(4,1)}), s8[4194304]{0:T(1024)(128)(4,1)S(1)}, s32[]{:S(2)}) async-start(s8[4526080]{0:T(1024)(128)(4,1)} %bitcast.8), calls=%async_computation | async-start | bytes 8388608
  204.3 11.0 %slice-start.1 = ((s8[4526080]{0:T(1024)(128)(4,1)}), s8[331776]{0:T(1024)(128)(4,1)S(1)}, s32[]{:S(2)}) async-start(s8[4526080]{0:T(1024)(128)(4,1)} %bitcast.8), calls=%async_computation.1 | async-start | bytes 663552
  207.4 31.1 %collective-permute-start.10 = (f32[16,128,128]{2,1,0:T(8,128)S(1)}, f32[16,128,128]{2,1,0:T(8,128)S(1)}, u32[]{:S(2)}, u32[]{:S(2)}) collective-permute-start(f32[16,128,128]{2,1,0:T(8,128)S(1)} %get-tuple-element.11), channel_id=1, source_target_pairs={{4,0},{5,1},{6,2},{7,3},{8,4},{9,5},{10,6},{11,7},{12,8},{13,9},{1... | collective-permute-start | bytes 3145736 | tf_op jit(solution)/shard_map/ppermute | solution.py:283
  209.8 13.3 %collective-permute-start.9 = (f32[64,16,128]{2,1,0:T(8,128)}, f32[64,16,128]{2,1,0:T(8,128)S(1)}, u32[]{:S(2)}, u32[]{:S(2)}) collective-permute-start(f32[64,16,128]{2,1,0:T(8,128)} %get-tuple-element.10), channel_id=1, source_target_pairs={{3,0},{0,1},{1,2},{2,3},{7,4},{4,5},{5,6},{6,7},{11,8},{8,9},{9,10... | collective-permute-start | bytes 1572872 | tf_op jit(solution)/shard_map/ppermute | solution.py:283
  215.3 10.1 %collective-permute-start.8 = (f32[64,16,128]{2,1,0:T(8,128)}, f32[64,16,128]{2,1,0:T(8,128)S(1)}, u32[]{:S(2)}, u32[]{:S(2)}) collective-permute-start(f32[64,16,128]{2,1,0:T(8,128)} %get-tuple-element.9), channel_id=1, source_target_pairs={{1,0},{2,1},{3,2},{0,3},{5,4},{6,5},{7,6},{4,7},{9,8},{10,9},{11,1... | collective-permute-start | bytes 1572872 | tf_op jit(solution)/shard_map/ppermute | solution.py:283
  215.3 23.1 %copy-start.3 = (f32[64,128,128]{2,1,0:T(8,128)S(1)}, f32[64,128,128]{2,1,0:T(8,128)}, u32[]{:S(2)}) copy-start(f32[64,128,128]{2,1,0:T(8,128)} %copy-done.2) | copy-start | bytes 12582916
  274.6 83.5 %copy-start.1 = (f32[32,32,32]{2,1,0:T(8,128)S(1)}, f32[32,32,32]{2,1,0:T(8,128)}, u32[]{:S(2)}) copy-start(f32[32,32,32]{2,1,0:T(8,128)} %param.15) | copy-start | bytes 393220
  (6 other events, 15.4 us)

commit v2 on v1

--- a/solution.py
+++ b/solution.py
@@ -22,7 +22,12 @@
     table = np.asarray(table, np.float64).astype(np.float32)
     high = table.astype(ml_dtypes.bfloat16)
     low = (table - high.astype(np.float32)).astype(ml_dtypes.bfloat16)
-    return np.stack([high, low])
+    return high, low
+
+
+def thrice(table, axis):
+    high, low = halves(table)
+    return np.concatenate([high, high, low], axis)
 
 
 def waves(left, right, length):
@@ -40,18 +45,18 @@
     return high, low
 
 
-def dot(left, right, dims):
+def dot(left, right, dims=((1,), (0,))):
     return lax.dot_general(left, right, (dims, ((), ())), preferred_element_type=jnp.float32)
 
 
-def by_table(value, table, dims=((1,), (0,))):
+def by_table(value, table):
     high, low = split(value)
-    return dot(high, table[0], dims) + (dot(low, table[0], dims) + dot(high, table[1], dims))
-
-
-def table_by(table, value, dims=((1,), (0,))):
+    return dot(jnp.concatenate([high, low, high], 1), table)
+
+
+def table_by(table, value):
     high, low = split(value)
-    return dot(table[0], high, dims) + (dot(table[0], low, dims) + dot(table[1], high, dims))
+    return dot(table, jnp.concatenate([high, low, high], 0))
 
 
 class Plan:
@@ -62,35 +67,36 @@
         self.col_whole = cols + edge
         self.modes = depth // 2 + 1
         self.mode_pad = up16(self.modes)
+        self.mode_step = -(-self.modes // ROWS) * ROWS
         modes = np.arange(self.modes)
 
         cosine, sine = waves(modes, np.arange(depth), depth)
-        table = np.zeros((2 * self.mode_pad, depth))
+        table = np.zeros((up16(2 * self.mode_step), depth))
         table[: self.modes] = cosine
-        table[self.mode_pad : self.mode_pad + self.modes] = -sine
-        self.depth_out = halves(table)
+        table[self.mode_step : self.mode_step + self.modes] = -sine
+        self.depth_out = thrice(table, 1)
         weight = np.where((modes == 0) | (2 * modes == depth), 1.0, 2.0)
         weight = weight / (depth * self.row_whole * self.col_whole)
         table = np.zeros((self.mode_pad, 2 * depth))
         table[: self.modes, :depth] = cosine * weight[:, None]
         table[: self.modes, depth:] = -sine * weight[:, None]
-        self.depth_home = halves(table)
+        self.depth_home = thrice(table, 0)
 
         freq = np.arange(self.row_whole)
         place = np.concatenate([np.arange(rows + half), np.arange(-half, 0)])
         cosine, sine = waves(place, freq, self.row_whole)
-        self.rows_out = halves(self.lane_table(cosine, -sine, LANES, LANES))
+        self.rows_out = thrice(self.lane_table(cosine, -sine, LANES, LANES), 0)
         cosine, sine = waves(freq, np.arange(rows), self.row_whole)
-        self.rows_home = halves(self.lane_table(cosine, sine, LANES, rows))
+        self.rows_home = thrice(self.lane_table(cosine, sine, LANES, rows), 0)
         offset = np.arange(edge) - half
         cosine, sine = waves(offset, freq, self.row_whole)
-        self.rows_psf = halves(self.lane_table(cosine, -sine, LANES, LANES))
+        self.rows_psf = thrice(self.lane_table(cosine, -sine, LANES, LANES), 0)
 
         freq = np.arange(self.col_whole)
         place = np.concatenate([np.arange(cols + half), np.arange(-half, 0)])
-        self.cols_out = halves(np.concatenate(waves(freq, place, self.col_whole)))
-        self.cols_home = halves(np.concatenate(waves(np.arange(cols), freq, self.col_whole)))
-        self.cols_psf = halves(np.concatenate(waves(freq, offset, self.col_whole)))
+        self.cols_out = thrice(np.concatenate(waves(freq, place, self.col_whole)), 1)
+        self.cols_home = thrice(np.concatenate(waves(np.arange(cols), freq, self.col_whole)), 1)
+        self.cols_psf = thrice(np.concatenate(waves(freq, offset, self.col_whole)), 1)
 
     @staticmethod
     def lane_table(real_part, imag_part, left, right):
@@ -118,14 +124,26 @@
 
 
 def depth_out_kernel(plan, volume_ref, table_ref, out_ref):
+    volume = volume_ref.reshape(plan.row_whole * ROWS, plan.depth)
+    out = out_ref.reshape(plan.modes * 2 * ROWS, LANES)
     pad = jnp.zeros((LANES - plan.row_whole, plan.depth), jnp.float32)
-    for j in range(ROWS):
-        slab = volume_ref[:, j, :]
-        if plan.row_whole < LANES:
-            slab = jnp.concatenate([slab, pad], 0)
-        result = table_by(table_ref, slab, ((1,), (1,)))
-        out_ref[:, j, :LANES] = result[: plan.modes]
-        out_ref[:, j, LANES:] = result[plan.mode_pad : plan.mode_pad + plan.modes]
+    depth = plan.depth
+    for j in range(0, ROWS, 2):
+        slabs = []
+        for row in (j, j + 1):
+            slabs.append(volume[pl.ds(row, plan.row_whole, stride=ROWS), :])
+            if plan.row_whole < LANES:
+                slabs.append(pad)
+        high, low = split(jnp.concatenate(slabs, 0))
+        across = ((1,), (1,))
+        result = dot(table_ref[:, : 2 * depth], jnp.concatenate([high, low], 1), across)
+        result = result + dot(table_ref[:, 2 * depth :], high, across)
+        for c in range(2):
+            part = result[c * plan.mode_step : c * plan.mode_step + plan.modes]
+            for row in range(2):
+                out[pl.ds(c * ROWS + j + row, plan.modes, stride=2 * ROWS), :] = part[
+                    :, row * LANES : (row + 1) * LANES
+                ]
 
 
 def depth_out(plan, volume):
@@ -136,8 +154,8 @@
             pl.BlockSpec((plan.row_whole, ROWS, plan.depth), lambda i: (0, i, 0)),
             whole_spec(plan.depth_out),
         ],
-        out_specs=pl.BlockSpec((plan.modes, ROWS, 2 * LANES), lambda i: (0, i, 0)),
-        out_shape=jax.ShapeDtypeStruct((plan.modes, plan.col_whole, 2 * LANES), jnp.float32),
+        out_specs=pl.BlockSpec((plan.modes, 2, ROWS, LANES), lambda i: (0, 0, i, 0)),
+        out_shape=jax.ShapeDtypeStruct((plan.modes, 2, plan.col_whole, LANES), jnp.float32),
         compiler_params=params(),
         cost_estimate=cost(3e9, 2e7),
         name="depth_out",
@@ -155,11 +173,11 @@
 
 
 def transfer_kernel(psf_ref, rows_ref, cols_ref, out_ref):
-    for j in range(out_ref.shape[0]):
-        value = by_table(psf_ref[j], rows_ref)
-        real_part, imag_part = turned(cols_ref, value, True)
-        out_ref[j, :, :LANES] = real_part
-        out_ref[j, :, LANES:] = imag_part
+    step, edge = psf_ref.shape[:2]
+    values = by_table(jnp.concatenate([psf_ref[j] for j in range(step)], 0), rows_ref[...])
+    for j in range(step):
+        value = values[j * edge : (j + 1) * edge]
+        out_ref[j] = jnp.concatenate(turned(cols_ref[...], value, True), 1)
 
 
 def step_of(modes):
@@ -199,9 +217,13 @@
 
 
 def filter_kernel(adjoint, modes_ref, transfer_ref, rows_out, cols_out, cols_home, rows_home, out_ref):
-    for j in range(out_ref.shape[0]):
-        value = by_table(modes_ref[j], rows_out)
-        real_part, imag_part = turned(cols_out, value, True)
+    step, _, size, _ = modes_ref.shape
+    cols = out_ref.shape[1]
+    slabs = [jnp.concatenate([modes_ref[j, 0], modes_ref[j, 1]], 1) for j in range(step)]
+    values = by_table(jnp.concatenate(slabs, 0), rows_out[...])
+    home = []
+    for j in range(step):
+        real_part, imag_part = turned(cols_out[...], values[j * size : (j + 1) * size], True)
         gain_real = transfer_ref[j, :, :LANES]
         gain_imag = transfer_ref[j, :, LANES:]
         if adjoint:
@@ -213,18 +235,21 @@
             ],
             1,
         )
-        value = jnp.concatenate(turned(cols_home, value, False), 1)
-        out_ref[j] = by_table(value, rows_home)
+        home.append(jnp.concatenate(turned(cols_home[...], value, False), 1))
+    values = by_table(jnp.concatenate(home, 0), rows_home[...])
+    for j in range(step):
+        out_ref[j] = values[j * cols : (j + 1) * cols]
 
 
 def filtered(plan, modes, gains, adjoint):
     step = step_of(plan.modes)
     block = pl.BlockSpec((step, plan.col_whole, 2 * LANES), lambda i: (i, 0, 0))
+    modes_block = pl.BlockSpec((step, 2, plan.col_whole, LANES), lambda i: (i, 0, 0, 0))
     tables = [plan.rows_out, plan.cols_out, plan.cols_home, plan.rows_home]
     return pl.pallas_call(
         functools.partial(filter_kernel, adjoint),
         grid=(plan.modes // step,),
-        in_specs=[block, block] + [whole_spec(table) for table in tables],
+        in_specs=[modes_block, block] + [whole_spec(table) for table in tables],
         out_specs=pl.BlockSpec((step, plan.cols, 2 * plan.rows), lambda i: (i, 0, 0)),
         out_shape=jax.ShapeDtypeStruct((plan.modes, plan.cols, 2 * plan.rows), jnp.float32),
         compiler_params=params(),
@@ -234,13 +259,19 @@
 
 
 def depth_home_kernel(plan, divide, modes_ref, other_ref, table_ref, out_ref):
-    pad = jnp.zeros((plan.mode_pad - plan.modes, 2 * plan.rows), jnp.float32)
+    lanes = 2 * plan.rows
+    modes = modes_ref.reshape(plan.modes * ROWS, lanes)
+    others = other_ref.reshape(plan.rows * ROWS, plan.depth)
+    out = out_ref.reshape(plan.rows * ROWS, plan.depth)
+    pad = jnp.zeros((plan.mode_pad - plan.modes, lanes), jnp.float32)
     for j in range(ROWS):
-        slab = jnp.concatenate([modes_ref[:, j, :], pad], 0).T
-        both = by_table(slab, table_ref)
+        slab = modes[pl.ds(j, plan.modes, stride=ROWS), :]
+        high, low = split(jnp.concatenate([slab, pad], 0))
+        slab = jnp.concatenate([high, low, high], 0)
+        both = dot(slab, table_ref[...], ((0,), (0,)))
         result = both[: plan.rows, : plan.depth] + both[plan.rows :, plan.depth :]
-        other = other_ref[:, j, :]
-        out_ref[:, j, :] = other / result if divide else other * result
+        other = others[pl.ds(j, plan.rows, stride=ROWS), :]
+        out[pl.ds(j, plan.rows, stride=ROWS), :] = other / result if divide else other * result
 
 
 def depth_home(plan, modes, other, divide):

time: 360 us -> 303 us (0.84)
  Pallas kernels: 225 us -> 160 us
  waiting for transfers between devices: 23.4 us -> 32 us
    pallas_call x2, Pallas kernels: 132 us -> 86.7 us  [filtered(): pl.pallas_call(functools.partial(filter_kernel, adjoint), grid=(plan.mode...]
    ppermute x16, waiting for transfers between devices: 23.4 us -> 32 us  [fetch(): return lax.ppermute(piece, ('px', 'py'), pairs)]
    pallas_call x1, Pallas kernels: 19.5 us -> 11 us  [transfer(): pl.pallas_call(transfer_kernel, grid=(plan.modes // step,), in_specs=[pl....]
    pallas_call x2, Pallas kernels: 31.3 us -> 24.8 us  [depth_home(): pl.pallas_call(functools.partial(depth_home_kernel, plan, divide), grid=(...]
    pallas_call x2, Pallas kernels: 42.5 us -> 37.4 us  [depth_out(): pl.pallas_call(functools.partial(depth_out_kernel, plan), grid=(plan.col_...]
  transfers between devices with their start and end apart: 16 -> 16, of which waited for: 5 -> 5; matrix products, arithmetic and copies ran while one was open for 13% -> 15% of each run, Pallas kernels for 5% -> 4%
where the time goes in v2:
time: 303 us; the launch traced here: 302 us
  Pallas kernels  160 us (53%)
  other arithmetic  42.9 us (14%)
  starting transfers between devices  34.2 us (11%)
  waiting for transfers between devices  32 us (11%)
  local copies, waits for them, and re-layouts  30.3 us (10%)
    pallas_call x2, Pallas kernels, filtered(): pl.pallas_call(functools.partial(filter_kernel, adjoint), grid=(plan.mode...  86.7 us
    pallas_call x2, Pallas kernels, depth_out(): pl.pallas_call(functools.partial(depth_out_kernel, plan), grid=(plan.col_...  37.4 us
    ppermute x16, starting transfers between devices, fetch(): return lax.ppermute(piece, ('px', 'py'), pairs)  34.2 us
    ppermute x16, waiting for transfers between devices, fetch(): return lax.ppermute(piece, ('px', 'py'), pairs)  32 us
    pallas_call x2, Pallas kernels, depth_home(): pl.pallas_call(functools.partial(depth_home_kernel, plan, divide), grid=(...  24.8 us
    concatenate x2, other arithmetic, with_halo(): jnp.concatenate([jnp.concatenate([fetch(row, col) for col in sides], 1) f...  17.5 us
    unnamed x50, local copies, waits for them, and re-layouts  12.1 us
    pallas_call x1, Pallas kernels, transfer(): pl.pallas_call(transfer_kernel, grid=(plan.modes // step,), in_specs=[pl....  11 us
  transfers between devices with their start and end apart: 16, of which 5 were waited for; matrix products, arithmetic and copies ran while one was open for 15% of the time, Pallas kernels for 4%

profile of v2, /device:TPU:1, one launch (start us, length us, event | category | flops | bytes accessed | tf_op | source)
XLA Modules:
  0.0 301.6 jit_solution(11988922225297049721)
XLA Ops:
  0.0 3.1 %fusion.16 = (f32[16,128,128]{2,1,0:T(8,128)}, f32[16,128,128]{2,1,0:T(8,128)}) fusion(f32[64,128,128]{2,1,0:T(8,128)} %param.13), kind=kLoop, calls=%fused_computation.43 | loop fusion | bytes 4194304 | tf_op jit(solution)/shard_map/slice | solution.py:304
  3.1 2.1 collective-permute-start.5
  7.1 2.1 collective-permute-start.6
  9.1 2.9 collective-permute-start.2
  12.1 2.2 fusion.14
  19.0 2.1 copy.14
  21.3 11.0 %transfer.1.transfer_ref = f32[65,160,256]{2,1,0:T(8,128)} custom-call(f32[65,32,256]{2,1,0:T(8,128)S(1)} %select_maximum_fusion.psf_ref, bf16[768,256]{1,0:T(8,128)(2,1)S(1)} %copy-done.9, bf16[320,96]{1,0:T(8,128)(2,1)S(1)} %copy-done.13), custom_call_target="tpu_custom_call" | custom-call | flops 8999999488 | bytes 14000000 | tf_op jit(solution)/shard_map/transfer/pallas_call | solution.py:203
  32.3 2.6 constant_dynamic-update-slice_fusion.2
  36.1 4.5 %collective-permute-start.3 = (f32[16,16,128]{2,1,0:T(8,128)S(1)}, f32[16,16,128]{2,1,0:T(8,128)S(1)}, u32[]{:S(2)}, u32[]{:S(2)}) collective-permute-start(f32[16,16,128]{2,1,0:T(8,128)S(1)} %get-tuple-element.21), channel_id=1, source_target_pairs={{5,0},{6,1},{7,2},{4,3},{9,4},{10,5},{11,6},{8,7},{13,8},{14,9},{1... | collective-permute-start | bytes 393224 | tf_op jit(solution)/shard_map/ppermute | solution.py:314
  41.7 13.7 %collective-permute-done.5 = f32[16,128,128]{2,1,0:T(8,128)} collective-permute-done((f32[16,128,128]{2,1,0:T(8,128)}, f32[16,128,128]{2,1,0:T(8,128)}, u32[]{:S(2)}, u32[]{:S(2)}) %collective-permute-start.5) | collective-permute-done | bytes 1048608 | tf_op jit(solution)/shard_map/ppermute | solution.py:314
  55.4 8.7 %collective-permute-start.4 = (f32[16,16,128]{2,1,0:T(8,128)S(1)}, f32[16,16,128]{2,1,0:T(8,128)S(1)}, u32[]{:S(2)}, u32[]{:S(2)}) collective-permute-start(f32[16,16,128]{2,1,0:T(8,128)S(1)} %get-tuple-element.19), channel_id=1, source_target_pairs={{7,0},{4,1},{5,2},{6,3},{11,4},{8,5},{9,6},{10,7},{15,8},{12,9},{1... | collective-permute-start | bytes 393224 | tf_op jit(solution)/shard_map/ppermute | solution.py:314
  67.0 3.4 %pad_maximum_fusion.volume_ref = f32[96,160,128]{2,1,0:T(8,128)} fusion(f32[16,160,128]{2,1,0:T(8,128)S(1)} %constant_dynamic-update-slice_fusion.6, f32[16,160,128]{2,1,0:T(8,128)S(1)} %constant_dynamic-update-slice_fusion.3, f32[64,160,128]{2,1,0:T(8,128)S(1)} %constant_dynamic-update-slice_fusion), kind=kLoop, calls=%fused_computation | loop fusion | flops 3932160 | bytes 15728640 | tf_op jit(solution)/shard_map/concatenate | solution.py:317
  70.4 18.7 %depth_out.2.modes_ref = f32[65,2,160,128]{3,2,1,0:T(8,128)} custom-call(f32[96,160,128]{2,1,0:T(8,128)} %pad_maximum_fusion.volume_ref, bf16[144,384]{1,0:T(8,128)(2,1)S(1)} %copy-done.7), custom_call_target="tpu_custom_call" | custom-call | flops 3000000000 | bytes 20000000 | tf_op jit(solution)/shard_map/depth_out/pallas_call | solution.py:150
  89.2 43.3 %filtered.2.modes_ref = f32[65,128,128]{2,1,0:T(8,128)S(1)} custom-call(f32[65,2,160,128]{3,2,1,0:T(8,128)} %depth_out.2.modes_ref, f32[65,160,256]{2,1,0:T(8,128)} %transfer.1.transfer_ref, bf16[768,256]{1,0:T(8,128)(2,1)S(1)} %copy-done.8, bf16[320,480]{1,0:T(8,128)(2,1)S(1)} %copy-done.10, bf16[256,480]{1,0:T(8,128)(2,1)S(1)} %copy-done.11, ...), custom_call_target="tpu_custom_call" | custom-call | flops 22000001024 | bytes 25000000 | tf_op jit(solution)/shard_map/filtered/pallas_call | solution.py:249
  132.5 2.0 copy-done.5
  134.6 12.1 %depth_home.2 = f32[64,128,128]{2,1,0:T(8,128)S(1)} custom-call(f32[65,128,128]{2,1,0:T(8,128)} %copy-done.5, f32[64,128,128]{2,1,0:T(8,128)} %other_ref.1, bf16[240,256]{1,0:T(8,128)(2,1)S(1)} %copy-done.6), custom_call_target="tpu_custom_call" | custom-call | flops 3000000000 | bytes 13000000 | tf_op jit(solution)/shard_map/depth_home/pallas_call | solution.py:279
  150.6 5.3 %collective-permute-start.12 = (f32[16,16,128]{2,1,0:T(8,128)S(1)}, f32[16,16,128]{2,1,0:T(8,128)S(1)}, u32[]{:S(2)}, u32[]{:S(2)}) collective-permute-start(f32[16,16,128]{2,1,0:T(8,128)S(1)} %get-tuple-element.16), channel_id=1, source_target_pairs={{7,0},{4,1},{5,2},{6,3},{11,4},{8,5},{9,6},{10,7},{15,8},{12,9},{1... | collective-permute-start | bytes 393224 | tf_op jit(solution)/shard_map/ppermute | solution.py:314
  161.3 4.8 %fusion.9 = (f32[65,129,128]{2,1,0:T(8,128)}, f32[65,129,128]{2,1,0:T(8,128)}) fusion(f32[66,130,128]{2,1,0:T(8,128)S(1)} %fusion.1, pred[65]{0:T(512)(128)(4,1)S(1)} %compare_and_fusion.1, f32[65,129,127]{2,1,0:T(8,128)S(1)} %slice_subtract_fusion, f32[66,160,128]{2,1,0:T(8,128)S(1)} %fusion, pred[129]{0:T(512)(128)(4,1)S(1)} %compare_and_fusion), kind=kLoop, calls=%fused_computation.25 | loop fusion | flops 11806080 | bytes 25725374 | tf_op jit(solution)/shard_map/mul | solution.py:339
  166.0 10.6 %fusion.10 = (f32[65,129,128]{2,1,0:T(8,128)}, f32[65,129,128]{2,1,0:T(8,128)}) fusion(f32[65,129,128]{2,1,0:T(8,128)} %get-tuple-element.6, f32[66,130,128]{2,1,0:T(8,128)} %copy-done.14, f32[66,160,128]{2,1,0:T(8,128)} %copy-done.15, pred[129]{0:T(512)(128)(4,1)S(1)} %compare_and_fusion, f32[65,129,127]{2,1,0:T(8,128)} %copy-done.16), kind=kLoop, calls=%fused_computation.26 | loop fusion | flops 4293120 | bytes 25725308 | tf_op jit(solution)/shard_map/mul | solution.py:340
  176.6 3.0 slice.149
  179.7 2.4 collective-permute-start.10
  182.1 2.6 collective-permute-start.9
  184.7 3.0 %collective-permute-done.12 = f32[16,16,128]{2,1,0:T(8,128)S(1)} collective-permute-done((f32[16,16,128]{2,1,0:T(8,128)S(1)}, f32[16,16,128]{2,1,0:T(8,128)S(1)}, u32[]{:S(2)}, u32[]{:S(2)}) %collective-permute-start.12) | collective-permute-done | bytes 131104 | tf_op jit(solution)/shard_map/ppermute | solution.py:314
  187.8 7.7 %fusion.7.other_ref = f32[64,128,128]{2,1,0:T(8,128)S(1)} fusion(f32[64,128,128]{2,1,0:T(8,128)} %param.13, f32[65,129,128]{2,1,0:T(8,128)} %get-tuple-element.8, f32[65,129,128]{2,1,0:T(8,128)} %get-tuple-element.7, f32[65,129,128]{2,1,0:T(8,128)S(1)} %bitcast.9, f32[64,128,127]{2,1,0:T(8,128)S(1)} %slice.149), kind=kLoop, calls=%fused_computation.18 | loop fusion | flops 8388608 | bytes 33521664 | tf_op jit(solution)/shard_map/div | solution.py:370
  195.5 2.1 collective-permute-done.8
  197.7 8.8 %collective-permute-done.13 = f32[16,128,128]{2,1,0:T(8,128)} collective-permute-done((f32[16,128,128]{2,1,0:T(8,128)}, f32[16,128,128]{2,1,0:T(8,128)}, u32[]{:S(2)}, u32[]{:S(2)}) %collective-permute-start.13) | collective-permute-done | bytes 1048608 | tf_op jit(solution)/shard_map/ppermute | solution.py:314
  206.5 4.3 %collective-permute-done.10 = f32[16,128,128]{2,1,0:T(8,128)S(1)} collective-permute-done((f32[16,128,128]{2,1,0:T(8,128)S(1)}, f32[16,128,128]{2,1,0:T(8,128)S(1)}, u32[]{:S(2)}, u32[]{:S(2)}) %collective-permute-start.10) | collective-permute-done | bytes 1048608 | tf_op jit(solution)/shard_map/ppermute | solution.py:314
  210.8 14.1 %maximum_maximum_fusion.volume_ref = f32[96,160,128]{2,1,0:T(8,128)} fusion(f32[16,16,128]{2,1,0:T(8,128)S(1)} %collective-permute-done.15, f32[16,16,128]{2,1,0:T(8,128)S(1)} %collective-permute-done.14, f32[16,128,128]{2,1,0:T(8,128)} %collective-permute-done.13, f32[16,16,128]{2,1,0:T(8,128)S(1)} %collective-permute-done.12, ...), kind=kLoop, calls=%fused_computation.1 | loop fusion | flops 15728640 | bytes 15728640 | tf_op jit(solution)/shard_map/concatenate | solution.py:317
  224.9 18.6 %depth_out.3.modes_ref = f32[65,2,160,128]{3,2,1,0:T(8,128)} custom-call(f32[96,160,128]{2,1,0:T(8,128)} %maximum_maximum_fusion.volume_ref, bf16[144,384]{1,0:T(8,128)(2,1)S(1)} %copy-done.7), custom_call_target="tpu_custom_call" | custom-call | flops 3000000000 | bytes 20000000 | tf_op jit(solution)/shard_map/depth_out/pallas_call | solution.py:150
  243.5 43.4 %filtered.3.modes_ref = f32[65,128,128]{2,1,0:T(8,128)S(1)} custom-call(f32[65,2,160,128]{3,2,1,0:T(8,128)} %depth_out.3.modes_ref, f32[65,160,256]{2,1,0:T(8,128)} %transfer.1.transfer_ref, bf16[768,256]{1,0:T(8,128)(2,1)S(1)} %copy-done.8, bf16[320,480]{1,0:T(8,128)(2,1)S(1)} %copy-done.10, bf16[256,480]{1,0:T(8,128)(2,1)S(1)} %copy-done.11, ...), custom_call_target="tpu_custom_call" | custom-call | flops 22000001024 | bytes 25000000 | tf_op jit(solution)/shard_map/filtered/pallas_call | solution.py:249
  286.9 2.0 copy-done.4
  288.9 12.7 %depth_home.3 = f32[64,128,128]{2,1,0:T(8,128)} custom-call(f32[65,128,128]{2,1,0:T(8,128)} %copy-done.4, f32[64,128,128]{2,1,0:T(8,128)S(1)} %fusion.7.other_ref, bf16[240,256]{1,0:T(8,128)(2,1)S(1)} %copy-done.6), custom_call_target="tpu_custom_call" | custom-call | flops 3000000000 | bytes 13000000 | tf_op jit(solution)/shard_map/depth_home/pallas_call | solution.py:279
  (85 shorter events, 20.9 us)
Async XLA Ops:
  0.0 16.1 %copy-start = (f32[32,32,32]{2,1,0:T(8,128)S(1)}, f32[32,32,32]{2,1,0:T(8,128)}, u32[]{:S(2)}) copy-start(f32[32,32,32]{2,1,0:T(8,128)} %param.15) | copy-start | bytes 393220
  0.0 16.1 %copy-start.18 = (f32[32,65,1]{1,0,2:T(8,128)S(1)}, f32[32,65,1]{1,0,2:T(8,128)}, u32[]{:S(2)}) copy-start(f32[32,65,1]{1,0,2:T(8,128)} %constant.74) | copy-start | bytes 24964
  0.0 17.6 %copy-start.19 = (f32[32,65,1]{1,0,2:T(8,128)S(1)}, f32[32,65,1]{1,0,2:T(8,128)}, u32[]{:S(2)}) copy-start(f32[32,65,1]{1,0,2:T(8,128)} %constant.73) | copy-start | bytes 24964
  3.1 52.3 %collective-permute-start.5 = (f32[16,128,128]{2,1,0:T(8,128)}, f32[16,128,128]{2,1,0:T(8,128)}, u32[]{:S(2)}, u32[]{:S(2)}) collective-permute-start(f32[16,128,128]{2,1,0:T(8,128)} %get-tuple-element.24), channel_id=1, source_target_pairs={{28,0},{29,1},{30,2},{31,3},{0,4},{1,5},{2,6},{3,7},{4,8},{5,9},{6... | collective-permute-start | bytes 3145736 | tf_op jit(solution)/shard_map/ppermute | solution.py:314
  7.1 59.8 %collective-permute-start.6 = (f32[16,16,128]{2,1,0:T(8,128)}, f32[16,16,128]{2,1,0:T(8,128)S(1)}, u32[]{:S(2)}, u32[]{:S(2)}) collective-permute-start(f32[16,16,128]{2,1,0:T(8,128)} %get-tuple-element.20), channel_id=1, source_target_pairs={{29,0},{30,1},{31,2},{28,3},{1,4},{2,5},{3,6},{0,7},{5,8},{6,9},{7... | collective-permute-start | bytes 393224 | tf_op jit(solution)/shard_map/ppermute | solution.py:314
  9.1 56.4 %collective-permute-start.2 = (f32[16,128,128]{2,1,0:T(8,128)}, f32[16,128,128]{2,1,0:T(8,128)}, u32[]{:S(2)}, u32[]{:S(2)}) collective-permute-start(f32[16,128,128]{2,1,0:T(8,128)} %get-tuple-element.23), channel_id=1, source_target_pairs={{4,0},{5,1},{6,2},{7,3},{8,4},{9,5},{10,6},{11,7},{12,8},{13,9},{1... | collective-permute-start | bytes 3145736 | tf_op jit(solution)/shard_map/ppermute | solution.py:314
  14.3 20.6 %collective-permute-start = (f32[64,16,128]{2,1,0:T(8,128)}, f32[64,16,128]{2,1,0:T(8,128)}, u32[]{:S(2)}, u32[]{:S(2)}) collective-permute-start(f32[64,16,128]{2,1,0:T(8,128)} %get-tuple-element.18), channel_id=1, source_target_pairs={{1,0},{2,1},{3,2},{0,3},{5,4},{6,5},{7,6},{4,7},{9,8},{10,9},{11,1... | collective-permute-start | bytes 1572872 | tf_op jit(solution)/shard_map/ppermute | solution.py:314
  15.1 6.2 %copy-start.9 = (bf16[768,256]{1,0:T(8,128)(2,1)S(1)}, bf16[768,256]{1,0:T(8,128)(2,1)}, u32[]{:S(2)}) copy-start(bf16[768,256]{1,0:T(8,128)(2,1)} %constant.57.clone.rows_ref) | copy-start | bytes 1179652
  15.1 6.2 %copy-start.13 = (bf16[320,96]{1,0:T(8,128)(2,1)S(1)}, bf16[320,96]{1,0:T(8,128)(2,1)}, u32[]{:S(2)}) copy-start(bf16[320,96]{1,0:T(8,128)(2,1)} %constant.58.clone.cols_ref) | copy-start | bytes 184324
  15.1 21.1 %collective-permute-start.1 = (f32[64,16,128]{2,1,0:T(8,128)}, f32[64,16,128]{2,1,0:T(8,128)}, u32[]{:S(2)}, u32[]{:S(2)}) collective-permute-start(f32[64,16,128]{2,1,0:T(8,128)} %get-tuple-element.17), channel_id=1, source_target_pairs={{3,0},{0,1},{1,2},{2,3},{7,4},{4,5},{5,6},{6,7},{11,8},{8,9},{9,10... | collective-permute-start | bytes 1572872 | tf_op jit(solution)/shard_map/ppermute | solution.py:314
  35.0 31.9 %collective-permute-start.7 = (f32[16,16,128]{2,1,0:T(8,128)S(1)}, f32[16,16,128]{2,1,0:T(8,128)S(1)}, u32[]{:S(2)}, u32[]{:S(2)}) collective-permute-start(f32[16,16,128]{2,1,0:T(8,128)S(1)} %copy-done.17), channel_id=1, source_target_pairs={{31,0},{28,1},{29,2},{30,3},{3,4},{0,5},{1,6},{2,7},{7,8},{4,9},{5... | collective-permute-start | bytes 393224 | tf_op jit(solution)/shard_map/ppermute | solution.py:314
  36.1 30.8 %collective-permute-start.3 = (f32[16,16,128]{2,1,0:T(8,128)S(1)}, f32[16,16,128]{2,1,0:T(8,128)S(1)}, u32[]{:S(2)}, u32[]{:S(2)}) collective-permute-start(f32[16,16,128]{2,1,0:T(8,128)S(1)} %get-tuple-element.21), channel_id=1, source_target_pairs={{5,0},{6,1},{7,2},{4,3},{9,4},{10,5},{11,6},{8,7},{13,8},{14,9},{1... | collective-permute-start | bytes 393224 | tf_op jit(solution)/shard_map/ppermute | solution.py:314
  55.4 11.5 %collective-permute-start.4 = (f32[16,16,128]{2,1,0:T(8,128)S(1)}, f32[16,16,128]{2,1,0:T(8,128)S(1)}, u32[]{:S(2)}, u32[]{:S(2)}) collective-permute-start(f32[16,16,128]{2,1,0:T(8,128)S(1)} %get-tuple-element.19), channel_id=1, source_target_pairs={{7,0},{4,1},{5,2},{6,3},{11,4},{8,5},{9,6},{10,7},{15,8},{12,9},{1... | collective-permute-start | bytes 393224 | tf_op jit(solution)/shard_map/ppermute | solution.py:314
  70.4 18.8 %copy-start.8 = (bf16[768,256]{1,0:T(8,128)(2,1)S(1)}, bf16[768,256]{1,0:T(8,128)(2,1)}, u32[]{:S(2)}) copy-start(bf16[768,256]{1,0:T(8,128)(2,1)} %constant.60.clone.rows_out) | copy-start | bytes 1179652
  70.4 18.8 %copy-start.10 = (bf16[320,480]{1,0:T(8,128)(2,1)S(1)}, bf16[320,480]{1,0:T(8,128)(2,1)}, u32[]{:S(2)}) copy-start(bf16[320,480]{1,0:T(8,128)(2,1)} %constant.61.clone.cols_out) | copy-start | bytes 921604
  70.4 18.8 %copy-start.11 = (bf16[256,480]{1,0:T(8,128)(2,1)S(1)}, bf16[256,480]{1,0:T(8,128)(2,1)}, u32[]{:S(2)}) copy-start(bf16[256,480]{1,0:T(8,128)(2,1)} %constant.62.clone.cols_home) | copy-start | bytes 737284
  70.4 18.8 %copy-start.12 = (bf16[768,128]{1,0:T(8,128)(2,1)S(1)}, bf16[768,128]{1,0:T(8,128)(2,1)}, u32[]{:S(2)}) copy-start(bf16[768,128]{1,0:T(8,128)(2,1)} %constant.63.clone.rows_home) | copy-start | bytes 589828
  89.2 45.4 %copy-start.6 = (bf16[240,256]{1,0:T(8,128)(2,1)S(1)}, bf16[240,256]{1,0:T(8,128)(2,1)}, u32[]{:S(2)}) copy-start(bf16[240,256]{1,0:T(8,128)(2,1)} %constant.64.clone.table_ref) | copy-start | bytes 368644
  146.7 10.8 %copy-start.2 = (f32[64,128,128]{2,1,0:T(8,128)}, f32[64,128,128]{2,1,0:T(8,128)S(1)}, u32[]{:S(2)}) copy-start(f32[64,128,128]{2,1,0:T(8,128)S(1)} %depth_home.2) | copy-start | bytes 12582916
  150.2 29.5 %collective-permute-start.15 = (f32[16,16,128]{2,1,0:T(8,128)S(1)}, f32[16,16,128]{2,1,0:T(8,128)S(1)}, u32[]{:S(2)}, u32[]{:S(2)}) collective-permute-start(f32[16,16,128]{2,1,0:T(8,128)S(1)} %get-tuple-element.14), channel_id=1, source_target_pairs={{31,0},{28,1},{29,2},{30,3},{3,4},{0,5},{1,6},{2,7},{7,8},{4,9},{5... | collective-permute-start | bytes 393224 | tf_op jit(solution)/shard_map/ppermute | solution.py:314
  150.6 31.5 %collective-permute-start.14 = (f32[16,16,128]{2,1,0:T(8,128)S(1)}, f32[16,16,128]{2,1,0:T(8,128)S(1)}, u32[]{:S(2)}, u32[]{:S(2)}) collective-permute-start(f32[16,16,128]{2,1,0:T(8,128)S(1)} %get-tuple-element.15), channel_id=1, source_target_pairs={{29,0},{30,1},{31,2},{28,3},{1,4},{2,5},{3,6},{0,7},{5,8},{6,9},{7... | collective-permute-start | bytes 393224 | tf_op jit(solution)/shard_map/ppermute | solution.py:314
  150.6 55.8 %collective-permute-start.13 = (f32[16,128,128]{2,1,0:T(8,128)}, f32[16,128,128]{2,1,0:T(8,128)}, u32[]{:S(2)}, u32[]{:S(2)}) collective-permute-start(f32[16,128,128]{2,1,0:T(8,128)} %get-tuple-element.12), channel_id=1, source_target_pairs={{28,0},{29,1},{30,2},{31,3},{0,4},{1,5},{2,6},{3,7},{4,8},{5,9},{6... | collective-permute-start | bytes 3145736 | tf_op jit(solution)/shard_map/ppermute | solution.py:314
  150.6 37.2 %collective-permute-start.12 = (f32[16,16,128]{2,1,0:T(8,128)S(1)}, f32[16,16,128]{2,1,0:T(8,128)S(1)}, u32[]{:S(2)}, u32[]{:S(2)}) collective-permute-start(f32[16,16,128]{2,1,0:T(8,128)S(1)} %get-tuple-element.16), channel_id=1, source_target_pairs={{7,0},{4,1},{5,2},{6,3},{11,4},{8,5},{9,6},{10,7},{15,8},{12,9},{1... | collective-permute-start | bytes 393224 | tf_op jit(solution)/shard_map/ppermute | solution.py:314
  156.0 39.6 %collective-permute-start.11 = (f32[16,16,128]{2,1,0:T(8,128)}, f32[16,16,128]{2,1,0:T(8,128)}, u32[]{:S(2)}, u32[]{:S(2)}) collective-permute-start(f32[16,16,128]{2,1,0:T(8,128)} %get-tuple-element.13), channel_id=1, source_target_pairs={{5,0},{6,1},{7,2},{4,3},{9,4},{10,5},{11,6},{8,7},{13,8},{14,9},{1... | collective-permute-start | bytes 393224 | tf_op jit(solution)/shard_map/ppermute | solution.py:314
  161.3 4.8 %copy-start.16 = (f32[65,129,127]{2,1,0:T(8,128)}, f32[65,129,127]{2,1,0:T(8,128)S(1)}, u32[]{:S(2)}) copy-start(f32[65,129,127]{2,1,0:T(8,128)S(1)} %slice_subtract_fusion) | copy-start | bytes 12778744
  176.6 11.1 %slice-start = ((s8[4526080]{0:T(1024)(128)(4,1)}), s8[4194304]{0:T(1024)(128)(4,1)S(1)}, s32[]{:S(2)}) async-start(s8[4526080]{0:T(1024)(128)(4,1)} %bitcast.8), calls=%async_computation | async-start | bytes 8388608
  176.6 11.1 %slice-start.1 = ((s8[4526080]{0:T(1024)(128)(4,1)}), s8[331776]{0:T(1024)(128)(4,1)S(1)}, s32[]{:S(2)}) async-start(s8[4526080]{0:T(1024)(128)(4,1)} %bitcast.8), calls=%async_computation.1 | async-start | bytes 663552
  179.7 31.1 %collective-permute-start.10 = (f32[16,128,128]{2,1,0:T(8,128)S(1)}, f32[16,128,128]{2,1,0:T(8,128)S(1)}, u32[]{:S(2)}, u32[]{:S(2)}) collective-permute-start(f32[16,128,128]{2,1,0:T(8,128)S(1)} %get-tuple-element.11), channel_id=1, source_target_pairs={{4,0},{5,1},{6,2},{7,3},{8,4},{9,5},{10,6},{11,7},{12,8},{13,9},{1... | collective-permute-start | bytes 3145736 | tf_op jit(solution)/shard_map/ppermute | solution.py:314
  182.1 13.4 %collective-permute-start.9 = (f32[64,16,128]{2,1,0:T(8,128)}, f32[64,16,128]{2,1,0:T(8,128)S(1)}, u32[]{:S(2)}, u32[]{:S(2)}) collective-permute-start(f32[64,16,128]{2,1,0:T(8,128)} %get-tuple-element.10), channel_id=1, source_target_pairs={{3,0},{0,1},{1,2},{2,3},{7,4},{4,5},{5,6},{6,7},{11,8},{8,9},{9,10... | collective-permute-start | bytes 1572872 | tf_op jit(solution)/shard_map/ppermute | solution.py:314
  187.8 9.9 %collective-permute-start.8 = (f32[64,16,128]{2,1,0:T(8,128)}, f32[64,16,128]{2,1,0:T(8,128)S(1)}, u32[]{:S(2)}, u32[]{:S(2)}) collective-permute-start(f32[64,16,128]{2,1,0:T(8,128)} %get-tuple-element.9), channel_id=1, source_target_pairs={{1,0},{2,1},{3,2},{0,3},{5,4},{6,5},{7,6},{4,7},{9,8},{10,9},{11,1... | collective-permute-start | bytes 1572872 | tf_op jit(solution)/shard_map/ppermute | solution.py:314
  187.8 23.0 %copy-start.3 = (f32[64,128,128]{2,1,0:T(8,128)S(1)}, f32[64,128,128]{2,1,0:T(8,128)}, u32[]{:S(2)}) copy-start(f32[64,128,128]{2,1,0:T(8,128)} %copy-done.2) | copy-start | bytes 12582916
  243.5 58.1 %copy-start.1 = (f32[32,32,32]{2,1,0:T(8,128)S(1)}, f32[32,32,32]{2,1,0:T(8,128)}, u32[]{:S(2)}) copy-start(f32[32,32,32]{2,1,0:T(8,128)} %param.15) | copy-start | bytes 393220
  (6 other events, 15.3 us)

commit v3 on v2

--- a/solution.py
+++ b/solution.py
@@ -14,6 +14,7 @@
 smoothing = 0.1
 
 LANES = 128
+HALF = LANES // 2
 ROWS = 8
 VMEM_LIMIT = 48 * 1024 * 1024
 
@@ -83,20 +84,24 @@
         self.depth_home = thrice(table, 0)
 
         freq = np.arange(self.row_whole)
-        place = np.concatenate([np.arange(rows + half), np.arange(-half, 0)])
-        cosine, sine = waves(place, freq, self.row_whole)
-        self.rows_out = thrice(self.lane_table(cosine, -sine, LANES, LANES), 0)
+        own = self.lane_table(*self.out_waves(np.arange(rows), freq), HALF, LANES)
+        place = np.concatenate([np.arange(rows, rows + half), np.arange(-half, 0)])
+        halo = self.lane_table(*self.out_waves(place, freq), HALF, LANES)
+        self.rows_out = thrice(np.concatenate([own, halo]), 0)
         cosine, sine = waves(freq, np.arange(rows), self.row_whole)
         self.rows_home = thrice(self.lane_table(cosine, sine, LANES, rows), 0)
         offset = np.arange(edge) - half
-        cosine, sine = waves(offset, freq, self.row_whole)
-        self.rows_psf = thrice(self.lane_table(cosine, -sine, LANES, LANES), 0)
+        self.rows_psf = thrice(self.lane_table(*self.out_waves(offset, freq), LANES, LANES), 0)
 
         freq = np.arange(self.col_whole)
         place = np.concatenate([np.arange(cols + half), np.arange(-half, 0)])
         self.cols_out = thrice(np.concatenate(waves(freq, place, self.col_whole)), 1)
         self.cols_home = thrice(np.concatenate(waves(np.arange(cols), freq, self.col_whole)), 1)
         self.cols_psf = thrice(np.concatenate(waves(freq, offset, self.col_whole)), 1)
+
+    def out_waves(self, place, freq):
+        cosine, sine = waves(place, freq, self.row_whole)
+        return cosine, -sine
 
     @staticmethod
     def lane_table(real_part, imag_part, left, right):
@@ -123,43 +128,90 @@
     return pl.CostEstimate(flops=int(flops), bytes_accessed=int(moved), transcendentals=0)
 
 
-def depth_out_kernel(plan, volume_ref, table_ref, out_ref):
-    volume = volume_ref.reshape(plan.row_whole * ROWS, plan.depth)
-    out = out_ref.reshape(plan.modes * 2 * ROWS, LANES)
-    pad = jnp.zeros((LANES - plan.row_whole, plan.depth), jnp.float32)
+def depth_out_kernel(plan, count, *refs):
+    pieces, table_ref, out_ref = refs[:count], refs[count], refs[count + 1]
+    sizes = [piece.shape[0] for piece in pieces]
+    pieces = [piece.reshape(piece.shape[0] * ROWS, plan.depth) for piece in pieces]
+    out = out_ref.reshape(plan.modes * ROWS, LANES)
+    size = sum(sizes)
+    group = min(ROWS, 2 * LANES // size)
     depth = plan.depth
-    for j in range(0, ROWS, 2):
-        slabs = []
-        for row in (j, j + 1):
-            slabs.append(volume[pl.ds(row, plan.row_whole, stride=ROWS), :])
-            if plan.row_whole < LANES:
-                slabs.append(pad)
+    across = ((1,), (1,))
+    for first in range(0, ROWS, group):
+        slabs = [
+            piece[pl.ds(j, length, stride=ROWS), :]
+            for j in range(first, first + group)
+            for piece, length in zip(pieces, sizes)
+        ]
         high, low = split(jnp.concatenate(slabs, 0))
-        across = ((1,), (1,))
         result = dot(table_ref[:, : 2 * depth], jnp.concatenate([high, low], 1), across)
         result = result + dot(table_ref[:, 2 * depth :], high, across)
-        for c in range(2):
-            part = result[c * plan.mode_step : c * plan.mode_step + plan.modes]
-            for row in range(2):
-                out[pl.ds(c * ROWS + j + row, plan.modes, stride=2 * ROWS), :] = part[
-                    :, row * LANES : (row + 1) * LANES
-                ]
-
-
-def depth_out(plan, volume):
+        real_part = result[: plan.modes]
+        imag_part = result[plan.mode_step : plan.mode_step + plan.modes]
+        gap = [jnp.zeros((plan.modes, HALF - size), jnp.float32)] if size < HALF else []
+        for j in range(group):
+            lanes = slice(j * size, (j + 1) * size)
+            value = jnp.concatenate([real_part[:, lanes], *gap, imag_part[:, lanes], *gap], 1)
+            out[pl.ds(first + j, plan.modes, stride=ROWS), :] = value
+
+
+def depth_out(plan, name, *pieces):
+    cols = pieces[0].shape[1]
     return pl.pallas_call(
-        functools.partial(depth_out_kernel, plan),
-        grid=(plan.col_whole // ROWS,),
+        functools.partial(depth_out_kernel, plan, len(pieces)),
+        grid=(cols // ROWS,),
         in_specs=[
-            pl.BlockSpec((plan.row_whole, ROWS, plan.depth), lambda i: (0, i, 0)),
-            whole_spec(plan.depth_out),
-        ],
-        out_specs=pl.BlockSpec((plan.modes, 2, ROWS, LANES), lambda i: (0, 0, i, 0)),
-        out_shape=jax.ShapeDtypeStruct((plan.modes, 2, plan.col_whole, LANES), jnp.float32),
+            pl.BlockSpec((piece.shape[0], ROWS, plan.depth), lambda i: (0, i, 0))
+            for piece in pieces
+        ]
+        + [whole_spec(plan.depth_out)],
+        out_specs=pl.BlockSpec((plan.modes, ROWS, LANES), lambda i: (0, i, 0)),
+        out_shape=jax.ShapeDtypeStruct((plan.modes, cols, LANES), jnp.float32),
         compiler_params=params(),
-        cost_estimate=cost(3e9, 2e7),
-        name="depth_out",
-    )(volume, plan.depth_out)
+        cost_estimate=cost(6e7 * cols, 7e4 * cols),
+        name=name,
+    )(*pieces, plan.depth_out)
+
+
+def turned_narrow(table, planes):
+    both = table_by(table, jnp.concatenate(planes, 1) if len(planes) > 1 else planes[0])
+    half = both.shape[0] // 2
+    lane = lax.broadcasted_iota(jnp.int32, (half, LANES), 1)
+    out = []
+    for j in range(len(planes)):
+        cosine = both[:half, j * LANES : (j + 1) * LANES]
+        sine = pltpu.roll(both[half:, j * LANES : (j + 1) * LANES], HALF, 1)
+        out.append(cosine + jnp.where(lane < HALF, sine, -sine))
+    return out
+
+
+def pairs_of(count):
+    return [range(j, min(j + 2, count)) for j in range(0, count, 2)]
+
+
+def cols_kernel(inner_ref, outer_ref, table_ref, out_ref):
+    for pair in pairs_of(out_ref.shape[0]):
+        planes = [jnp.concatenate([inner_ref[j], outer_ref[j]], 0) for j in pair]
+        for j, plane in zip(pair, turned_narrow(table_ref[...], planes)):
+            out_ref[j] = plane
+
+
+def cols_out(plan, inner, outer):
+    step = step_of(plan.modes, 13)
+
+    def spec(size):
+        return pl.BlockSpec((step, size, LANES), lambda i: (i, 0, 0))
+
+    return pl.pallas_call(
+        cols_kernel,
+        grid=(plan.modes // step,),
+        in_specs=[spec(plan.cols), spec(plan.edge), whole_spec(plan.cols_out)],
+        out_specs=spec(plan.col_whole),
+        out_shape=jax.ShapeDtypeStruct((plan.modes, plan.col_whole, LANES), jnp.float32),
+        compiler_params=params(),
+        cost_estimate=cost(8e9, 1.1e7),
+        name="cols_out",
+    )(inner, outer, plan.cols_out)
 
 
 def turned(table, value, forward):
@@ -180,8 +232,8 @@
         out_ref[j] = jnp.concatenate(turned(cols_ref[...], value, True), 1)
 
 
-def step_of(modes):
-    return max(size for size in range(1, 6) if modes % size == 0)
+def step_of(modes, most):
+    return max(size for size in range(1, most + 1) if modes % size == 0)
 
 
 def transfer(plan, psf):
@@ -199,7 +251,7 @@
     ]
     parts = [jnp.pad(part, ((0, 0), (0, 0), (0, LANES - edge))) for part in parts]
     modes = jnp.concatenate(parts, 2)
-    step = step_of(plan.modes)
+    step = step_of(plan.modes, 5)
     return pl.pallas_call(
         transfer_kernel,
         grid=(plan.modes // step,),
@@ -216,14 +268,22 @@
     )(modes, plan.rows_psf, plan.cols_psf)
 
 
-def filter_kernel(adjoint, modes_ref, transfer_ref, rows_out, cols_out, cols_home, rows_home, out_ref):
-    step, _, size, _ = modes_ref.shape
+def filter_kernel(
+    adjoint, own_ref, inner_ref, outer_ref, transfer_ref,
+    rows_out, cols_out, cols_home, rows_home, out_ref,
+):
+    step, size, _ = own_ref.shape
     cols = out_ref.shape[1]
-    slabs = [jnp.concatenate([modes_ref[j, 0], modes_ref[j, 1]], 1) for j in range(step)]
+    slabs = []
+    for pair in pairs_of(step):
+        planes = [jnp.concatenate([inner_ref[j], outer_ref[j]], 0) for j in pair]
+        for j, plane in zip(pair, turned_narrow(cols_out[...], planes)):
+            slabs.append(jnp.concatenate([own_ref[j], plane], 1))
     values = by_table(jnp.concatenate(slabs, 0), rows_out[...])
     home = []
     for j in range(step):
-        real_part, imag_part = turned(cols_out[...], values[j * size : (j + 1) * size], True)
+        real_part = values[j * size : (j + 1) * size, :LANES]
+        imag_part = values[j * size : (j + 1) * size, LANES:]
         gain_real = transfer_ref[j, :, :LANES]
         gain_imag = transfer_ref[j, :, LANES:]
         if adjoint:
@@ -241,21 +301,25 @@
         out_ref[j] = values[j * cols : (j + 1) * cols]
 
 
-def filtered(plan, modes, gains, adjoint):
-    step = step_of(plan.modes)
+def filtered(plan, own, inner, outer, gains, adjoint):
+    step = step_of(plan.modes, 5)
     block = pl.BlockSpec((step, plan.col_whole, 2 * LANES), lambda i: (i, 0, 0))
-    modes_block = pl.BlockSpec((step, 2, plan.col_whole, LANES), lambda i: (i, 0, 0, 0))
+
+    def spec(size):
+        return pl.BlockSpec((step, size, LANES), lambda i: (i, 0, 0))
+
     tables = [plan.rows_out, plan.cols_out, plan.cols_home, plan.rows_home]
     return pl.pallas_call(
         functools.partial(filter_kernel, adjoint),
         grid=(plan.modes // step,),
-        in_specs=[modes_block, block] + [whole_spec(table) for table in tables],
+        in_specs=[spec(plan.col_whole), spec(plan.cols), spec(plan.edge), block]
+        + [whole_spec(table) for table in tables],
         out_specs=pl.BlockSpec((step, plan.cols, 2 * plan.rows), lambda i: (i, 0, 0)),
         out_shape=jax.ShapeDtypeStruct((plan.modes, plan.cols, 2 * plan.rows), jnp.float32),
         compiler_params=params(),
         cost_estimate=cost(2.2e10, 2.5e7),
         name="filtered",
-    )(modes, gains, *tables)
+    )(own, inner, outer, gains, *tables)
 
 
 def depth_home_kernel(plan, divide, modes_ref, other_ref, table_ref, out_ref):
@@ -292,31 +356,29 @@
     )(modes, other, plan.depth_home)
 
 
-def with_halo(block, width):
-    row_count = lax.axis_size("px")
-    col_count = lax.axis_size("py")
-    devices = [(i, j) for i in range(row_count) for j in range(col_count)]
-
-    def part(size, side):
-        return {0: slice(None), 1: slice(0, width), -1: slice(size - width, size)}[side]
-
-    def fetch(row_side, col_side):
-        piece = block[part(block.shape[0], row_side), part(block.shape[1], col_side)]
-        if row_side == 0 and col_side == 0:
-            return piece
-        pairs = [
-            (
-                ((i + row_side) % row_count) * col_count + (j + col_side) % col_count,
-                i * col_count + j,
-            )
-            for i, j in devices
-        ]
-        return lax.ppermute(piece, ("px", "py"), pairs)
-
-    sides = (0, 1, -1)
-    return jnp.concatenate(
-        [jnp.concatenate([fetch(row, col) for col in sides], 1) for row in sides], 0
-    )
+def neighbours(axis, after, before):
+    count = lax.axis_size(axis)
+    return (
+        lax.ppermute(after, axis, [((i + 1) % count, i) for i in range(count)]),
+        lax.ppermute(before, axis, [(i, (i + 1) % count) for i in range(count)]),
+    )
+
+
+def halos(block, width):
+    rows = neighbours("px", block[:width], block[-width:])
+    cols = jnp.concatenate(neighbours("py", block[:, :width], block[:, -width:]), 1)
+    corners = neighbours("px", cols[:width], cols[-width:])
+    return rows, cols, corners
+
+
+def convolved(plan, block, around, gains, adjoint):
+    rows, cols, corners = around
+    own = cols_out(
+        plan, depth_out(plan, "depth_own", block), depth_out(plan, "depth_cols", cols)
+    )
+    inner = depth_out(plan, "depth_rows", *rows)
+    outer = depth_out(plan, "depth_corners", *corners)
+    return filtered(plan, own, inner, outer, gains, adjoint)
 
 
 def variation(padded, row_count, col_count, row_whole, col_whole):
@@ -348,27 +410,31 @@
     )
 
 
-def ring(padded, rows, cols):
-    padded = jnp.concatenate([padded[-1:], padded[: rows + 1]], 0)
-    return jnp.concatenate([padded[:, -1:], padded[:, : cols + 1]], 1)
+def ring(block, around):
+    rows, cols, corners = around
+    after = jnp.concatenate([corners[0][:1, -1:], rows[0][:1], corners[0][:1, :1]], 1)
+    before = jnp.concatenate([corners[1][-1:, -1:], rows[1][-1:], corners[1][-1:, :1]], 1)
+    middle = jnp.concatenate([cols[:, -1:], block, cols[:, :1]], 1)
+    return jnp.concatenate([before, middle, after], 0)
 
 
 def shards(estimate, observed, psf):
     rows, cols, depth = estimate.shape
     plan = Plan(rows, cols, depth, psf.shape[0])
+    around = halos(estimate, plan.half)
     gains = transfer(plan, psf)
-    padded = with_halo(estimate, plan.half)
-    modes = filtered(plan, depth_out(plan, padded), gains, False)
+    modes = convolved(plan, estimate, around, gains, False)
     quotient = depth_home(plan, modes, observed, True)
+    quotient_around = halos(quotient, plan.half)
     divergence = variation(
-        ring(padded, rows, cols),
+        ring(estimate, around),
         rows,
         cols,
         rows * lax.axis_size("px"),
         cols * lax.axis_size("py"),
     )
     weight = estimate / (1.0 - penalty_weight * divergence)
-    modes = filtered(plan, depth_out(plan, with_halo(quotient, plan.half)), gains, True)
+    modes = convolved(plan, quotient, quotient_around, gains, True)
     return depth_home(plan, modes, weight, False)
 
 

time: 303 us -> 263 us (0.87)
  starting transfers between devices: 34.2 us -> 20.3 us
  other arithmetic: 42.9 us -> 31.3 us
  Pallas kernels: 160 us -> 149 us
    pallas_call x2, Pallas kernels: 86.7 us -> 56.1 us  [filtered(): pl.pallas_call(functools.partial(filter_kernel, adjoint), grid=(plan.mode...]
    pallas_call x2 -> x10, Pallas kernels: 37.4 us -> 57 us  [the longest x8 45.8 us: depth_out(): pl.pallas_call(functools.partial(depth_out_kernel, plan, len(pieces)), gr...]
    concatenate x4 -> x1, other arithmetic: 18.4 us -> 0.66 us  [ring(): return jnp.concatenate([before, middle, after], 0)]
    ppermute x16 -> x12, starting transfers between devices: 34.2 us -> 20.3 us  [the longest x6 15.4 us: neighbours(): lax.ppermute(after, axis, [((i + 1) % count, i) for i in range(count)])]
    unnamed x50 -> x48, local copies, waits for them, and re-layouts: 12.1 us -> 7.43 us
    ppermute x16 -> x12, waiting for transfers between devices: 32 us -> 30.1 us  [the longest x6 23.9 us: neighbours(): lax.ppermute(after, axis, [((i + 1) % count, i) for i in range(count)])]
    slice x8 -> x12, local copies, waits for them, and re-layouts: 11 us -> 10.2 us  [the longest x2 4.81 us: halos(): rows = neighbours('px', block[:width], block[-width:])]
  transfers between devices with their start and end apart: 16 -> 12, of which waited for: 5 -> 3; matrix products, arithmetic and copies ran while one was open for 15% -> 11% of each run, Pallas kernels for 4% -> 19%
where the time goes in v3:
time: 263 us; the launch traced here: 262 us
  Pallas kernels  149 us (57%)
  other arithmetic  31.3 us (12%)
  waiting for transfers between devices  30.1 us (11%)
  local copies, waits for them, and re-layouts  27.8 us (11%)
  starting transfers between devices  20.3 us (8%)
  matrix products  2.71 us (1%)
    pallas_call x2, Pallas kernels, filtered(): pl.pallas_call(functools.partial(filter_kernel, adjoint), grid=(plan.mode...  56.1 us
    pallas_call x8, Pallas kernels, depth_out(): pl.pallas_call(functools.partial(depth_out_kernel, plan, len(pieces)), gr...  45.8 us
    pallas_call x2, Pallas kernels, depth_home(): pl.pallas_call(functools.partial(depth_home_kernel, plan, divide), grid=(...  24.8 us
    ppermute x6, waiting for transfers between devices, neighbours(): lax.ppermute(after, axis, [((i + 1) % count, i) for i in range(count)])  23.9 us
    ppermute x6, starting transfers between devices, neighbours(): lax.ppermute(after, axis, [((i + 1) % count, i) for i in range(count)])  15.4 us
    pallas_call x2, Pallas kernels, cols_out(): pl.pallas_call(cols_kernel, grid=(plan.modes // step,), in_specs=[spec(pl...  11.1 us
    mul x1, other arithmetic, variation(): flux_cols = slope_cols * factor  11 us
    pallas_call x1, Pallas kernels, transfer(): pl.pallas_call(transfer_kernel, grid=(plan.modes // step,), in_specs=[pl....  11 us
  transfers between devices with their start and end apart: 12, of which 3 were waited for; matrix products, arithmetic and copies ran while one was open for 11% of the time, Pallas kernels for 19%

profile of v3, /device:TPU:1, one launch (start us, length us, event | category | flops | bytes accessed | tf_op | source)
XLA Modules:
  0.0 261.5 jit_solution(6015058152947855049)
XLA Ops:
  0.0 2.3 fusion.14
  2.4 2.6 collective-permute-start.1
  4.9 3.2 %fusion.13 = (f32[16,128,128]{2,1,0:T(8,128)}, f32[16,128,128]{2,1,0:T(8,128)}) fusion(f32[64,128,128]{2,1,0:T(8,128)} %refs_0_.1), kind=kLoop, calls=%fused_computation.34 | loop fusion | bytes 4194304 | tf_op jit(solution)/shard_map/slice | solution.py:368
  9.4 3.1 %collective-permute-start.2 = (f32[16,128,128]{2,1,0:T(8,128)}, f32[16,128,128]{2,1,0:T(8,128)S(1)}, u32[]{:S(2)}, u32[]{:S(2)}) collective-permute-start(f32[16,128,128]{2,1,0:T(8,128)} %get-tuple-element.14), channel_id=1, source_target_pairs={{4,0},{8,4},{12,8},{16,12},{20,16},{24,20},{28,24},{0,28},{5,1},{9... | collective-permute-start | bytes 3145736 | tf_op jit(solution)/shard_map/ppermute | solution.py:362
  13.8 2.9 %copy.14 = f32[65,32,32]{1,2,0:T(8,128)} copy(f32[65,32,32]{0,2,1:T(8,128)} %fusion.19) | data formatting | bytes 532480 | tf_op jit(solution)/shard_map/abc,ck->kba/dot_general | solution.py:244
  18.1 2.9 %copy.15 = f32[65,32,32]{1,2,0:T(8,128)} copy(f32[65,32,32]{0,2,1:T(8,128)} %fusion.20) | data formatting | bytes 532480 | tf_op jit(solution)/shard_map/abc,ck->kba/dot_general | solution.py:244
  21.0 1.8 select_maximum_fusion.psf_ref
  22.8 11.0 %transfer.1.transfer_ref = f32[65,160,256]{2,1,0:T(8,128)} custom-call(f32[65,32,256]{2,1,0:T(8,128)S(1)} %select_maximum_fusion.psf_ref, bf16[768,256]{1,0:T(8,128)(2,1)S(1)} %copy-done.9, bf16[320,96]{1,0:T(8,128)(2,1)S(1)} %copy-done.16), custom_call_target="tpu_custom_call" | custom-call | flops 8999999488 | bytes 14000000 | tf_op jit(solution)/shard_map/transfer/pallas_call | solution.py:255
  33.8 9.9 %depth_own.2.inner_ref = f32[65,128,128]{2,1,0:T(8,128)} custom-call(f32[64,128,128]{2,1,0:T(8,128)S(1)} %copy-done.2, bf16[144,384]{1,0:T(8,128)(2,1)S(1)} %copy-done.15), custom_call_target="tpu_custom_call" | custom-call | flops 7680000000 | bytes 8960000 | tf_op jit(solution)/shard_map/depth_own/pallas_call | solution.py:160
  46.2 1.9 depth_cols.2.outer_ref
  48.1 4.2 %collective-permute-start.4 = (f32[16,32,128]{2,1,0:T(8,128)S(1)}, f32[16,32,128]{2,1,0:T(8,128)S(1)}, u32[]{:S(2)}, u32[]{:S(2)}) collective-permute-start(f32[16,32,128]{2,1,0:T(8,128)S(1)} %get-tuple-element.20), channel_id=1, source_target_pairs={{4,0},{8,4},{12,8},{16,12},{20,16},{24,20},{28,24},{0,28},{5,1},{9... | collective-permute-start | bytes 786440 | tf_op jit(solution)/shard_map/ppermute | solution.py:362
  52.3 5.5 %cols_out.4.own_ref = f32[65,160,128]{2,1,0:T(8,128)} custom-call(f32[65,128,128]{2,1,0:T(8,128)S(1)} %copy-done.17, f32[65,32,128]{2,1,0:T(8,128)S(1)} %depth_cols.2.outer_ref, bf16[320,480]{1,0:T(8,128)(2,1)S(1)} %copy-done.10), custom_call_target="tpu_custom_call" | custom-call | flops 8000000000 | bytes 11000000 | tf_op jit(solution)/shard_map/cols_out/pallas_call | solution.py:205
  59.8 6.2 %collective-permute-done.5.refs_1_ = f32[16,32,128]{2,1,0:T(8,128)S(1)} collective-permute-done((f32[16,32,128]{2,1,0:T(8,128)S(1)}, f32[16,32,128]{2,1,0:T(8,128)S(1)}, u32[]{:S(2)}, u32[]{:S(2)}) %collective-permute-start.5) | collective-permute-done | bytes 262176 | tf_op jit(solution)/shard_map/ppermute | solution.py:363
  66.0 2.1 collective-permute-done.4.refs_0_
  69.8 9.5 %depth_rows.2.inner_ref = f32[65,128,128]{2,1,0:T(8,128)} custom-call(f32[16,128,128]{2,1,0:T(8,128)S(1)} %collective-permute-done.2.refs_0_, f32[16,128,128]{2,1,0:T(8,128)S(1)} %collective-permute-done.3.refs_1_, bf16[144,384]{1,0:T(8,128)(2,1)S(1)} %copy-done.15), custom_call_target="tpu_custom_call" | custom-call | flops 7680000000 | bytes 8960000 | tf_op jit(solution)/shard_map/depth_rows/pallas_call | solution.py:160
  79.3 28.2 %filtered.2.modes_ref = f32[65,128,128]{2,1,0:T(8,128)} custom-call(f32[65,160,128]{2,1,0:T(8,128)} %cols_out.4.own_ref, f32[65,128,128]{2,1,0:T(8,128)} %depth_rows.2.inner_ref, f32[65,32,128]{2,1,0:T(8,128)S(1)} %depth_corners.2.outer_ref, f32[65,160,256]{2,1,0:T(8,128)} %transfer.1.transfer_ref, bf16[768,256]{1,0:T(8,128)(2,1)S(1)} %copy-done.8, ...), custom_call_target="tpu_custom_call" | custom-call | flops 22000001024 | bytes 25000000 | tf_op jit(solution)/shard_map/filtered/pallas_call | solution.py:312
  107.5 12.1 %depth_home.2.refs_0_ = f32[64,128,128]{2,1,0:T(8,128)S(1)} custom-call(f32[65,128,128]{2,1,0:T(8,128)} %filtered.2.modes_ref, f32[64,128,128]{2,1,0:T(8,128)} %other_ref.1, bf16[240,256]{1,0:T(8,128)(2,1)S(1)} %copy-done.7), custom_call_target="tpu_custom_call" | custom-call | flops 3000000000 | bytes 13000000 | tf_op jit(solution)/shard_map/depth_home/pallas_call | solution.py:343
  122.3 2.1 copy-done.3
  127.2 7.6 %fusion.10 = (f32[65,129,128]{2,1,0:T(8,128)}, f32[65,129,128]{2,1,0:T(8,128)}) fusion(f32[65,130,128]{2,1,0:T(8,128)S(1)} %maximum_maximum_fusion, f32[1,1,128]{2,1,0:T(1,128)S(1)} %get-tuple-element.22, f32[1,128,128]{2,1,0:T(8,128)S(1)} %slice.141, f32[1,1,128]{2,1,0:T(1,128)S(1)} %get-tuple-element.21, f32[64,1,128]{2,1,0:T(1,128)S(1)} %slice.139, ...), kind=kLoop, calls=%fused_computation.31 | loop fusion | flops 17172480 | bytes 25758654 | tf_op jit(solution)/shard_map/mul | solution.py:401
  134.8 11.0 %fusion.9 = (f32[65,129,128]{2,1,0:T(8,128)}, f32[65,129,128]{2,1,0:T(8,128)}) fusion(f32[65,129,128]{2,1,0:T(8,128)} %get-tuple-element.6, f32[65,130,128]{2,1,0:T(8,128)} %copy-done.19, pred[129]{0:T(512)(128)(4,1)S(1)} %compare_and_fusion, f32[65,129,127]{2,1,0:T(8,128)} %copy-done.20), kind=kLoop, calls=%fused_computation.24 | loop fusion | flops 4293120 | bytes 25725308 | tf_op jit(solution)/shard_map/mul | solution.py:402
  145.9 3.0 %slice.155 = f32[64,128,127]{2,1,0:T(8,128)S(1)} slice(f32[65,129,128]{2,1,0:T(8,128)} %get-tuple-element.8), slice={[1:65], [1:129], [0:127]} | slice | bytes 8323072 | tf_op jit(solution)/shard_map/slice | solution.py:404
  150.9 3.0 %collective-permute-start.8 = (f32[16,128,128]{2,1,0:T(8,128)}, f32[16,128,128]{2,1,0:T(8,128)S(1)}, u32[]{:S(2)}, u32[]{:S(2)}) collective-permute-start(f32[16,128,128]{2,1,0:T(8,128)} %get-tuple-element.10), channel_id=1, source_target_pairs={{4,0},{8,4},{12,8},{16,12},{20,16},{24,20},{28,24},{0,28},{5,1},{9... | collective-permute-start | bytes 3145736 | tf_op jit(solution)/shard_map/ppermute | solution.py:362
  153.9 9.0 %fusion.7.other_ref = f32[64,128,128]{2,1,0:T(8,128)S(1)} fusion(f32[64,128,128]{2,1,0:T(8,128)S(1)} %copy-done.4, f32[65,129,128]{2,1,0:T(8,128)} %get-tuple-element.8, f32[65,129,128]{2,1,0:T(8,128)} %get-tuple-element.7, f32[65,129,128]{2,1,0:T(8,128)} %get-tuple-element.5, f32[64,128,127]{2,1,0:T(8,128)S(1)} %slice.155), kind=kLoop, calls=%fused_computation.17 | loop fusion | flops 8388608 | bytes 33521664 | tf_op jit(solution)/shard_map/div | solution.py:436
  162.9 9.8 %depth_own.3.inner_ref = f32[65,128,128]{2,1,0:T(8,128)} custom-call(f32[64,128,128]{2,1,0:T(8,128)S(1)} %copy-done.6, bf16[144,384]{1,0:T(8,128)(2,1)S(1)} %copy-done.15), custom_call_target="tpu_custom_call" | custom-call | flops 7680000000 | bytes 8960000 | tf_op jit(solution)/shard_map/depth_own/pallas_call | solution.py:160
  173.9 4.2 %collective-permute-start.10 = (f32[16,32,128]{2,1,0:T(8,128)S(1)}, f32[16,32,128]{2,1,0:T(8,128)S(1)}, u32[]{:S(2)}, u32[]{:S(2)}) collective-permute-start(f32[16,32,128]{2,1,0:T(8,128)S(1)} %get-tuple-element.18), channel_id=1, source_target_pairs={{4,0},{8,4},{12,8},{16,12},{20,16},{24,20},{28,24},{0,28},{5,1},{9... | collective-permute-start | bytes 786440 | tf_op jit(solution)/shard_map/ppermute | solution.py:362
  178.2 1.9 depth_cols.3.outer_ref
  180.0 2.2 copy-done.18
  182.2 5.6 %cols_out.5.own_ref = f32[65,160,128]{2,1,0:T(8,128)} custom-call(f32[65,128,128]{2,1,0:T(8,128)S(1)} %copy-done.18, f32[65,32,128]{2,1,0:T(8,128)S(1)} %depth_cols.3.outer_ref, bf16[320,480]{1,0:T(8,128)(2,1)S(1)} %copy-done.10), custom_call_target="tpu_custom_call" | custom-call | flops 8000000000 | bytes 11000000 | tf_op jit(solution)/shard_map/cols_out/pallas_call | solution.py:205
  187.8 21.8 %collective-permute-done.10.refs_0_ = f32[16,32,128]{2,1,0:T(8,128)S(1)} collective-permute-done((f32[16,32,128]{2,1,0:T(8,128)S(1)}, f32[16,32,128]{2,1,0:T(8,128)S(1)}, u32[]{:S(2)}, u32[]{:S(2)}) %collective-permute-start.10) | collective-permute-done | bytes 262176 | tf_op jit(solution)/shard_map/ppermute | solution.py:362
  211.4 9.5 %depth_rows.3.inner_ref = f32[65,128,128]{2,1,0:T(8,128)} custom-call(f32[16,128,128]{2,1,0:T(8,128)S(1)} %collective-permute-done.8.refs_0_, f32[16,128,128]{2,1,0:T(8,128)S(1)} %collective-permute-done.9.refs_1_, bf16[144,384]{1,0:T(8,128)(2,1)S(1)} %copy-done.15), custom_call_target="tpu_custom_call" | custom-call | flops 7680000000 | bytes 8960000 | tf_op jit(solution)/shard_map/depth_rows/pallas_call | solution.py:160
  220.9 27.9 %filtered.3.modes_ref = f32[65,128,128]{2,1,0:T(8,128)} custom-call(f32[65,160,128]{2,1,0:T(8,128)} %cols_out.5.own_ref, f32[65,128,128]{2,1,0:T(8,128)} %depth_rows.3.inner_ref, f32[65,32,128]{2,1,0:T(8,128)S(1)} %depth_corners.3.outer_ref, f32[65,160,256]{2,1,0:T(8,128)} %transfer.1.transfer_ref, bf16[768,256]{1,0:T(8,128)(2,1)S(1)} %copy-done.8, ...), custom_call_target="tpu_custom_call" | custom-call | flops 22000001024 | bytes 25000000 | tf_op jit(solution)/shard_map/filtered/pallas_call | solution.py:312
  248.9 12.7 %depth_home.3 = f32[64,128,128]{2,1,0:T(8,128)} custom-call(f32[65,128,128]{2,1,0:T(8,128)} %filtered.3.modes_ref, f32[64,128,128]{2,1,0:T(8,128)S(1)} %fusion.7.other_ref, bf16[240,256]{1,0:T(8,128)(2,1)S(1)} %copy-done.7), custom_call_target="tpu_custom_call" | custom-call | flops 3000000000 | bytes 13000000 | tf_op jit(solution)/shard_map/depth_home/pallas_call | solution.py:343
  (82 shorter events, 20.6 us)
Async XLA Ops:
  0.0 12.5 %copy-start = (f32[32,32,32]{2,1,0:T(8,128)S(1)}, f32[32,32,32]{2,1,0:T(8,128)}, u32[]{:S(2)}) copy-start(f32[32,32,32]{2,1,0:T(8,128)} %param.15) | copy-start | bytes 393220
  0.0 12.5 %copy-start.21 = (f32[32,65,1]{1,0,2:T(8,128)S(1)}, f32[32,65,1]{1,0,2:T(8,128)}, u32[]{:S(2)}) copy-start(f32[32,65,1]{1,0,2:T(8,128)} %constant.73) | copy-start | bytes 24964
  0.0 16.7 %copy-start.22 = (f32[32,65,1]{1,0,2:T(8,128)S(1)}, f32[32,65,1]{1,0,2:T(8,128)}, u32[]{:S(2)}) copy-start(f32[32,65,1]{1,0,2:T(8,128)} %constant.74) | copy-start | bytes 24964
  2.3 41.4 %collective-permute-start = (f32[64,16,128]{2,1,0:T(8,128)}, f32[64,16,128]{2,1,0:T(8,128)}, u32[]{:S(2)}, u32[]{:S(2)}) collective-permute-start(f32[64,16,128]{2,1,0:T(8,128)} %get-tuple-element.16), channel_id=1, source_target_pairs={{1,0},{2,1},{3,2},{0,3},{5,4},{6,5},{7,6},{4,7},{9,8},{10,9},{11,1... | collective-permute-start | bytes 1572872 | tf_op jit(solution)/shard_map/ppermute | solution.py:362
  2.4 42.5 %collective-permute-start.1 = (f32[64,16,128]{2,1,0:T(8,128)}, f32[64,16,128]{2,1,0:T(8,128)}, u32[]{:S(2)}, u32[]{:S(2)}) collective-permute-start(f32[64,16,128]{2,1,0:T(8,128)} %get-tuple-element.15), channel_id=1, source_target_pairs={{0,1},{1,2},{2,3},{3,0},{4,5},{5,6},{6,7},{7,4},{8,9},{9,10},{10,1... | collective-permute-start | bytes 1572872 | tf_op jit(solution)/shard_map/ppermute | solution.py:363
  8.1 61.7 %collective-permute-start.3 = (f32[16,128,128]{2,1,0:T(8,128)}, f32[16,128,128]{2,1,0:T(8,128)S(1)}, u32[]{:S(2)}, u32[]{:S(2)}) collective-permute-start(f32[16,128,128]{2,1,0:T(8,128)} %get-tuple-element.13), channel_id=1, source_target_pairs={{0,4},{4,8},{8,12},{12,16},{16,20},{20,24},{24,28},{28,0},{1,5},{5... | collective-permute-start | bytes 3145736 | tf_op jit(solution)/shard_map/ppermute | solution.py:363
  9.4 13.4 %copy-start.9 = (bf16[768,256]{1,0:T(8,128)(2,1)S(1)}, bf16[768,256]{1,0:T(8,128)(2,1)}, u32[]{:S(2)}) copy-start(bf16[768,256]{1,0:T(8,128)(2,1)} %constant.57.clone.rows_ref) | copy-start | bytes 1179652
  9.4 13.4 %copy-start.16 = (bf16[320,96]{1,0:T(8,128)(2,1)S(1)}, bf16[320,96]{1,0:T(8,128)(2,1)}, u32[]{:S(2)}) copy-start(bf16[320,96]{1,0:T(8,128)(2,1)} %constant.58.clone.cols_ref) | copy-start | bytes 184324
  9.4 60.4 %collective-permute-start.2 = (f32[16,128,128]{2,1,0:T(8,128)}, f32[16,128,128]{2,1,0:T(8,128)S(1)}, u32[]{:S(2)}, u32[]{:S(2)}) collective-permute-start(f32[16,128,128]{2,1,0:T(8,128)} %get-tuple-element.14), channel_id=1, source_target_pairs={{4,0},{8,4},{12,8},{16,12},{20,16},{24,20},{28,24},{0,28},{5,1},{9... | collective-permute-start | bytes 3145736 | tf_op jit(solution)/shard_map/ppermute | solution.py:362
  22.8 11.0 %copy-start.2 = (f32[64,128,128]{2,1,0:T(8,128)S(1)}, f32[64,128,128]{2,1,0:T(8,128)}, u32[]{:S(2)}) copy-start(f32[64,128,128]{2,1,0:T(8,128)} %refs_0_.1) | copy-start | bytes 12582916
  22.8 11.0 %copy-start.15 = (bf16[144,384]{1,0:T(8,128)(2,1)S(1)}, bf16[144,384]{1,0:T(8,128)(2,1)}, u32[]{:S(2)}) copy-start(bf16[144,384]{1,0:T(8,128)(2,1)} %constant.59.clone.refs_1_.refs_2_) | copy-start | bytes 331780
  44.8 7.5 %copy-start.10 = (bf16[320,480]{1,0:T(8,128)(2,1)S(1)}, bf16[320,480]{1,0:T(8,128)(2,1)}, u32[]{:S(2)}) copy-start(bf16[320,480]{1,0:T(8,128)(2,1)} %constant.60.clone.table_ref.cols_out) | copy-start | bytes 921604
  44.8 7.5 %copy-start.17 = (f32[65,128,128]{2,1,0:T(8,128)S(1)}, f32[65,128,128]{2,1,0:T(8,128)}, u32[]{:S(2)}) copy-start(f32[65,128,128]{2,1,0:T(8,128)} %depth_own.2.inner_ref) | copy-start | bytes 12779524
  48.1 17.9 %collective-permute-start.5 = (f32[16,32,128]{2,1,0:T(8,128)S(1)}, f32[16,32,128]{2,1,0:T(8,128)S(1)}, u32[]{:S(2)}, u32[]{:S(2)}) collective-permute-start(f32[16,32,128]{2,1,0:T(8,128)S(1)} %get-tuple-element.19), channel_id=1, source_target_pairs={{0,4},{4,8},{8,12},{12,16},{16,20},{20,24},{24,28},{28,0},{1,5},{5... | collective-permute-start | bytes 786440 | tf_op jit(solution)/shard_map/ppermute | solution.py:363
  48.1 19.9 %collective-permute-start.4 = (f32[16,32,128]{2,1,0:T(8,128)S(1)}, f32[16,32,128]{2,1,0:T(8,128)S(1)}, u32[]{:S(2)}, u32[]{:S(2)}) collective-permute-start(f32[16,32,128]{2,1,0:T(8,128)S(1)} %get-tuple-element.20), channel_id=1, source_target_pairs={{4,0},{8,4},{12,8},{16,12},{20,16},{24,20},{28,24},{0,28},{5,1},{9... | collective-permute-start | bytes 786440 | tf_op jit(solution)/shard_map/ppermute | solution.py:362
  69.8 9.5 %copy-start.8 = (bf16[768,256]{1,0:T(8,128)(2,1)S(1)}, bf16[768,256]{1,0:T(8,128)(2,1)}, u32[]{:S(2)}) copy-start(bf16[768,256]{1,0:T(8,128)(2,1)} %constant.61.clone.rows_out) | copy-start | bytes 1179652
  69.8 9.5 %copy-start.11 = (bf16[256,480]{1,0:T(8,128)(2,1)S(1)}, bf16[256,480]{1,0:T(8,128)(2,1)}, u32[]{:S(2)}) copy-start(bf16[256,480]{1,0:T(8,128)(2,1)} %constant.62.clone.cols_home) | copy-start | bytes 737284
  69.8 9.5 %copy-start.13 = (bf16[768,128]{1,0:T(8,128)(2,1)S(1)}, bf16[768,128]{1,0:T(8,128)(2,1)}, u32[]{:S(2)}) copy-start(bf16[768,128]{1,0:T(8,128)(2,1)} %constant.63.clone.rows_home) | copy-start | bytes 589828
  79.3 28.2 %copy-start.7 = (bf16[240,256]{1,0:T(8,128)(2,1)S(1)}, bf16[240,256]{1,0:T(8,128)(2,1)}, u32[]{:S(2)}) copy-start(bf16[240,256]{1,0:T(8,128)(2,1)} %constant.64.clone.table_ref) | copy-start | bytes 368644
  119.6 5.4 %copy-start.5 = (f32[64,128,128]{2,1,0:T(8,128)}, f32[64,128,128]{2,1,0:T(8,128)S(1)}, u32[]{:S(2)}) copy-start(f32[64,128,128]{2,1,0:T(8,128)S(1)} %depth_home.2.refs_0_) | copy-start | bytes 12582916
  126.3 8.5 %copy-start.20 = (f32[65,129,127]{2,1,0:T(8,128)}, f32[65,129,127]{2,1,0:T(8,128)S(1)}, u32[]{:S(2)}) copy-start(f32[65,129,127]{2,1,0:T(8,128)S(1)} %slice_subtract_fusion) | copy-start | bytes 12778744
  145.9 8.0 %copy-start.4 = (f32[64,128,128]{2,1,0:T(8,128)S(1)}, f32[64,128,128]{2,1,0:T(8,128)}, u32[]{:S(2)}) copy-start(f32[64,128,128]{2,1,0:T(8,128)} %refs_0_.1) | copy-start | bytes 12582916
  148.9 23.8 %collective-permute-start.6 = (f32[64,16,128]{2,1,0:T(8,128)}, f32[64,16,128]{2,1,0:T(8,128)}, u32[]{:S(2)}, u32[]{:S(2)}) collective-permute-start(f32[64,16,128]{2,1,0:T(8,128)} %get-tuple-element.12), channel_id=1, source_target_pairs={{1,0},{2,1},{3,2},{0,3},{5,4},{6,5},{7,6},{4,7},{9,8},{10,9},{11,1... | collective-permute-start | bytes 1572872 | tf_op jit(solution)/shard_map/ppermute | solution.py:362
  149.8 24.0 %collective-permute-start.7 = (f32[64,16,128]{2,1,0:T(8,128)}, f32[64,16,128]{2,1,0:T(8,128)S(1)}, u32[]{:S(2)}, u32[]{:S(2)}) collective-permute-start(f32[64,16,128]{2,1,0:T(8,128)} %get-tuple-element.11), channel_id=1, source_target_pairs={{0,1},{1,2},{2,3},{3,0},{4,5},{5,6},{6,7},{7,4},{8,9},{9,10},{10,1... | collective-permute-start | bytes 1572872 | tf_op jit(solution)/shard_map/ppermute | solution.py:363
  150.9 60.5 %collective-permute-start.8 = (f32[16,128,128]{2,1,0:T(8,128)}, f32[16,128,128]{2,1,0:T(8,128)S(1)}, u32[]{:S(2)}, u32[]{:S(2)}) collective-permute-start(f32[16,128,128]{2,1,0:T(8,128)} %get-tuple-element.10), channel_id=1, source_target_pairs={{4,0},{8,4},{12,8},{16,12},{20,16},{24,20},{28,24},{0,28},{5,1},{9... | collective-permute-start | bytes 3145736 | tf_op jit(solution)/shard_map/ppermute | solution.py:362
  153.9 57.6 %collective-permute-start.9 = (f32[16,128,128]{2,1,0:T(8,128)}, f32[16,128,128]{2,1,0:T(8,128)S(1)}, u32[]{:S(2)}, u32[]{:S(2)}) collective-permute-start(f32[16,128,128]{2,1,0:T(8,128)} %get-tuple-element.9), channel_id=1, source_target_pairs={{0,4},{4,8},{8,12},{12,16},{16,20},{20,24},{24,28},{28,0},{1,5},{5... | collective-permute-start | bytes 3145736 | tf_op jit(solution)/shard_map/ppermute | solution.py:363
  153.9 9.0 %copy-start.6 = (f32[64,128,128]{2,1,0:T(8,128)S(1)}, f32[64,128,128]{2,1,0:T(8,128)}, u32[]{:S(2)}) copy-start(f32[64,128,128]{2,1,0:T(8,128)} %copy-done.5) | copy-start | bytes 12582916
  173.9 35.7 %collective-permute-start.10 = (f32[16,32,128]{2,1,0:T(8,128)S(1)}, f32[16,32,128]{2,1,0:T(8,128)S(1)}, u32[]{:S(2)}, u32[]{:S(2)}) collective-permute-start(f32[16,32,128]{2,1,0:T(8,128)S(1)} %get-tuple-element.18), channel_id=1, source_target_pairs={{4,0},{8,4},{12,8},{16,12},{20,16},{24,20},{28,24},{0,28},{5,1},{9... | collective-permute-start | bytes 786440 | tf_op jit(solution)/shard_map/ppermute | solution.py:362
  178.1 31.5 %collective-permute-start.11 = (f32[16,32,128]{2,1,0:T(8,128)S(1)}, f32[16,32,128]{2,1,0:T(8,128)S(1)}, u32[]{:S(2)}, u32[]{:S(2)}) collective-permute-start(f32[16,32,128]{2,1,0:T(8,128)S(1)} %get-tuple-element.17), channel_id=1, source_target_pairs={{0,4},{4,8},{8,12},{12,16},{16,20},{20,24},{24,28},{28,0},{1,5},{5... | collective-permute-start | bytes 786440 | tf_op jit(solution)/shard_map/ppermute | solution.py:363
  211.4 9.6 %copy-start.12 = (bf16[256,480]{1,0:T(8,128)(2,1)S(1)}, bf16[256,480]{1,0:T(8,128)(2,1)}, u32[]{:S(2)}) copy-start(bf16[256,480]{1,0:T(8,128)(2,1)} %constant.62.clone.cols_home) | copy-start | bytes 737284
  211.4 9.5 %copy-start.14 = (bf16[768,128]{1,0:T(8,128)(2,1)S(1)}, bf16[768,128]{1,0:T(8,128)(2,1)}, u32[]{:S(2)}) copy-start(bf16[768,128]{1,0:T(8,128)(2,1)} %constant.63.clone.rows_home) | copy-start | bytes 589828
  220.9 40.6 %copy-start.1 = (f32[32,32,32]{2,1,0:T(8,128)S(1)}, f32[32,32,32]{2,1,0:T(8,128)}, u32[]{:S(2)}) copy-start(f32[32,32,32]{2,1,0:T(8,128)} %param.15) | copy-start | bytes 393220
  (3 other events, 9.1 us)

commit v4 on v3

--- a/solution.py
+++ b/solution.py
@@ -126,6 +126,10 @@
 
 def cost(flops, moved):
     return pl.CostEstimate(flops=int(flops), bytes_accessed=int(moved), transcendentals=0)
+
+
+def beside():
+    return cost(1e6, 1e5)
 
 
 def depth_out_kernel(plan, count, *refs):
@@ -168,7 +172,7 @@
         out_specs=pl.BlockSpec((plan.modes, ROWS, LANES), lambda i: (0, i, 0)),
         out_shape=jax.ShapeDtypeStruct((plan.modes, cols, LANES), jnp.float32),
         compiler_params=params(),
-        cost_estimate=cost(6e7 * cols, 7e4 * cols),
+        cost_estimate=beside(),
         name=name,
     )(*pieces, plan.depth_out)
 
@@ -209,7 +213,7 @@
         out_specs=spec(plan.col_whole),
         out_shape=jax.ShapeDtypeStruct((plan.modes, plan.col_whole, LANES), jnp.float32),
         compiler_params=params(),
-        cost_estimate=cost(8e9, 1.1e7),
+        cost_estimate=beside(),
         name="cols_out",
     )(inner, outer, plan.cols_out)
 
@@ -263,7 +267,7 @@
         out_specs=pl.BlockSpec((step, plan.col_whole, 2 * LANES), lambda i: (i, 0, 0)),
         out_shape=jax.ShapeDtypeStruct((plan.modes, plan.col_whole, 2 * LANES), jnp.float32),
         compiler_params=params(),
-        cost_estimate=cost(9e9, 1.4e7),
+        cost_estimate=beside(),
         name="transfer",
     )(modes, plan.rows_psf, plan.cols_psf)
 
@@ -381,41 +385,74 @@
     return filtered(plan, own, inner, outer, gains, adjoint)
 
 
-def variation(padded, row_count, col_count, row_whole, col_whole):
-    region = padded[:-1, :-1]
-    row_global = lax.axis_index("px") * row_count - 1 + jnp.arange(row_count + 1)
-    col_global = lax.axis_index("py") * col_count - 1 + jnp.arange(col_count + 1)
-    row_valid = ((row_global >= 0) & (row_global <= row_whole - 2))[:, None, None]
-    col_valid = ((col_global >= 0) & (col_global <= col_whole - 2))[None, :, None]
-    slope_rows = jnp.where(row_valid, padded[1:, :-1] - region, 0.0)
-    slope_cols = jnp.where(col_valid, padded[:-1, 1:] - region, 0.0)
-    slope_depth = jnp.concatenate(
-        [region[:, :, 1:] - region[:, :, :-1], jnp.zeros_like(region[:, :, :1])], 2
+def variation_kernel(whole, volume_ref, out_ref):
+    step, cols, depth = out_ref.shape
+    size = volume_ref.shape[1]
+    row_start = pl.program_id(0) * step
+    row_first = lax.axis_index("px") * (whole[0] // lax.axis_size("px")) + row_start - 1
+    col_first = lax.axis_index("py") * cols
+    sub = lax.broadcasted_iota(jnp.int32, (size, depth), 0)
+    lane = lax.broadcasted_iota(jnp.int32, (size, depth), 1)
+    col = col_first + jnp.where(sub <= cols, sub, sub - size)
+    col_valid = (col >= 0) & (col <= whole[1] - 2)
+    here = volume_ref[row_start]
+    before = None
+    for r in range(step + 1):
+        after = volume_ref[row_start + r + 1]
+        row = row_first + r
+        row_valid = ((row >= 0) & (row <= whole[0] - 2)).astype(jnp.float32)
+        slope_rows = (after - here) * row_valid
+        slope_cols = jnp.where(col_valid, pltpu.roll(here, size - 1, 0) - here, 0.0)
+        slope_depth = jnp.where(lane < depth - 1, pltpu.roll(here, depth - 1, 1) - here, 0.0)
+        factor = lax.rsqrt(
+            slope_rows * slope_rows
+            + slope_cols * slope_cols
+            + slope_depth * slope_depth
+            + smoothing * smoothing
+        )
+        flux_rows = slope_rows * factor
+        if r > 0:
+            flux_cols = slope_cols * factor
+            flux_depth = slope_depth * factor
+            divergence = (
+                (flux_rows - before)
+                + (flux_cols - pltpu.roll(flux_cols, 1, 0))
+                + (flux_depth - jnp.where(lane > 0, pltpu.roll(flux_depth, 1, 1), 0.0))
+            )
+            out_ref[r - 1] = (here / (1.0 - penalty_weight * divergence))[:cols]
+        before = flux_rows
+        here = after
+
+
+def weighted(block, around):
+    rows, cols, corners = around
+    stack = [
+        jnp.concatenate([corners[1][-1:], rows[1][-1:]], 1),
+        jnp.concatenate([cols, block], 1),
+        jnp.concatenate([corners[0][:1], rows[0][:1]], 1),
+    ]
+    edge, size = cols.shape[1], block.shape[1]
+    volume = jnp.concatenate(
+        [
+            jnp.concatenate(
+                [part[:, edge:], part[:, :1], part[:, edge - ROWS + 1 : edge]], 1
+            )
+            for part in stack
+        ],
+        0,
     )
-    factor = lax.rsqrt(
-        slope_rows * slope_rows
-        + slope_cols * slope_cols
-        + slope_depth * slope_depth
-        + smoothing * smoothing
-    )
-    flux_rows = slope_rows * factor
-    flux_cols = slope_cols * factor
-    flux_depth = (slope_depth * factor)[1:, 1:]
-    before = jnp.concatenate([jnp.zeros_like(flux_depth[:, :, :1]), flux_depth[:, :, :-1]], 2)
-    return (
-        flux_rows[1:, 1:]
-        - flux_rows[:-1, 1:]
-        + (flux_cols[1:, 1:] - flux_cols[1:, :-1])
-        + (flux_depth - before)
-    )
-
-
-def ring(block, around):
-    rows, cols, corners = around
-    after = jnp.concatenate([corners[0][:1, -1:], rows[0][:1], corners[0][:1, :1]], 1)
-    before = jnp.concatenate([corners[1][-1:, -1:], rows[1][-1:], corners[1][-1:, :1]], 1)
-    middle = jnp.concatenate([cols[:, -1:], block, cols[:, :1]], 1)
-    return jnp.concatenate([before, middle, after], 0)
+    whole = (block.shape[0] * lax.axis_size("px"), size * lax.axis_size("py"))
+    step = ROWS
+    return pl.pallas_call(
+        functools.partial(variation_kernel, whole),
+        grid=(block.shape[0] // step,),
+        in_specs=[whole_spec(volume)],
+        out_specs=pl.BlockSpec((step,) + block.shape[1:], lambda i: (i, 0, 0)),
+        out_shape=jax.ShapeDtypeStruct(block.shape, jnp.float32),
+        compiler_params=params(),
+        cost_estimate=beside(),
+        name="weighted",
+    )(volume)
 
 
 def shards(estimate, observed, psf):
@@ -426,14 +463,7 @@
     modes = convolved(plan, estimate, around, gains, False)
     quotient = depth_home(plan, modes, observed, True)
     quotient_around = halos(quotient, plan.half)
-    divergence = variation(
-        ring(estimate, around),
-        rows,
-        cols,
-        rows * lax.axis_size("px"),
-        cols * lax.axis_size("py"),
-    )
-    weight = estimate / (1.0 - penalty_weight * divergence)
+    weight = weighted(estimate, around)
     modes = convolved(plan, quotient, quotient_around, gains, True)
     return depth_home(plan, modes, weight, False)
 

time: 263 us -> 242 us (0.920)
  other arithmetic: 31.3 us -> 3.75 us
  Pallas kernels: 149 us -> 163 us
  local copies, waits for them, and re-layouts: 27.8 us -> 20 us
  waiting for transfers between devices: 30.1 us -> 27 us
    mul x2 -> x0, other arithmetic: 18.7 us -> none  [the longest x1 11 us: variation(): flux_cols = slope_cols * factor]
    ppermute x6, waiting for transfers between devices: 23.9 us -> 9.09 us  [neighbours(): lax.ppermute(after, axis, [((i + 1) % count, i) for i in range(count)])]
    ppermute x6, waiting for transfers between devices: 6.25 us -> 17.9 us  [neighbours(): lax.ppermute(before, axis, [(i, (i + 1) % count) for i in range(count)])]
    div x1 -> x0, other arithmetic: 8.97 us -> none  [shards(): weight = estimate / (1.0 - penalty_weight * divergence)]
    pallas_call x0 -> x1, Pallas kernels: none -> 7.9 us  [weighted(): pl.pallas_call(functools.partial(variation_kernel, whole), grid=(block.sh...]
    pallas_call x8, Pallas kernels: 45.8 us -> 50.8 us  [depth_out(): pl.pallas_call(functools.partial(depth_out_kernel, plan, len(pieces)), gr...]
    slice x7 -> x9, local copies, waits for them, and re-layouts: 4.98 us -> 1.86 us  [the longest x3 0.97 us: weighted(): part[:, :1]]
    concatenate x1, other arithmetic: 0.66 us -> 3.53 us  [weighted(): jnp.concatenate([jnp.concatenate([part[:, edge:], part[:, :1], part[:, ed...]
  transfers between devices with their start and end apart: 12 -> 12, of which waited for: 3 -> 5; matrix products, arithmetic and copies ran while one was open for 11% -> 8% of each run, Pallas kernels for 19% -> 24%
where the time goes in v4:
time: 242 us; the launch traced here: 239 us
  Pallas kernels  163 us (67%)
  waiting for transfers between devices  27 us (11%)
  starting transfers between devices  22.5 us (9%)
  local copies, waits for them, and re-layouts  20 us (8%)
  other arithmetic  3.75 us (2%)
  matrix products  2.73 us (1%)
    pallas_call x2, Pallas kernels, filtered(): pl.pallas_call(functools.partial(filter_kernel, adjoint), grid=(plan.mode...  57 us
    pallas_call x8, Pallas kernels, depth_out(): pl.pallas_call(functools.partial(depth_out_kernel, plan, len(pieces)), gr...  50.8 us
    pallas_call x2, Pallas kernels, depth_home(): pl.pallas_call(functools.partial(depth_home_kernel, plan, divide), grid=(...  24.8 us
    ppermute x6, waiting for transfers between devices, neighbours(): lax.ppermute(before, axis, [(i, (i + 1) % count) for i in range(count)])  17.9 us
    ppermute x6, starting transfers between devices, neighbours(): lax.ppermute(after, axis, [((i + 1) % count, i) for i in range(count)])  16.3 us
    pallas_call x2, Pallas kernels, cols_out(): pl.pallas_call(cols_kernel, grid=(plan.modes // step,), in_specs=[spec(pl...  11.3 us
    pallas_call x1, Pallas kernels, transfer(): pl.pallas_call(transfer_kernel, grid=(plan.modes // step,), in_specs=[pl....  11 us
    ppermute x6, waiting for transfers between devices, neighbours(): lax.ppermute(after, axis, [((i + 1) % count, i) for i in range(count)])  9.09 us
  transfers between devices with their start and end apart: 12, of which 5 were waited for; matrix products, arithmetic and copies ran while one was open for 8% of the time, Pallas kernels for 24%

profile of v4, /device:TPU:1, one launch (start us, length us, event | category | flops | bytes accessed | tf_op | source)
XLA Modules:
  0.0 239.3 jit_solution(8632701313251073753)
XLA Ops:
  1.3 2.7 %collective-permute-start.1 = (f32[64,16,128]{2,1,0:T(8,128)S(1)}, f32[64,16,128]{2,1,0:T(8,128)S(1)}, u32[]{:S(2)}, u32[]{:S(2)}) collective-permute-start(f32[64,16,128]{2,1,0:T(8,128)S(1)} %get-tuple-element.11), channel_id=1, source_target_pairs={{0,1},{1,2},{2,3},{3,0},{4,5},{5,6},{6,7},{7,4},{8,9},{9,10},{10,1... | collective-permute-start | bytes 1572872 | tf_op jit(solution)/shard_map/ppermute | solution.py:367
  4.0 3.1 %fusion.2 = (f32[16,128,128]{2,1,0:T(8,128)}, f32[16,128,128]{2,1,0:T(8,128)}) fusion(f32[64,128,128]{2,1,0:T(8,128)} %refs_0_.1), kind=kLoop, calls=%fused_computation.10 | loop fusion | bytes 4194304 | tf_op jit(solution)/shard_map/slice | solution.py:372
  8.4 3.0 %collective-permute-start.2 = (f32[16,128,128]{2,1,0:T(8,128)}, f32[16,128,128]{2,1,0:T(8,128)}, u32[]{:S(2)}, u32[]{:S(2)}) collective-permute-start(f32[16,128,128]{2,1,0:T(8,128)} %get-tuple-element.10), channel_id=1, source_target_pairs={{4,0},{8,4},{12,8},{16,12},{20,16},{24,20},{28,24},{0,28},{5,1},{9... | collective-permute-start | bytes 3145736 | tf_op jit(solution)/shard_map/ppermute | solution.py:366
  12.8 3.3 %collective-permute-done = f32[64,16,128]{2,1,0:T(8,128)S(1)} collective-permute-done((f32[64,16,128]{2,1,0:T(8,128)S(1)}, f32[64,16,128]{2,1,0:T(8,128)S(1)}, u32[]{:S(2)}, u32[]{:S(2)}) %collective-permute-start) | collective-permute-done | bytes 524320 | tf_op jit(solution)/shard_map/ppermute | solution.py:366
  17.2 2.0 collective-permute-start.5
  19.2 3.1 %collective-permute-start.4 = (f32[16,32,128]{2,1,0:T(8,128)}, f32[16,32,128]{2,1,0:T(8,128)S(1)}, u32[]{:S(2)}, u32[]{:S(2)}) collective-permute-start(f32[16,32,128]{2,1,0:T(8,128)} %get-tuple-element.16), channel_id=1, source_target_pairs={{4,0},{8,4},{12,8},{16,12},{20,16},{24,20},{28,24},{0,28},{5,1},{9... | collective-permute-start | bytes 786440 | tf_op jit(solution)/shard_map/ppermute | solution.py:366
  23.7 2.9 %copy.15 = f32[65,32,32]{1,2,0:T(8,128)} copy(f32[65,32,32]{0,2,1:T(8,128)} %fusion.7) | data formatting | bytes 532480 | tf_op jit(solution)/shard_map/abc,ck->kba/dot_general | solution.py:248
  26.6 2.9 %copy.14 = f32[65,32,32]{1,2,0:T(8,128)} copy(f32[65,32,32]{0,2,1:T(8,128)} %fusion.6) | data formatting | bytes 532480 | tf_op jit(solution)/shard_map/abc,ck->kba/dot_general | solution.py:248
  29.5 2.2 copy-done.2
  31.7 9.8 %depth_own.2.inner_ref = f32[65,128,128]{2,1,0:T(8,128)} custom-call(f32[64,128,128]{2,1,0:T(8,128)S(1)} %copy-done.2, bf16[144,384]{1,0:T(8,128)(2,1)S(1)} %copy-done.6), custom_call_target="tpu_custom_call" | custom-call | flops 1000000 | bytes 100000 | tf_op jit(solution)/shard_map/depth_own/pallas_call | solution.py:164
  42.4 11.0 %transfer.1.transfer_ref = f32[65,160,256]{2,1,0:T(8,128)} custom-call(f32[65,32,256]{2,1,0:T(8,128)S(1)} %select_maximum_fusion.psf_ref, bf16[768,256]{1,0:T(8,128)(2,1)S(1)} %copy-done.10, bf16[320,96]{1,0:T(8,128)(2,1)S(1)} %copy-done.11), custom_call_target="tpu_custom_call" | custom-call | flops 1000000 | bytes 100000 | tf_op jit(solution)/shard_map/transfer/pallas_call | solution.py:259
  53.4 1.9 depth_cols.2.outer_ref
  55.4 5.7 %cols_out.4.own_ref = f32[65,160,128]{2,1,0:T(8,128)} custom-call(f32[65,128,128]{2,1,0:T(8,128)S(1)} %bitcast.11, f32[65,32,128]{2,1,0:T(8,128)S(1)} %depth_cols.2.outer_ref, bf16[320,480]{1,0:T(8,128)(2,1)S(1)} %copy-done.7), custom_call_target="tpu_custom_call" | custom-call | flops 1000000 | bytes 100000 | tf_op jit(solution)/shard_map/cols_out/pallas_call | solution.py:209
  61.0 3.2 %collective-permute-done.5.refs_1_ = f32[16,32,128]{2,1,0:T(8,128)S(1)} collective-permute-done((f32[16,32,128]{2,1,0:T(8,128)}, f32[16,32,128]{2,1,0:T(8,128)S(1)}, u32[]{:S(2)}, u32[]{:S(2)}) %collective-permute-start.5) | collective-permute-done | bytes 262176 | tf_op jit(solution)/shard_map/ppermute | solution.py:367
  64.2 1.8 collective-permute-done.4.refs_0_
  67.8 12.0 %depth_rows.2.inner_ref = f32[65,128,128]{2,1,0:T(8,128)} custom-call(f32[16,128,128]{2,1,0:T(8,128)} %collective-permute-done.2.refs_0_, f32[16,128,128]{2,1,0:T(8,128)S(1)} %collective-permute-done.3.refs_1_, bf16[144,384]{1,0:T(8,128)(2,1)S(1)} %copy-done.6), custom_call_target="tpu_custom_call" | custom-call | flops 1000000 | bytes 100000 | tf_op jit(solution)/shard_map/depth_rows/pallas_call | solution.py:164
  79.8 28.4 %filtered.2.modes_ref = f32[65,128,128]{2,1,0:T(8,128)} custom-call(f32[65,160,128]{2,1,0:T(8,128)} %cols_out.4.own_ref, f32[65,128,128]{2,1,0:T(8,128)} %depth_rows.2.inner_ref, f32[65,32,128]{2,1,0:T(8,128)S(1)} %depth_corners.2.outer_ref, f32[65,160,256]{2,1,0:T(8,128)} %transfer.1.transfer_ref, bf16[768,256]{1,0:T(8,128)(2,1)S(1)} %copy-done.12, ...), custom_call_target="tpu_custom_call" | custom-call | flops 22000001024 | bytes 25000000 | tf_op jit(solution)/shard_map/filtered/pallas_call | solution.py:316
  108.3 12.1 %depth_home.2.refs_0_ = f32[64,128,128]{2,1,0:T(8,128)S(1)} custom-call(f32[65,128,128]{2,1,0:T(8,128)} %filtered.2.modes_ref, f32[64,128,128]{2,1,0:T(8,128)} %other_ref.1, bf16[240,256]{1,0:T(8,128)(2,1)S(1)} %copy-done.9), custom_call_target="tpu_custom_call" | custom-call | flops 3000000000 | bytes 13000000 | tf_op jit(solution)/shard_map/depth_home/pallas_call | solution.py:347
  120.5 1.9 collective-permute-start.6
  124.1 4.1 %collective-permute-start.8 = (f32[16,128,128]{2,1,0:T(8,128)}, f32[16,128,128]{2,1,0:T(8,128)}, u32[]{:S(2)}, u32[]{:S(2)}) collective-permute-start(f32[16,128,128]{2,1,0:T(8,128)} %get-tuple-element.6), channel_id=1, source_target_pairs={{4,0},{8,4},{12,8},{16,12},{20,16},{24,20},{28,24},{0,28},{5,1},{9... | collective-permute-start | bytes 3145736 | tf_op jit(solution)/shard_map/ppermute | solution.py:366
  130.1 10.0 %depth_own.3.inner_ref = f32[65,128,128]{2,1,0:T(8,128)} custom-call(f32[64,128,128]{2,1,0:T(8,128)S(1)} %depth_home.2.refs_0_, bf16[144,384]{1,0:T(8,128)(2,1)S(1)} %copy-done.6), custom_call_target="tpu_custom_call" | custom-call | flops 1000000 | bytes 100000 | tf_op jit(solution)/shard_map/depth_own/pallas_call | solution.py:164
  140.4 4.2 %collective-permute-start.10 = (f32[16,32,128]{2,1,0:T(8,128)S(1)}, f32[16,32,128]{2,1,0:T(8,128)S(1)}, u32[]{:S(2)}, u32[]{:S(2)}) collective-permute-start(f32[16,32,128]{2,1,0:T(8,128)S(1)} %get-tuple-element.14), channel_id=1, source_target_pairs={{4,0},{8,4},{12,8},{16,12},{20,16},{24,20},{28,24},{0,28},{5,1},{9... | collective-permute-start | bytes 786440 | tf_op jit(solution)/shard_map/ppermute | solution.py:366
  144.5 3.5 %maximum_maximum_fusion.volume_ref = f32[66,136,128]{2,1,0:T(8,128)} fusion(f32[1,7,128]{2,1,0:T(8,128)S(1)} %slice.101, f32[1,1,128]{2,1,0:T(1,128)S(1)} %slice.100, f32[1,128,128]{2,1,0:T(8,128)S(1)} %slice.99, f32[64,7,128]{2,1,0:T(8,128)S(1)} %slice.98, f32[64,1,128]{2,1,0:T(1,128)S(1)} %slice.97, f32[64,128,128]{2,1,0:T(8,128)S(1)} %copy-done.3, ...), kind=kLoop, calls=%fused_computation | loop fusion | flops 9191424 | bytes 9191424 | tf_op jit(solution)/shard_map/concatenate | solution.py:435
  148.1 7.9 %weighted.1.other_ref = f32[64,128,128]{2,1,0:T(8,128)S(1)} custom-call(f32[66,136,128]{2,1,0:T(8,128)} %maximum_maximum_fusion.volume_ref), custom_call_target="tpu_custom_call" | custom-call | flops 1000000 | bytes 100000 | tf_op jit(solution)/shard_map/weighted/pallas_call | solution.py:446
  156.0 2.0 copy-done.4
  158.0 1.9 depth_cols.3.outer_ref
  159.9 5.7 %cols_out.5.own_ref = f32[65,160,128]{2,1,0:T(8,128)} custom-call(f32[65,128,128]{2,1,0:T(8,128)S(1)} %bitcast.9, f32[65,32,128]{2,1,0:T(8,128)S(1)} %depth_cols.3.outer_ref, bf16[320,480]{1,0:T(8,128)(2,1)S(1)} %copy-done.7), custom_call_target="tpu_custom_call" | custom-call | flops 1000000 | bytes 100000 | tf_op jit(solution)/shard_map/cols_out/pallas_call | solution.py:209
  165.6 14.7 %collective-permute-done.11.refs_1_ = f32[16,32,128]{2,1,0:T(8,128)S(1)} collective-permute-done((f32[16,32,128]{2,1,0:T(8,128)S(1)}, f32[16,32,128]{2,1,0:T(8,128)S(1)}, u32[]{:S(2)}, u32[]{:S(2)}) %collective-permute-start.11) | collective-permute-done | bytes 262176 | tf_op jit(solution)/shard_map/ppermute | solution.py:367
  180.3 4.0 %collective-permute-done.10.refs_0_ = f32[16,32,128]{2,1,0:T(8,128)S(1)} collective-permute-done((f32[16,32,128]{2,1,0:T(8,128)S(1)}, f32[16,32,128]{2,1,0:T(8,128)S(1)}, u32[]{:S(2)}, u32[]{:S(2)}) %collective-permute-start.10) | collective-permute-done | bytes 262176 | tf_op jit(solution)/shard_map/ppermute | solution.py:366
  186.1 11.9 %depth_rows.3.inner_ref = f32[65,128,128]{2,1,0:T(8,128)} custom-call(f32[16,128,128]{2,1,0:T(8,128)} %collective-permute-done.8.refs_0_, f32[16,128,128]{2,1,0:T(8,128)S(1)} %collective-permute-done.9.refs_1_, bf16[144,384]{1,0:T(8,128)(2,1)S(1)} %copy-done.6), custom_call_target="tpu_custom_call" | custom-call | flops 1000000 | bytes 100000 | tf_op jit(solution)/shard_map/depth_rows/pallas_call | solution.py:164
  198.0 28.6 %filtered.3.modes_ref = f32[65,128,128]{2,1,0:T(8,128)} custom-call(f32[65,160,128]{2,1,0:T(8,128)} %cols_out.5.own_ref, f32[65,128,128]{2,1,0:T(8,128)} %depth_rows.3.inner_ref, f32[65,32,128]{2,1,0:T(8,128)S(1)} %depth_corners.3.outer_ref, f32[65,160,256]{2,1,0:T(8,128)} %transfer.1.transfer_ref, bf16[768,256]{1,0:T(8,128)(2,1)S(1)} %copy-done.13, ...), custom_call_target="tpu_custom_call" | custom-call | flops 22000001024 | bytes 25000000 | tf_op jit(solution)/shard_map/filtered/pallas_call | solution.py:316
  226.6 12.7 %depth_home.3 = f32[64,128,128]{2,1,0:T(8,128)} custom-call(f32[65,128,128]{2,1,0:T(8,128)} %filtered.3.modes_ref, f32[64,128,128]{2,1,0:T(8,128)S(1)} %copy-done.5, bf16[240,256]{1,0:T(8,128)(2,1)S(1)} %copy-done.9), custom_call_target="tpu_custom_call" | custom-call | flops 3000000000 | bytes 13000000 | tf_op jit(solution)/shard_map/depth_home/pallas_call | solution.py:347
  (93 shorter events, 14.8 us)
Async XLA Ops:
  0.0 11.4 %copy-start = (f32[32,32,32]{2,1,0:T(8,128)S(1)}, f32[32,32,32]{2,1,0:T(8,128)}, u32[]{:S(2)}) copy-start(f32[32,32,32]{2,1,0:T(8,128)} %param.15) | copy-start | bytes 393220
  1.3 14.8 %collective-permute-start.1 = (f32[64,16,128]{2,1,0:T(8,128)S(1)}, f32[64,16,128]{2,1,0:T(8,128)S(1)}, u32[]{:S(2)}, u32[]{:S(2)}) collective-permute-start(f32[64,16,128]{2,1,0:T(8,128)S(1)} %get-tuple-element.11), channel_id=1, source_target_pairs={{0,1},{1,2},{2,3},{3,0},{4,5},{5,6},{6,7},{7,4},{8,9},{9,10},{10,1... | collective-permute-start | bytes 1572872 | tf_op jit(solution)/shard_map/ppermute | solution.py:367
  4.0 18.3 %copy-start.23 = (f32[32,65,1]{1,0,2:T(8,128)S(1)}, f32[32,65,1]{1,0,2:T(8,128)}, u32[]{:S(2)}) copy-start(f32[32,65,1]{1,0,2:T(8,128)} %constant.38) | copy-start | bytes 24964
  4.0 12.0 %collective-permute-start = (f32[64,16,128]{2,1,0:T(8,128)S(1)}, f32[64,16,128]{2,1,0:T(8,128)S(1)}, u32[]{:S(2)}, u32[]{:S(2)}) collective-permute-start(f32[64,16,128]{2,1,0:T(8,128)S(1)} %get-tuple-element.12), channel_id=1, source_target_pairs={{1,0},{2,1},{3,2},{0,3},{5,4},{6,5},{7,6},{4,7},{9,8},{10,9},{11,1... | collective-permute-start | bytes 1572872 | tf_op jit(solution)/shard_map/ppermute | solution.py:366
  7.1 60.6 %collective-permute-start.3 = (f32[16,128,128]{2,1,0:T(8,128)}, f32[16,128,128]{2,1,0:T(8,128)S(1)}, u32[]{:S(2)}, u32[]{:S(2)}) collective-permute-start(f32[16,128,128]{2,1,0:T(8,128)} %get-tuple-element.9), channel_id=1, source_target_pairs={{0,4},{4,8},{8,12},{12,16},{16,20},{20,24},{24,28},{28,0},{1,5},{5... | collective-permute-start | bytes 3145736 | tf_op jit(solution)/shard_map/ppermute | solution.py:367
  8.4 21.1 %copy-start.6 = (bf16[144,384]{1,0:T(8,128)(2,1)S(1)}, bf16[144,384]{1,0:T(8,128)(2,1)}, u32[]{:S(2)}) copy-start(bf16[144,384]{1,0:T(8,128)(2,1)} %constant.27.clone.refs_1_.refs_2_) | copy-start | bytes 331780
  8.4 59.4 %collective-permute-start.2 = (f32[16,128,128]{2,1,0:T(8,128)}, f32[16,128,128]{2,1,0:T(8,128)}, u32[]{:S(2)}, u32[]{:S(2)}) collective-permute-start(f32[16,128,128]{2,1,0:T(8,128)} %get-tuple-element.10), channel_id=1, source_target_pairs={{4,0},{8,4},{12,8},{16,12},{20,16},{24,20},{28,24},{0,28},{5,1},{9... | collective-permute-start | bytes 3145736 | tf_op jit(solution)/shard_map/ppermute | solution.py:366
  17.2 47.1 %collective-permute-start.5 = (f32[16,32,128]{2,1,0:T(8,128)}, f32[16,32,128]{2,1,0:T(8,128)S(1)}, u32[]{:S(2)}, u32[]{:S(2)}) collective-permute-start(f32[16,32,128]{2,1,0:T(8,128)} %get-tuple-element.15), channel_id=1, source_target_pairs={{0,4},{4,8},{8,12},{12,16},{16,20},{20,24},{24,28},{28,0},{1,5},{5... | collective-permute-start | bytes 786440 | tf_op jit(solution)/shard_map/ppermute | solution.py:367
  19.2 46.8 %collective-permute-start.4 = (f32[16,32,128]{2,1,0:T(8,128)}, f32[16,32,128]{2,1,0:T(8,128)S(1)}, u32[]{:S(2)}, u32[]{:S(2)}) collective-permute-start(f32[16,32,128]{2,1,0:T(8,128)} %get-tuple-element.16), channel_id=1, source_target_pairs={{4,0},{8,4},{12,8},{16,12},{20,16},{24,20},{28,24},{0,28},{5,1},{9... | collective-permute-start | bytes 786440 | tf_op jit(solution)/shard_map/ppermute | solution.py:366
  41.4 13.9 %slice-start.2 = ((s8[4259840]{0:T(1024)(128)(4,1)}), s8[4194304]{0:T(1024)(128)(4,1)S(1)}, s32[]{:S(2)}) async-start(s8[4259840]{0:T(1024)(128)(4,1)} %bitcast.10), calls=%async_computation.2 | async-start | bytes 8388608
  42.4 12.9 %slice-start.3 = ((s8[4259840]{0:T(1024)(128)(4,1)}), s8[65536]{0:T(1024)(128)(4,1)S(1)}, s32[]{:S(2)}) async-start(s8[4259840]{0:T(1024)(128)(4,1)} %bitcast.10), calls=%async_computation.3 | async-start | bytes 131072
  42.4 12.9 %copy-start.7 = (bf16[320,480]{1,0:T(8,128)(2,1)S(1)}, bf16[320,480]{1,0:T(8,128)(2,1)}, u32[]{:S(2)}) copy-start(bf16[320,480]{1,0:T(8,128)(2,1)} %constant.28.clone.table_ref.cols_out) | copy-start | bytes 921604
  61.0 18.8 %copy-start.12 = (bf16[768,256]{1,0:T(8,128)(2,1)S(1)}, bf16[768,256]{1,0:T(8,128)(2,1)}, u32[]{:S(2)}) copy-start(bf16[768,256]{1,0:T(8,128)(2,1)} %constant.29.clone.rows_out) | copy-start | bytes 1179652
  61.0 18.8 %copy-start.14 = (bf16[256,480]{1,0:T(8,128)(2,1)S(1)}, bf16[256,480]{1,0:T(8,128)(2,1)}, u32[]{:S(2)}) copy-start(bf16[256,480]{1,0:T(8,128)(2,1)} %constant.30.clone.cols_home) | copy-start | bytes 737284
  61.0 18.8 %copy-start.16 = (bf16[768,128]{1,0:T(8,128)(2,1)S(1)}, bf16[768,128]{1,0:T(8,128)(2,1)}, u32[]{:S(2)}) copy-start(bf16[768,128]{1,0:T(8,128)(2,1)} %constant.31.clone.rows_home) | copy-start | bytes 589828
  67.7 61.5 %copy-start.8 = (f32[16,128,128]{2,1,0:T(8,128)}, f32[16,128,128]{2,1,0:T(8,128)S(1)}, u32[]{:S(2)}) copy-start(f32[16,128,128]{2,1,0:T(8,128)S(1)} %collective-permute-done.3.refs_1_) | copy-start | bytes 3145732
  79.8 28.5 %copy-start.9 = (bf16[240,256]{1,0:T(8,128)(2,1)S(1)}, bf16[240,256]{1,0:T(8,128)(2,1)}, u32[]{:S(2)}) copy-start(bf16[240,256]{1,0:T(8,128)(2,1)} %constant.32.clone.table_ref) | copy-start | bytes 368644
  120.5 19.6 %collective-permute-start.6 = (f32[64,16,128]{2,1,0:T(8,128)S(1)}, f32[64,16,128]{2,1,0:T(8,128)S(1)}, u32[]{:S(2)}, u32[]{:S(2)}) collective-permute-start(f32[64,16,128]{2,1,0:T(8,128)S(1)} %get-tuple-element.8), channel_id=1, source_target_pairs={{1,0},{2,1},{3,2},{0,3},{5,4},{6,5},{7,6},{4,7},{9,8},{10,9},{11,1... | collective-permute-start | bytes 1572872 | tf_op jit(solution)/shard_map/ppermute | solution.py:366
  122.4 17.8 %collective-permute-start.7 = (f32[64,16,128]{2,1,0:T(8,128)S(1)}, f32[64,16,128]{2,1,0:T(8,128)S(1)}, u32[]{:S(2)}, u32[]{:S(2)}) collective-permute-start(f32[64,16,128]{2,1,0:T(8,128)S(1)} %get-tuple-element.7), channel_id=1, source_target_pairs={{0,1},{1,2},{2,3},{3,0},{4,5},{5,6},{6,7},{7,4},{8,9},{9,10},{10,1... | collective-permute-start | bytes 1572872 | tf_op jit(solution)/shard_map/ppermute | solution.py:367
  124.1 62.0 %collective-permute-start.9 = (f32[16,128,128]{2,1,0:T(8,128)}, f32[16,128,128]{2,1,0:T(8,128)S(1)}, u32[]{:S(2)}, u32[]{:S(2)}) collective-permute-start(f32[16,128,128]{2,1,0:T(8,128)} %get-tuple-element.5), channel_id=1, source_target_pairs={{0,4},{4,8},{8,12},{12,16},{16,20},{20,24},{24,28},{28,0},{1,5},{5... | collective-permute-start | bytes 3145736 | tf_op jit(solution)/shard_map/ppermute | solution.py:367
  124.1 62.0 %collective-permute-start.8 = (f32[16,128,128]{2,1,0:T(8,128)}, f32[16,128,128]{2,1,0:T(8,128)}, u32[]{:S(2)}, u32[]{:S(2)}) collective-permute-start(f32[16,128,128]{2,1,0:T(8,128)} %get-tuple-element.6), channel_id=1, source_target_pairs={{4,0},{8,4},{12,8},{16,12},{20,16},{24,20},{28,24},{0,28},{5,1},{9... | collective-permute-start | bytes 3145736 | tf_op jit(solution)/shard_map/ppermute | solution.py:366
  130.1 14.4 %copy-start.3 = (f32[64,128,128]{2,1,0:T(8,128)S(1)}, f32[64,128,128]{2,1,0:T(8,128)}, u32[]{:S(2)}) copy-start(f32[64,128,128]{2,1,0:T(8,128)} %refs_0_.1) | copy-start | bytes 12582916
  130.1 14.4 %slice-start.4 = ((f32[16,128,128]{2,1,0:T(8,128)}), f32[1,128,128]{2,1,0:T(8,128)S(1)}, s32[]{:S(2)}) async-start(f32[16,128,128]{2,1,0:T(8,128)} %copy-done.8), calls=%async_computation.4 | async-start | bytes 131072 | tf_op jit(solution)/shard_map/slice | solution.py:430
  140.3 40.0 %collective-permute-start.11 = (f32[16,32,128]{2,1,0:T(8,128)S(1)}, f32[16,32,128]{2,1,0:T(8,128)S(1)}, u32[]{:S(2)}, u32[]{:S(2)}) collective-permute-start(f32[16,32,128]{2,1,0:T(8,128)S(1)} %get-tuple-element.13), channel_id=1, source_target_pairs={{0,4},{4,8},{8,12},{12,16},{16,20},{20,24},{24,28},{28,0},{1,5},{5... | collective-permute-start | bytes 786440 | tf_op jit(solution)/shard_map/ppermute | solution.py:367
  140.4 44.0 %collective-permute-start.10 = (f32[16,32,128]{2,1,0:T(8,128)S(1)}, f32[16,32,128]{2,1,0:T(8,128)S(1)}, u32[]{:S(2)}, u32[]{:S(2)}) collective-permute-start(f32[16,32,128]{2,1,0:T(8,128)S(1)} %get-tuple-element.14), channel_id=1, source_target_pairs={{4,0},{8,4},{12,8},{16,12},{20,16},{24,20},{28,24},{0,28},{5,1},{9... | collective-permute-start | bytes 786440 | tf_op jit(solution)/shard_map/ppermute | solution.py:366
  144.5 15.3 %slice-start = ((s8[4259840]{0:T(1024)(128)(4,1)}), s8[65536]{0:T(1024)(128)(4,1)S(1)}, s32[]{:S(2)}) async-start(s8[4259840]{0:T(1024)(128)(4,1)} %bitcast.8), calls=%async_computation | async-start | bytes 131072
  148.1 11.8 %slice-start.1 = ((s8[4259840]{0:T(1024)(128)(4,1)}), s8[4194304]{0:T(1024)(128)(4,1)S(1)}, s32[]{:S(2)}) async-start(s8[4259840]{0:T(1024)(128)(4,1)} %bitcast.8), calls=%async_computation.1 | async-start | bytes 8388608
  165.6 32.4 %copy-start.13 = (bf16[768,256]{1,0:T(8,128)(2,1)S(1)}, bf16[768,256]{1,0:T(8,128)(2,1)}, u32[]{:S(2)}) copy-start(bf16[768,256]{1,0:T(8,128)(2,1)} %constant.29.clone.rows_out) | copy-start | bytes 1179652
  165.6 32.4 %copy-start.15 = (bf16[256,480]{1,0:T(8,128)(2,1)S(1)}, bf16[256,480]{1,0:T(8,128)(2,1)}, u32[]{:S(2)}) copy-start(bf16[256,480]{1,0:T(8,128)(2,1)} %constant.30.clone.cols_home) | copy-start | bytes 737284
  165.6 32.4 %copy-start.17 = (bf16[768,128]{1,0:T(8,128)(2,1)S(1)}, bf16[768,128]{1,0:T(8,128)(2,1)}, u32[]{:S(2)}) copy-start(bf16[768,128]{1,0:T(8,128)(2,1)} %constant.31.clone.rows_home) | copy-start | bytes 589828
  198.0 28.6 %copy-start.5 = (f32[64,128,128]{2,1,0:T(8,128)S(1)}, f32[64,128,128]{2,1,0:T(8,128)}, u32[]{:S(2)}) copy-start(f32[64,128,128]{2,1,0:T(8,128)} %copy-done.4) | copy-start | bytes 12582916
  198.0 41.3 %copy-start.1 = (f32[32,32,32]{2,1,0:T(8,128)S(1)}, f32[32,32,32]{2,1,0:T(8,128)}, u32[]{:S(2)}) copy-start(f32[32,32,32]{2,1,0:T(8,128)} %param.15) | copy-start | bytes 393220
  (10 other events, 51.3 us)

commit v5 on v4

--- a/solution.py
+++ b/solution.py
@@ -371,7 +371,9 @@
 def halos(block, width):
     rows = neighbours("px", block[:width], block[-width:])
     cols = jnp.concatenate(neighbours("py", block[:, :width], block[:, -width:]), 1)
-    corners = neighbours("px", cols[:width], cols[-width:])
+    first = jnp.concatenate([part[:, :width] for part in rows], 0)
+    last = jnp.concatenate([part[:, -width:] for part in rows], 0)
+    corners = jnp.concatenate(neighbours("py", first, last), 1)
     return rows, cols, corners
 
 
@@ -381,7 +383,7 @@
         plan, depth_out(plan, "depth_own", block), depth_out(plan, "depth_cols", cols)
     )
     inner = depth_out(plan, "depth_rows", *rows)
-    outer = depth_out(plan, "depth_corners", *corners)
+    outer = depth_out(plan, "depth_corners", corners)
     return filtered(plan, own, inner, outer, gains, adjoint)
 
 
@@ -427,9 +429,9 @@
 def weighted(block, around):
     rows, cols, corners = around
     stack = [
-        jnp.concatenate([corners[1][-1:], rows[1][-1:]], 1),
+        jnp.concatenate([corners[-1:], rows[1][-1:]], 1),
         jnp.concatenate([cols, block], 1),
-        jnp.concatenate([corners[0][:1], rows[0][:1]], 1),
+        jnp.concatenate([corners[:1], rows[0][:1]], 1),
     ]
     edge, size = cols.shape[1], block.shape[1]
     volume = jnp.concatenate(

time: 242 us -> 264 us (1.091)
  waiting for transfers between devices: 27 us -> 62.5 us
  starting transfers between devices: 22.5 us -> 16.9 us
  Pallas kernels: 163 us -> 158 us
  other arithmetic: 3.75 us -> 7.9 us
  local copies, waits for them, and re-layouts: 20 us -> 16 us
    ppermute x6, waiting for transfers between devices: 9.09 us -> 61.3 us  [neighbours(): lax.ppermute(after, axis, [((i + 1) % count, i) for i in range(count)])]
    ppermute x6, waiting for transfers between devices: 17.9 us -> 1.2 us  [neighbours(): lax.ppermute(before, axis, [(i, (i + 1) % count) for i in range(count)])]
    pallas_call x8, Pallas kernels: 50.8 us -> 45.9 us  [depth_out(): pl.pallas_call(functools.partial(depth_out_kernel, plan, len(pieces)), gr...]
    ppermute x6, starting transfers between devices: 16.3 us -> 11.4 us  [neighbours(): lax.ppermute(after, axis, [((i + 1) % count, i) for i in range(count)])]
    concatenate x0 -> x8, other arithmetic: none -> 4.11 us  [the longest x2 1.47 us: halos(): jnp.concatenate(neighbours('py', block[:, :width], block[:, -width:]), 1)]
  transfers between devices with their start and end apart: 12 -> 12, of which waited for: 5 -> 4; matrix products, arithmetic and copies ran while one was open for 8% -> 6% of each run, Pallas kernels for 24% -> 28%
where the time goes in v5:
time: 264 us; the launch traced here: 263 us
  Pallas kernels  158 us (60%)
  waiting for transfers between devices  62.5 us (24%)
  starting transfers between devices  16.9 us (6%)
  local copies, waits for them, and re-layouts  16 us (6%)
  other arithmetic  7.9 us (3%)
    ppermute x6, waiting for transfers between devices, neighbours(): lax.ppermute(after, axis, [((i + 1) % count, i) for i in range(count)])  61.3 us
    pallas_call x2, Pallas kernels, filtered(): pl.pallas_call(functools.partial(filter_kernel, adjoint), grid=(plan.mode...  57.1 us
    pallas_call x8, Pallas kernels, depth_out(): pl.pallas_call(functools.partial(depth_out_kernel, plan, len(pieces)), gr...  45.9 us
    pallas_call x2, Pallas kernels, depth_home(): pl.pallas_call(functools.partial(depth_home_kernel, plan, divide), grid=(...  24.8 us
    ppermute x6, starting transfers between devices, neighbours(): lax.ppermute(after, axis, [((i + 1) % count, i) for i in range(count)])  11.4 us
    pallas_call x2, Pallas kernels, cols_out(): pl.pallas_call(cols_kernel, grid=(plan.modes // step,), in_specs=[spec(pl...  11.3 us
    pallas_call x1, Pallas kernels, transfer(): pl.pallas_call(transfer_kernel, grid=(plan.modes // step,), in_specs=[pl....  11 us
    pallas_call x1, Pallas kernels, weighted(): pl.pallas_call(functools.partial(variation_kernel, whole), grid=(block.sh...  7.75 us
  transfers between devices with their start and end apart: 12, of which 4 were waited for; matrix products, arithmetic and copies ran while one was open for 6% of the time, Pallas kernels for 28%

profile of v5, /device:TPU:1, one launch (start us, length us, event | category | flops | bytes accessed | tf_op | source)
XLA Modules:
  0.0 262.7 jit_solution(11836264529450900832)
XLA Ops:
  0.0 3.1 %fusion.2 = (f32[16,128,128]{2,1,0:T(8,128)}, f32[16,128,128]{2,1,0:T(8,128)}) fusion(f32[64,128,128]{2,1,0:T(8,128)} %refs_0_.1), kind=kLoop, calls=%fused_computation.14 | loop fusion | bytes 4194304 | tf_op jit(solution)/shard_map/slice | solution.py:372
  3.1 5.1 %collective-permute-start.2 = (f32[16,128,128]{2,1,0:T(8,128)}, f32[16,128,128]{2,1,0:T(8,128)S(1)}, u32[]{:S(2)}, u32[]{:S(2)}) collective-permute-start(f32[16,128,128]{2,1,0:T(8,128)} %get-tuple-element.10), channel_id=1, source_target_pairs={{4,0},{8,4},{12,8},{16,12},{20,16},{24,20},{28,24},{0,28},{5,1},{9... | collective-permute-start | bytes 3145736 | tf_op jit(solution)/shard_map/ppermute | solution.py:366
  8.3 2.3 fusion.3
  11.5 1.1 collective-permute-start.1
  13.1 1.9 copy.14
  15.6 1.9 copy.15
  17.5 2.2 copy-done.2
  19.7 9.8 %depth_own.2.inner_ref = f32[65,128,128]{2,1,0:T(8,128)} custom-call(f32[64,128,128]{2,1,0:T(8,128)S(1)} %copy-done.2, bf16[144,384]{1,0:T(8,128)(2,1)S(1)} %copy-done.7), custom_call_target="tpu_custom_call" | custom-call | flops 1000000 | bytes 100000 | tf_op jit(solution)/shard_map/depth_own/pallas_call | solution.py:164
  29.4 21.3 %collective-permute-done.2.refs_0_ = f32[16,128,128]{2,1,0:T(8,128)S(1)} collective-permute-done((f32[16,128,128]{2,1,0:T(8,128)}, f32[16,128,128]{2,1,0:T(8,128)S(1)}, u32[]{:S(2)}, u32[]{:S(2)}) %collective-permute-start.2) | collective-permute-done | bytes 1048608 | tf_op jit(solution)/shard_map/ppermute | solution.py:366
  52.4 1.3 collective-permute-start.5
  54.0 11.0 %transfer.1.transfer_ref = f32[65,160,256]{2,1,0:T(8,128)} custom-call(f32[65,32,256]{2,1,0:T(8,128)S(1)} %select_maximum_fusion.psf_ref, bf16[768,256]{1,0:T(8,128)(2,1)S(1)} %copy-done.14, bf16[320,96]{1,0:T(8,128)(2,1)S(1)} %copy-done.15), custom_call_target="tpu_custom_call" | custom-call | flops 1000000 | bytes 100000 | tf_op jit(solution)/shard_map/transfer/pallas_call | solution.py:259
  65.0 1.4 pad_maximum_fusion.refs_0_
  66.3 1.9 depth_cols.2.outer_ref
  68.3 5.7 %cols_out.4.own_ref = f32[65,160,128]{2,1,0:T(8,128)} custom-call(f32[65,128,128]{2,1,0:T(8,128)S(1)} %bitcast.9, f32[65,32,128]{2,1,0:T(8,128)S(1)} %depth_cols.2.outer_ref, bf16[320,480]{1,0:T(8,128)(2,1)S(1)} %copy-done.12), custom_call_target="tpu_custom_call" | custom-call | flops 1000000 | bytes 100000 | tf_op jit(solution)/shard_map/cols_out/pallas_call | solution.py:209
  73.9 9.5 %depth_rows.2.inner_ref = f32[65,128,128]{2,1,0:T(8,128)} custom-call(f32[16,128,128]{2,1,0:T(8,128)S(1)} %collective-permute-done.2.refs_0_, f32[16,128,128]{2,1,0:T(8,128)S(1)} %collective-permute-done.3.refs_1_, bf16[144,384]{1,0:T(8,128)(2,1)S(1)} %copy-done.7), custom_call_target="tpu_custom_call" | custom-call | flops 1000000 | bytes 100000 | tf_op jit(solution)/shard_map/depth_rows/pallas_call | solution.py:164
  83.5 1.7 depth_corners.2.outer_ref
  85.3 28.4 %filtered.2.modes_ref = f32[65,128,128]{2,1,0:T(8,128)} custom-call(f32[65,160,128]{2,1,0:T(8,128)} %cols_out.4.own_ref, f32[65,128,128]{2,1,0:T(8,128)} %depth_rows.2.inner_ref, f32[65,32,128]{2,1,0:T(8,128)S(1)} %depth_corners.2.outer_ref, f32[65,160,256]{2,1,0:T(8,128)} %transfer.1.transfer_ref, bf16[768,256]{1,0:T(8,128)(2,1)S(1)} %copy-done.16, ...), custom_call_target="tpu_custom_call" | custom-call | flops 22000001024 | bytes 25000000 | tf_op jit(solution)/shard_map/filtered/pallas_call | solution.py:316
  113.7 12.1 %depth_home.2.refs_0_ = f32[64,128,128]{2,1,0:T(8,128)S(1)} custom-call(f32[65,128,128]{2,1,0:T(8,128)} %filtered.2.modes_ref, f32[64,128,128]{2,1,0:T(8,128)} %other_ref.1, bf16[240,256]{1,0:T(8,128)(2,1)S(1)} %copy-done.13), custom_call_target="tpu_custom_call" | custom-call | flops 3000000000 | bytes 13000000 | tf_op jit(solution)/shard_map/depth_home/pallas_call | solution.py:347
  126.1 4.4 %collective-permute-start.8 = (f32[16,128,128]{2,1,0:T(8,128)S(1)}, f32[16,128,128]{2,1,0:T(8,128)S(1)}, u32[]{:S(2)}, u32[]{:S(2)}) collective-permute-start(f32[16,128,128]{2,1,0:T(8,128)S(1)} %get-tuple-element.6), channel_id=1, source_target_pairs={{4,0},{8,4},{12,8},{16,12},{20,16},{24,20},{28,24},{0,28},{5,1},{9... | collective-permute-start | bytes 3145736 | tf_op jit(solution)/shard_map/ppermute | solution.py:366
  132.6 1.7 collective-permute-start.7
  134.4 40.0 %collective-permute-done.8.refs_0_ = f32[16,128,128]{2,1,0:T(8,128)S(1)} collective-permute-done((f32[16,128,128]{2,1,0:T(8,128)S(1)}, f32[16,128,128]{2,1,0:T(8,128)S(1)}, u32[]{:S(2)}, u32[]{:S(2)}) %collective-permute-start.8) | collective-permute-done | bytes 1048608 | tf_op jit(solution)/shard_map/ppermute | solution.py:366
  176.5 1.4 collective-permute-start.11
  177.9 3.6 %maximum_maximum_fusion.volume_ref = f32[66,136,128]{2,1,0:T(8,128)} fusion(f32[1,7,128]{2,1,0:T(8,128)S(1)} %get-tuple-element.24, f32[1,1,128]{2,1,0:T(1,128)S(1)} %get-tuple-element.22, f32[1,128,128]{2,1,0:T(8,128)S(1)} %slice-done.2, f32[64,7,128]{2,1,0:T(8,128)S(1)} %slice.122, f32[64,1,128]{2,1,0:T(1,128)S(1)} %slice.121, ...), kind=kLoop, calls=%fused_computation | loop fusion | flops 9191424 | bytes 9191424 | tf_op jit(solution)/shard_map/concatenate | solution.py:437
  181.5 9.9 %depth_own.3.inner_ref = f32[65,128,128]{2,1,0:T(8,128)} custom-call(f32[64,128,128]{2,1,0:T(8,128)S(1)} %depth_home.2.refs_0_, bf16[144,384]{1,0:T(8,128)(2,1)S(1)} %copy-done.7), custom_call_target="tpu_custom_call" | custom-call | flops 1000000 | bytes 100000 | tf_op jit(solution)/shard_map/depth_own/pallas_call | solution.py:164
  191.4 7.7 %weighted.1.other_ref = f32[64,128,128]{2,1,0:T(8,128)S(1)} custom-call(f32[66,136,128]{2,1,0:T(8,128)} %maximum_maximum_fusion.volume_ref), custom_call_target="tpu_custom_call" | custom-call | flops 1000000 | bytes 100000 | tf_op jit(solution)/shard_map/weighted/pallas_call | solution.py:448
  199.2 2.0 copy-done.5
  201.3 1.9 depth_cols.3.outer_ref
  203.4 5.6 %cols_out.5.own_ref = f32[65,160,128]{2,1,0:T(8,128)} custom-call(f32[65,128,128]{2,1,0:T(8,128)S(1)} %copy-done.4, f32[65,32,128]{2,1,0:T(8,128)S(1)} %depth_cols.3.outer_ref, bf16[320,480]{1,0:T(8,128)(2,1)S(1)} %copy-done.12), custom_call_target="tpu_custom_call" | custom-call | flops 1000000 | bytes 100000 | tf_op jit(solution)/shard_map/cols_out/pallas_call | solution.py:209
  209.0 9.5 %depth_rows.3.inner_ref = f32[65,128,128]{2,1,0:T(8,128)} custom-call(f32[16,128,128]{2,1,0:T(8,128)S(1)} %collective-permute-done.8.refs_0_, f32[16,128,128]{2,1,0:T(8,128)S(1)} %copy-done.11, bf16[144,384]{1,0:T(8,128)(2,1)S(1)} %copy-done.7), custom_call_target="tpu_custom_call" | custom-call | flops 1000000 | bytes 100000 | tf_op jit(solution)/shard_map/depth_rows/pallas_call | solution.py:164
  219.5 1.7 depth_corners.3.outer_ref
  221.3 28.7 %filtered.3.modes_ref = f32[65,128,128]{2,1,0:T(8,128)} custom-call(f32[65,160,128]{2,1,0:T(8,128)} %cols_out.5.own_ref, f32[65,128,128]{2,1,0:T(8,128)} %depth_rows.3.inner_ref, f32[65,32,128]{2,1,0:T(8,128)S(1)} %depth_corners.3.outer_ref, f32[65,160,256]{2,1,0:T(8,128)} %transfer.1.transfer_ref, bf16[768,256]{1,0:T(8,128)(2,1)S(1)} %copy-done.17, ...), custom_call_target="tpu_custom_call" | custom-call | flops 22000001024 | bytes 25000000 | tf_op jit(solution)/shard_map/filtered/pallas_call | solution.py:316
  250.0 12.7 %depth_home.3 = f32[64,128,128]{2,1,0:T(8,128)} custom-call(f32[65,128,128]{2,1,0:T(8,128)} %filtered.3.modes_ref, f32[64,128,128]{2,1,0:T(8,128)S(1)} %copy-done.6, bf16[240,256]{1,0:T(8,128)(2,1)S(1)} %copy-done.13), custom_call_target="tpu_custom_call" | custom-call | flops 3000000000 | bytes 13000000 | tf_op jit(solution)/shard_map/depth_home/pallas_call | solution.py:347
  (93 shorter events, 9.8 us)
Async XLA Ops:
  0.0 12.6 %copy-start = (f32[32,32,32]{2,1,0:T(8,128)S(1)}, f32[32,32,32]{2,1,0:T(8,128)}, u32[]{:S(2)}) copy-start(f32[32,32,32]{2,1,0:T(8,128)} %param.15) | copy-start | bytes 393220
  0.0 12.6 %copy-start.23 = (f32[32,65,1]{1,0,2:T(8,128)S(1)}, f32[32,65,1]{1,0,2:T(8,128)}, u32[]{:S(2)}) copy-start(f32[32,65,1]{1,0,2:T(8,128)} %constant.37) | copy-start | bytes 24964
  0.0 15.0 %copy-start.24 = (f32[32,65,1]{1,0,2:T(8,128)S(1)}, f32[32,65,1]{1,0,2:T(8,128)}, u32[]{:S(2)}) copy-start(f32[32,65,1]{1,0,2:T(8,128)} %constant.38) | copy-start | bytes 24964
  3.1 14.3 %copy-start.7 = (bf16[144,384]{1,0:T(8,128)(2,1)S(1)}, bf16[144,384]{1,0:T(8,128)(2,1)}, u32[]{:S(2)}) copy-start(bf16[144,384]{1,0:T(8,128)(2,1)} %constant.27.clone.refs_1_.refs_2_) | copy-start | bytes 331780
  3.1 47.6 %collective-permute-start.2 = (f32[16,128,128]{2,1,0:T(8,128)}, f32[16,128,128]{2,1,0:T(8,128)S(1)}, u32[]{:S(2)}, u32[]{:S(2)}) collective-permute-start(f32[16,128,128]{2,1,0:T(8,128)} %get-tuple-element.10), channel_id=1, source_target_pairs={{4,0},{8,4},{12,8},{16,12},{20,16},{24,20},{28,24},{0,28},{5,1},{9... | collective-permute-start | bytes 3145736 | tf_op jit(solution)/shard_map/ppermute | solution.py:366
  8.2 43.5 %collective-permute-start.3 = (f32[16,128,128]{2,1,0:T(8,128)}, f32[16,128,128]{2,1,0:T(8,128)S(1)}, u32[]{:S(2)}, u32[]{:S(2)}) collective-permute-start(f32[16,128,128]{2,1,0:T(8,128)} %get-tuple-element.9), channel_id=1, source_target_pairs={{0,4},{4,8},{8,12},{12,16},{16,20},{20,24},{24,28},{28,0},{1,5},{5... | collective-permute-start | bytes 3145736 | tf_op jit(solution)/shard_map/ppermute | solution.py:367
  10.5 54.4 %collective-permute-start = (f32[64,16,128]{2,1,0:T(8,128)}, f32[64,16,128]{2,1,0:T(8,128)}, u32[]{:S(2)}, u32[]{:S(2)}) collective-permute-start(f32[64,16,128]{2,1,0:T(8,128)} %get-tuple-element.11), channel_id=1, source_target_pairs={{1,0},{2,1},{3,2},{0,3},{5,4},{6,5},{7,6},{4,7},{9,8},{10,9},{11,1... | collective-permute-start | bytes 1572872 | tf_op jit(solution)/shard_map/ppermute | solution.py:366
  11.5 53.5 %collective-permute-start.1 = (f32[64,16,128]{2,1,0:T(8,128)}, f32[64,16,128]{2,1,0:T(8,128)}, u32[]{:S(2)}, u32[]{:S(2)}) collective-permute-start(f32[64,16,128]{2,1,0:T(8,128)} %get-tuple-element.12), channel_id=1, source_target_pairs={{0,1},{1,2},{2,3},{3,0},{4,5},{5,6},{6,7},{7,4},{8,9},{9,10},{10,1... | collective-permute-start | bytes 1572872 | tf_op jit(solution)/shard_map/ppermute | solution.py:367
  19.7 34.0 %copy-start.21 = (f32[65,32,32]{1,2,0:T(8,128)S(1)}, f32[65,32,32]{1,2,0:T(8,128)}, u32[]{:S(2)}) copy-start(f32[65,32,32]{1,2,0:T(8,128)} %copy.14) | copy-start | bytes 798724
  19.7 34.0 %copy-start.22 = (f32[65,32,32]{1,2,0:T(8,128)S(1)}, f32[65,32,32]{1,2,0:T(8,128)}, u32[]{:S(2)}) copy-start(f32[65,32,32]{1,2,0:T(8,128)} %copy.15) | copy-start | bytes 798724
  29.4 24.5 %copy-start.14 = (bf16[768,256]{1,0:T(8,128)(2,1)S(1)}, bf16[768,256]{1,0:T(8,128)(2,1)}, u32[]{:S(2)}) copy-start(bf16[768,256]{1,0:T(8,128)(2,1)} %constant.25.clone.rows_ref) | copy-start | bytes 1179652
  29.4 24.5 %copy-start.15 = (bf16[320,96]{1,0:T(8,128)(2,1)S(1)}, bf16[320,96]{1,0:T(8,128)(2,1)}, u32[]{:S(2)}) copy-start(bf16[320,96]{1,0:T(8,128)(2,1)} %constant.26.clone.cols_ref) | copy-start | bytes 184324
  50.8 81.6 %copy-start.8 = (f32[16,128,128]{2,1,0:T(8,128)}, f32[16,128,128]{2,1,0:T(8,128)S(1)}, u32[]{:S(2)}) copy-start(f32[16,128,128]{2,1,0:T(8,128)S(1)} %collective-permute-done.2.refs_0_) | copy-start | bytes 3145732
  51.8 80.6 %copy-start.9 = (f32[16,128,128]{2,1,0:T(8,128)}, f32[16,128,128]{2,1,0:T(8,128)S(1)}, u32[]{:S(2)}) copy-start(f32[16,128,128]{2,1,0:T(8,128)S(1)} %collective-permute-done.3.refs_1_) | copy-start | bytes 3145732
  51.8 31.6 %collective-permute-start.4 = (f32[32,16,128]{2,1,0:T(8,128)S(1)}, f32[32,16,128]{2,1,0:T(8,128)S(1)}, u32[]{:S(2)}, u32[]{:S(2)}) collective-permute-start(f32[32,16,128]{2,1,0:T(8,128)S(1)} %pad_maximum_fusion.4), channel_id=1, source_target_pairs={{1,0},{2,1},{3,2},{0,3},{5,4},{6,5},{7,6},{4,7},{9,8},{10,9},{11,1... | collective-permute-start | bytes 786440 | tf_op jit(solution)/shard_map/ppermute | solution.py:366
  52.4 31.1 %collective-permute-start.5 = (f32[32,16,128]{2,1,0:T(8,128)S(1)}, f32[32,16,128]{2,1,0:T(8,128)S(1)}, u32[]{:S(2)}, u32[]{:S(2)}) collective-permute-start(f32[32,16,128]{2,1,0:T(8,128)S(1)} %pad_maximum_fusion.5), channel_id=1, source_target_pairs={{0,1},{1,2},{2,3},{3,0},{4,5},{5,6},{6,7},{7,4},{8,9},{9,10},{10,1... | collective-permute-start | bytes 786440 | tf_op jit(solution)/shard_map/ppermute | solution.py:367
  53.7 14.5 %slice-start = ((s8[4259840]{0:T(1024)(128)(4,1)}), s8[4194304]{0:T(1024)(128)(4,1)S(1)}, s32[]{:S(2)}) async-start(s8[4259840]{0:T(1024)(128)(4,1)} %bitcast.8), calls=%async_computation | async-start | bytes 8388608
  54.0 14.3 %slice-start.1 = ((s8[4259840]{0:T(1024)(128)(4,1)}), s8[65536]{0:T(1024)(128)(4,1)S(1)}, s32[]{:S(2)}) async-start(s8[4259840]{0:T(1024)(128)(4,1)} %bitcast.8), calls=%async_computation.1 | async-start | bytes 131072
  85.3 28.4 %copy-start.13 = (bf16[240,256]{1,0:T(8,128)(2,1)S(1)}, bf16[240,256]{1,0:T(8,128)(2,1)}, u32[]{:S(2)}) copy-start(bf16[240,256]{1,0:T(8,128)(2,1)} %constant.32.clone.table_ref) | copy-start | bytes 368644
  125.8 52.1 %copy-start.3 = (f32[64,128,128]{2,1,0:T(8,128)S(1)}, f32[64,128,128]{2,1,0:T(8,128)}, u32[]{:S(2)}) copy-start(f32[64,128,128]{2,1,0:T(8,128)} %refs_0_.1) | copy-start | bytes 12582916
  126.1 48.3 %collective-permute-start.8 = (f32[16,128,128]{2,1,0:T(8,128)S(1)}, f32[16,128,128]{2,1,0:T(8,128)S(1)}, u32[]{:S(2)}, u32[]{:S(2)}) collective-permute-start(f32[16,128,128]{2,1,0:T(8,128)S(1)} %get-tuple-element.6), channel_id=1, source_target_pairs={{4,0},{8,4},{12,8},{16,12},{20,16},{24,20},{28,24},{0,28},{5,1},{9... | collective-permute-start | bytes 3145736 | tf_op jit(solution)/shard_map/ppermute | solution.py:366
  130.5 44.1 %collective-permute-start.9 = (f32[16,128,128]{2,1,0:T(8,128)S(1)}, f32[16,128,128]{2,1,0:T(8,128)S(1)}, u32[]{:S(2)}, u32[]{:S(2)}) collective-permute-start(f32[16,128,128]{2,1,0:T(8,128)S(1)} %get-tuple-element.5), channel_id=1, source_target_pairs={{0,4},{4,8},{8,12},{12,16},{16,20},{20,24},{24,28},{28,0},{1,5},{5... | collective-permute-start | bytes 3145736 | tf_op jit(solution)/shard_map/ppermute | solution.py:367
  132.4 45.5 %slice-start.3 = ((f32[16,128,128]{2,1,0:T(8,128)}), f32[1,128,128]{2,1,0:T(8,128)S(1)}, s32[]{:S(2)}) async-start(f32[16,128,128]{2,1,0:T(8,128)} %copy-done.9), calls=%async_computation.3 | async-start | bytes 131072 | tf_op jit(solution)/shard_map/slice | solution.py:432
  132.4 45.5 %slice-start.2 = ((f32[16,128,128]{2,1,0:T(8,128)}), f32[1,128,128]{2,1,0:T(8,128)S(1)}, s32[]{:S(2)}) async-start(f32[16,128,128]{2,1,0:T(8,128)} %copy-done.8), calls=%async_computation.2 | async-start | bytes 131072 | tf_op jit(solution)/shard_map/slice | solution.py:434
  132.5 68.6 %collective-permute-start.6 = (f32[64,16,128]{2,1,0:T(8,128)S(1)}, f32[64,16,128]{2,1,0:T(8,128)S(1)}, u32[]{:S(2)}, u32[]{:S(2)}) collective-permute-start(f32[64,16,128]{2,1,0:T(8,128)S(1)} %get-tuple-element.7), channel_id=1, source_target_pairs={{1,0},{2,1},{3,2},{0,3},{5,4},{6,5},{7,6},{4,7},{9,8},{10,9},{11,1... | collective-permute-start | bytes 1572872 | tf_op jit(solution)/shard_map/ppermute | solution.py:366
  132.6 68.6 %collective-permute-start.7 = (f32[64,16,128]{2,1,0:T(8,128)S(1)}, f32[64,16,128]{2,1,0:T(8,128)S(1)}, u32[]{:S(2)}, u32[]{:S(2)}) collective-permute-start(f32[64,16,128]{2,1,0:T(8,128)S(1)} %get-tuple-element.8), channel_id=1, source_target_pairs={{0,1},{1,2},{2,3},{3,0},{4,5},{5,6},{6,7},{7,4},{8,9},{9,10},{10,1... | collective-permute-start | bytes 1572872 | tf_op jit(solution)/shard_map/ppermute | solution.py:367
  175.4 43.1 %collective-permute-start.10 = (f32[32,16,128]{2,1,0:T(8,128)}, f32[32,16,128]{2,1,0:T(8,128)}, u32[]{:S(2)}, u32[]{:S(2)}) collective-permute-start(f32[32,16,128]{2,1,0:T(8,128)} %pad_maximum_fusion.6), channel_id=1, source_target_pairs={{1,0},{2,1},{3,2},{0,3},{5,4},{6,5},{7,6},{4,7},{9,8},{10,9},{11,1... | collective-permute-start | bytes 786440 | tf_op jit(solution)/shard_map/ppermute | solution.py:366
  176.5 42.0 %collective-permute-start.11 = (f32[32,16,128]{2,1,0:T(8,128)}, f32[32,16,128]{2,1,0:T(8,128)S(1)}, u32[]{:S(2)}, u32[]{:S(2)}) collective-permute-start(f32[32,16,128]{2,1,0:T(8,128)} %pad_maximum_fusion.7), channel_id=1, source_target_pairs={{0,1},{1,2},{2,3},{3,0},{4,5},{5,6},{6,7},{7,4},{8,9},{9,10},{10,1... | collective-permute-start | bytes 786440 | tf_op jit(solution)/shard_map/ppermute | solution.py:367
  209.0 12.2 %copy-start.17 = (bf16[768,256]{1,0:T(8,128)(2,1)S(1)}, bf16[768,256]{1,0:T(8,128)(2,1)}, u32[]{:S(2)}) copy-start(bf16[768,256]{1,0:T(8,128)(2,1)} %constant.29.clone.rows_out) | copy-start | bytes 1179652
  209.0 12.3 %copy-start.20 = (bf16[768,128]{1,0:T(8,128)(2,1)S(1)}, bf16[768,128]{1,0:T(8,128)(2,1)}, u32[]{:S(2)}) copy-start(bf16[768,128]{1,0:T(8,128)(2,1)} %constant.31.clone.rows_home) | copy-start | bytes 589828
  221.3 28.7 %copy-start.6 = (f32[64,128,128]{2,1,0:T(8,128)S(1)}, f32[64,128,128]{2,1,0:T(8,128)}, u32[]{:S(2)}) copy-start(f32[64,128,128]{2,1,0:T(8,128)} %copy-done.5) | copy-start | bytes 12582916
  221.3 41.4 %copy-start.1 = (f32[32,32,32]{2,1,0:T(8,128)S(1)}, f32[32,32,32]{2,1,0:T(8,128)}, u32[]{:S(2)}) copy-start(f32[32,32,32]{2,1,0:T(8,128)} %param.15) | copy-start | bytes 393220
  (9 other events, 56.1 us)

commit v6 on v5

--- a/solution.py
+++ b/solution.py
@@ -368,23 +368,23 @@
     )
 
 
-def halos(block, width):
+def convolved(plan, block, gains, adjoint, beside_rows):
+    width = plan.half
     rows = neighbours("px", block[:width], block[-width:])
     cols = jnp.concatenate(neighbours("py", block[:, :width], block[:, -width:]), 1)
+    own = cols_out(
+        plan, depth_out(plan, "depth_own", block), depth_out(plan, "depth_cols", cols)
+    )
+    rows, own, beside_rows = lax.optimization_barrier((rows, own, beside_rows))
     first = jnp.concatenate([part[:, :width] for part in rows], 0)
     last = jnp.concatenate([part[:, -width:] for part in rows], 0)
     corners = jnp.concatenate(neighbours("py", first, last), 1)
-    return rows, cols, corners
-
-
-def convolved(plan, block, around, gains, adjoint):
-    rows, cols, corners = around
-    own = cols_out(
-        plan, depth_out(plan, "depth_own", block), depth_out(plan, "depth_cols", cols)
-    )
     inner = depth_out(plan, "depth_rows", *rows)
     outer = depth_out(plan, "depth_corners", corners)
-    return filtered(plan, own, inner, outer, gains, adjoint)
+    if gains is None:
+        gains = beside_rows
+    modes = filtered(plan, own, inner, outer, gains, adjoint)
+    return modes, (rows, cols, corners), beside_rows
 
 
 def variation_kernel(whole, volume_ref, out_ref):
@@ -460,13 +460,10 @@
 def shards(estimate, observed, psf):
     rows, cols, depth = estimate.shape
     plan = Plan(rows, cols, depth, psf.shape[0])
-    around = halos(estimate, plan.half)
-    gains = transfer(plan, psf)
-    modes = convolved(plan, estimate, around, gains, False)
+    modes, around, gains = convolved(plan, estimate, None, False, transfer(plan, psf))
     quotient = depth_home(plan, modes, observed, True)
-    quotient_around = halos(quotient, plan.half)
     weight = weighted(estimate, around)
-    modes = convolved(plan, quotient, quotient_around, gains, True)
+    modes, _, weight = convolved(plan, quotient, gains, True, weight)
     return depth_home(plan, modes, weight, False)
 
 

time: 264 us -> 217 us (0.82)
  waiting for transfers between devices: 62.5 us -> 12.8 us
  local copies, waits for them, and re-layouts: 16 us -> 18.9 us
    ppermute x6, waiting for transfers between devices: 61.3 us -> 3.69 us  [neighbours(): lax.ppermute(after, axis, [((i + 1) % count, i) for i in range(count)])]
    ppermute x6, waiting for transfers between devices: 1.2 us -> 9.11 us  [neighbours(): lax.ppermute(before, axis, [(i, (i + 1) % count) for i in range(count)])]
    ppermute x6, starting transfers between devices: 5.51 us -> 8.34 us  [neighbours(): lax.ppermute(before, axis, [(i, (i + 1) % count) for i in range(count)])]
    slice x8 -> x7, local copies, waits for them, and re-layouts: 5.76 us -> 8.06 us  [the longest x2 4.68 us: convolved(): rows = neighbours('px', block[:width], block[-width:])]
  transfers between devices with their start and end apart: 12 -> 12, of which waited for: 4 -> 3; matrix products, arithmetic and copies ran while one was open for 6% -> 7% of each run, Pallas kernels for 28% -> 34%
where the time goes in v6:
time: 217 us; the launch traced here: 215 us
  Pallas kernels  158 us (73%)
  local copies, waits for them, and re-layouts  18.9 us (9%)
  starting transfers between devices  17.2 us (8%)
  waiting for transfers between devices  12.8 us (6%)
  other arithmetic  6.62 us (3%)
    pallas_call x2, Pallas kernels, filtered(): pl.pallas_call(functools.partial(filter_kernel, adjoint), grid=(plan.mode...  57.1 us
    pallas_call x8, Pallas kernels, depth_out(): pl.pallas_call(functools.partial(depth_out_kernel, plan, len(pieces)), gr...  46 us
    pallas_call x2, Pallas kernels, depth_home(): pl.pallas_call(functools.partial(depth_home_kernel, plan, divide), grid=(...  24.8 us
    pallas_call x2, Pallas kernels, cols_out(): pl.pallas_call(cols_kernel, grid=(plan.modes // step,), in_specs=[spec(pl...  11.3 us
    pallas_call x1, Pallas kernels, transfer(): pl.pallas_call(transfer_kernel, grid=(plan.modes // step,), in_specs=[pl....  11 us
    ppermute x6, waiting for transfers between devices, neighbours(): lax.ppermute(before, axis, [(i, (i + 1) % count) for i in range(count)])  9.11 us
    ppermute x6, starting transfers between devices, neighbours(): lax.ppermute(after, axis, [((i + 1) % count, i) for i in range(count)])  8.9 us
    ppermute x6, starting transfers between devices, neighbours(): lax.ppermute(before, axis, [(i, (i + 1) % count) for i in range(count)])  8.34 us
  transfers between devices with their start and end apart: 12, of which 3 were waited for; matrix products, arithmetic and copies ran while one was open for 7% of the time, Pallas kernels for 34%

profile of v6, /device:TPU:1, one launch (start us, length us, event | category | flops | bytes accessed | tf_op | source)
XLA Modules:
  0.0 215.1 jit_solution(11329281185985337298)
XLA Ops:
  0.0 3.2 %fusion.3 = (f32[16,128,128]{2,1,0:T(8,128)}, f32[16,128,128]{2,1,0:T(8,128)}) fusion(f32[64,128,128]{2,1,0:T(8,128)} %refs_0_.1), kind=kLoop, calls=%fused_computation.15 | loop fusion | bytes 4194304 | tf_op jit(solution)/shard_map/slice | solution.py:373
  3.2 2.1 collective-permute-start.1
  5.2 3.0 %collective-permute-start = (f32[16,128,128]{2,1,0:T(8,128)}, f32[16,128,128]{2,1,0:T(8,128)S(1)}, u32[]{:S(2)}, u32[]{:S(2)}) collective-permute-start(f32[16,128,128]{2,1,0:T(8,128)} %get-tuple-element.28), channel_id=1, source_target_pairs={{4,0},{8,4},{12,8},{16,12},{20,16},{24,20},{28,24},{0,28},{5,1},{9... | collective-permute-start | bytes 3145736 | tf_op jit(solution)/shard_map/ppermute | solution.py:366
  8.3 2.3 %fusion.2 = (f32[64,16,128]{2,1,0:T(8,128)}, f32[64,16,128]{2,1,0:T(8,128)}) fusion(f32[64,128,128]{2,1,0:T(8,128)} %refs_0_.1), kind=kLoop, calls=%fused_computation.14 | loop fusion | bytes 2097152 | tf_op jit(solution)/shard_map/slice | solution.py:374
  13.3 1.9 copy.15
  15.8 1.9 copy.14
  17.7 2.2 %copy-done.2 = f32[64,128,128]{2,1,0:T(8,128)S(1)} copy-done((f32[64,128,128]{2,1,0:T(8,128)S(1)}, f32[64,128,128]{2,1,0:T(8,128)}, u32[]{:S(2)}) %copy-start.2) | copy-done | bytes 4194328
  19.9 9.8 %depth_own.2.inner_ref = f32[65,128,128]{2,1,0:T(8,128)} custom-call(f32[64,128,128]{2,1,0:T(8,128)S(1)} %copy-done.2, bf16[144,384]{1,0:T(8,128)(2,1)S(1)} %copy-done.6), custom_call_target="tpu_custom_call" | custom-call | flops 1000000 | bytes 100000 | tf_op jit(solution)/shard_map/depth_own/pallas_call | solution.py:164
  30.6 11.0 %transfer.1.transfer_ref = f32[65,160,256]{2,1,0:T(8,128)} custom-call(f32[65,32,256]{2,1,0:T(8,128)S(1)} %select_maximum_fusion.psf_ref, bf16[768,256]{1,0:T(8,128)(2,1)S(1)} %copy-done.11, bf16[320,96]{1,0:T(8,128)(2,1)S(1)} %copy-done.12), custom_call_target="tpu_custom_call" | custom-call | flops 1000000 | bytes 100000 | tf_op jit(solution)/shard_map/transfer/pallas_call | solution.py:259
  41.6 1.4 pad_maximum_fusion.refs_0_
  43.0 1.9 depth_cols.2.outer_ref
  44.9 5.6 %cols_out.4.own_ref = f32[65,160,128]{2,1,0:T(8,128)} custom-call(f32[65,128,128]{2,1,0:T(8,128)S(1)} %bitcast.11, f32[65,32,128]{2,1,0:T(8,128)S(1)} %depth_cols.2.outer_ref, bf16[320,480]{1,0:T(8,128)(2,1)S(1)} %copy-done.9), custom_call_target="tpu_custom_call" | custom-call | flops 1000000 | bytes 100000 | tf_op jit(solution)/shard_map/cols_out/pallas_call | solution.py:209
  51.7 3.0 %collective-permute-start.5 = (f32[32,16,128]{2,1,0:T(8,128)S(1)}, f32[32,16,128]{2,1,0:T(8,128)S(1)}, u32[]{:S(2)}, u32[]{:S(2)}) collective-permute-start(f32[32,16,128]{2,1,0:T(8,128)S(1)} %pad_maximum_fusion.5), channel_id=1, source_target_pairs={{0,1},{1,2},{2,3},{3,0},{4,5},{5,6},{6,7},{7,4},{8,9},{9,10},{10,1... | collective-permute-start | bytes 786440 | tf_op jit(solution)/shard_map/ppermute | solution.py:367
  56.8 9.5 %depth_rows.2.inner_ref = f32[65,128,128]{2,1,0:T(8,128)} custom-call(f32[16,128,128]{2,1,0:T(8,128)S(1)} %collective-permute-done.refs_0_, f32[16,128,128]{2,1,0:T(8,128)S(1)} %collective-permute-done.1.refs_1_, bf16[144,384]{1,0:T(8,128)(2,1)S(1)} %copy-done.6), custom_call_target="tpu_custom_call" | custom-call | flops 1000000 | bytes 100000 | tf_op jit(solution)/shard_map/depth_rows/pallas_call | solution.py:164
  66.4 1.7 depth_corners.2.outer_ref
  68.2 28.4 %filtered.2.modes_ref = f32[65,128,128]{2,1,0:T(8,128)} custom-call(f32[65,160,128]{2,1,0:T(8,128)} %cols_out.4.own_ref, f32[65,128,128]{2,1,0:T(8,128)} %depth_rows.2.inner_ref, f32[65,32,128]{2,1,0:T(8,128)S(1)} %depth_corners.2.outer_ref, f32[65,160,256]{2,1,0:T(8,128)} %transfer.1.transfer_ref, bf16[768,256]{1,0:T(8,128)(2,1)S(1)} %copy-done.13, ...), custom_call_target="tpu_custom_call" | custom-call | flops 22000001024 | bytes 25000000 | tf_op jit(solution)/shard_map/filtered/pallas_call | solution.py:316
  96.6 12.1 %depth_home.2.refs_0_ = f32[64,128,128]{2,1,0:T(8,128)S(1)} custom-call(f32[65,128,128]{2,1,0:T(8,128)} %filtered.2.modes_ref, f32[64,128,128]{2,1,0:T(8,128)} %other_ref.1, bf16[240,256]{1,0:T(8,128)(2,1)S(1)} %copy-done.10), custom_call_target="tpu_custom_call" | custom-call | flops 3000000000 | bytes 13000000 | tf_op jit(solution)/shard_map/depth_home/pallas_call | solution.py:347
  109.8 1.5 fusion.1
  113.1 4.2 %collective-permute-start.6 = (f32[16,128,128]{2,1,0:T(8,128)}, f32[16,128,128]{2,1,0:T(8,128)S(1)}, u32[]{:S(2)}, u32[]{:S(2)}) collective-permute-start(f32[16,128,128]{2,1,0:T(8,128)} %get-tuple-element.24), channel_id=1, source_target_pairs={{4,0},{8,4},{12,8},{16,12},{20,16},{24,20},{28,24},{0,28},{5,1},{9... | collective-permute-start | bytes 3145736 | tf_op jit(solution)/shard_map/ppermute | solution.py:366
  117.3 9.9 %depth_own.3.inner_ref = f32[65,128,128]{2,1,0:T(8,128)} custom-call(f32[64,128,128]{2,1,0:T(8,128)S(1)} %depth_home.2.refs_0_, bf16[144,384]{1,0:T(8,128)(2,1)S(1)} %copy-done.6), custom_call_target="tpu_custom_call" | custom-call | flops 1000000 | bytes 100000 | tf_op jit(solution)/shard_map/depth_own/pallas_call | solution.py:164
  127.2 3.6 %maximum_maximum_fusion.volume_ref = f32[66,136,128]{2,1,0:T(8,128)} fusion(f32[1,7,128]{2,1,0:T(8,128)S(1)} %get-tuple-element.40, f32[1,1,128]{2,1,0:T(1,128)S(1)} %get-tuple-element.38, f32[1,128,128]{2,1,0:T(8,128)S(1)} %slice-done.5, f32[64,7,128]{2,1,0:T(8,128)S(1)} %slice.113, f32[64,1,128]{2,1,0:T(1,128)S(1)} %slice.112, ...), kind=kLoop, calls=%fused_computation | loop fusion | flops 9191424 | bytes 9191424 | tf_op jit(solution)/shard_map/concatenate | solution.py:437
  130.8 7.9 %weighted.1.other_ref = f32[64,128,128]{2,1,0:T(8,128)S(1)} custom-call(f32[66,136,128]{2,1,0:T(8,128)} %maximum_maximum_fusion.volume_ref), custom_call_target="tpu_custom_call" | custom-call | flops 1000000 | bytes 100000 | tf_op jit(solution)/shard_map/weighted/pallas_call | solution.py:448
  138.7 2.0 copy-done.4
  140.7 1.3 pad_maximum_fusion.1.refs_0_
  142.0 1.9 depth_cols.3.outer_ref
  143.9 5.6 %cols_out.5.own_ref = f32[65,160,128]{2,1,0:T(8,128)} custom-call(f32[65,128,128]{2,1,0:T(8,128)S(1)} %bitcast.9, f32[65,32,128]{2,1,0:T(8,128)S(1)} %depth_cols.3.outer_ref, bf16[320,480]{1,0:T(8,128)(2,1)S(1)} %copy-done.9), custom_call_target="tpu_custom_call" | custom-call | flops 1000000 | bytes 100000 | tf_op jit(solution)/shard_map/cols_out/pallas_call | solution.py:209
  149.6 9.1 %collective-permute-done.7.refs_1_ = f32[16,128,128]{2,1,0:T(8,128)S(1)} collective-permute-done((f32[16,128,128]{2,1,0:T(8,128)}, f32[16,128,128]{2,1,0:T(8,128)S(1)}, u32[]{:S(2)}, u32[]{:S(2)}) %collective-permute-start.7) | collective-permute-done | bytes 1048608 | tf_op jit(solution)/shard_map/ppermute | solution.py:367
  158.7 2.6 %collective-permute-done.6.refs_0_ = f32[16,128,128]{2,1,0:T(8,128)S(1)} collective-permute-done((f32[16,128,128]{2,1,0:T(8,128)}, f32[16,128,128]{2,1,0:T(8,128)S(1)}, u32[]{:S(2)}, u32[]{:S(2)}) %collective-permute-start.6) | collective-permute-done | bytes 1048608 | tf_op jit(solution)/shard_map/ppermute | solution.py:366
  162.4 9.5 %depth_rows.3.inner_ref = f32[65,128,128]{2,1,0:T(8,128)} custom-call(f32[16,128,128]{2,1,0:T(8,128)S(1)} %collective-permute-done.6.refs_0_, f32[16,128,128]{2,1,0:T(8,128)S(1)} %collective-permute-done.7.refs_1_, bf16[144,384]{1,0:T(8,128)(2,1)S(1)} %copy-done.6), custom_call_target="tpu_custom_call" | custom-call | flops 1000000 | bytes 100000 | tf_op jit(solution)/shard_map/depth_rows/pallas_call | solution.py:164
  172.0 1.7 depth_corners.3.outer_ref
  173.7 28.7 %filtered.3.modes_ref = f32[65,128,128]{2,1,0:T(8,128)} custom-call(f32[65,160,128]{2,1,0:T(8,128)} %cols_out.5.own_ref, f32[65,128,128]{2,1,0:T(8,128)} %depth_rows.3.inner_ref, f32[65,32,128]{2,1,0:T(8,128)S(1)} %depth_corners.3.outer_ref, f32[65,160,256]{2,1,0:T(8,128)} %transfer.1.transfer_ref, bf16[768,256]{1,0:T(8,128)(2,1)S(1)} %copy-done.13, ...), custom_call_target="tpu_custom_call" | custom-call | flops 22000001024 | bytes 25000000 | tf_op jit(solution)/shard_map/filtered/pallas_call | solution.py:316
  202.4 12.7 %depth_home.3 = f32[64,128,128]{2,1,0:T(8,128)} custom-call(f32[65,128,128]{2,1,0:T(8,128)} %filtered.3.modes_ref, f32[64,128,128]{2,1,0:T(8,128)S(1)} %copy-done.5, bf16[240,256]{1,0:T(8,128)(2,1)S(1)} %copy-done.10), custom_call_target="tpu_custom_call" | custom-call | flops 3000000000 | bytes 13000000 | tf_op jit(solution)/shard_map/depth_home/pallas_call | solution.py:347
  (89 shorter events, 11.5 us)
Async XLA Ops:
  0.0 12.8 %copy-start = (f32[32,32,32]{2,1,0:T(8,128)S(1)}, f32[32,32,32]{2,1,0:T(8,128)}, u32[]{:S(2)}) copy-start(f32[32,32,32]{2,1,0:T(8,128)} %param.15) | copy-start | bytes 393220
  0.0 12.8 %copy-start.19 = (f32[32,65,1]{1,0,2:T(8,128)S(1)}, f32[32,65,1]{1,0,2:T(8,128)}, u32[]{:S(2)}) copy-start(f32[32,65,1]{1,0,2:T(8,128)} %constant.38) | copy-start | bytes 24964
  0.0 15.2 %copy-start.20 = (f32[32,65,1]{1,0,2:T(8,128)S(1)}, f32[32,65,1]{1,0,2:T(8,128)}, u32[]{:S(2)}) copy-start(f32[32,65,1]{1,0,2:T(8,128)} %constant.37) | copy-start | bytes 24964
  3.2 14.5 %copy-start.6 = (bf16[144,384]{1,0:T(8,128)(2,1)S(1)}, bf16[144,384]{1,0:T(8,128)(2,1)}, u32[]{:S(2)}) copy-start(bf16[144,384]{1,0:T(8,128)(2,1)} %constant.27.clone.refs_1_.refs_2_) | copy-start | bytes 331780
  3.2 47.4 %collective-permute-start.1 = (f32[16,128,128]{2,1,0:T(8,128)}, f32[16,128,128]{2,1,0:T(8,128)S(1)}, u32[]{:S(2)}, u32[]{:S(2)}) collective-permute-start(f32[16,128,128]{2,1,0:T(8,128)} %get-tuple-element.27), channel_id=1, source_target_pairs={{0,4},{4,8},{8,12},{12,16},{16,20},{20,24},{24,28},{28,0},{1,5},{5... | collective-permute-start | bytes 3145736 | tf_op jit(solution)/shard_map/ppermute | solution.py:367
  5.2 46.4 %collective-permute-start = (f32[16,128,128]{2,1,0:T(8,128)}, f32[16,128,128]{2,1,0:T(8,128)S(1)}, u32[]{:S(2)}, u32[]{:S(2)}) collective-permute-start(f32[16,128,128]{2,1,0:T(8,128)} %get-tuple-element.28), channel_id=1, source_target_pairs={{4,0},{8,4},{12,8},{16,12},{20,16},{24,20},{28,24},{0,28},{5,1},{9... | collective-permute-start | bytes 3145736 | tf_op jit(solution)/shard_map/ppermute | solution.py:366
  10.5 31.1 %collective-permute-start.2 = (f32[64,16,128]{2,1,0:T(8,128)}, f32[64,16,128]{2,1,0:T(8,128)}, u32[]{:S(2)}, u32[]{:S(2)}) collective-permute-start(f32[64,16,128]{2,1,0:T(8,128)} %get-tuple-element.25), channel_id=1, source_target_pairs={{1,0},{2,1},{3,2},{0,3},{5,4},{6,5},{7,6},{4,7},{9,8},{10,9},{11,1... | collective-permute-start | bytes 1572872 | tf_op jit(solution)/shard_map/ppermute | solution.py:366
  11.5 30.1 %collective-permute-start.3 = (f32[64,16,128]{2,1,0:T(8,128)}, f32[64,16,128]{2,1,0:T(8,128)}, u32[]{:S(2)}, u32[]{:S(2)}) collective-permute-start(f32[64,16,128]{2,1,0:T(8,128)} %get-tuple-element.26), channel_id=1, source_target_pairs={{0,1},{1,2},{2,3},{3,0},{4,5},{5,6},{6,7},{7,4},{8,9},{9,10},{10,1... | collective-permute-start | bytes 1572872 | tf_op jit(solution)/shard_map/ppermute | solution.py:367
  29.6 15.2 %slice-start.2 = ((s8[4259840]{0:T(1024)(128)(4,1)}), s8[4194304]{0:T(1024)(128)(4,1)S(1)}, s32[]{:S(2)}) async-start(s8[4259840]{0:T(1024)(128)(4,1)} %bitcast.10), calls=%async_computation.2 | async-start | bytes 8388608
  30.6 14.3 %slice-start.3 = ((s8[4259840]{0:T(1024)(128)(4,1)}), s8[65536]{0:T(1024)(128)(4,1)S(1)}, s32[]{:S(2)}) async-start(s8[4259840]{0:T(1024)(128)(4,1)} %bitcast.10), calls=%async_computation.3 | async-start | bytes 131072
  50.6 15.8 %copy-start.7 = (f32[16,128,128]{2,1,0:T(8,128)}, f32[16,128,128]{2,1,0:T(8,128)S(1)}, u32[]{:S(2)}) copy-start(f32[16,128,128]{2,1,0:T(8,128)S(1)} %collective-permute-done.1.refs_1_) | copy-start | bytes 3145732
  51.6 14.7 %copy-start.8 = (f32[16,128,128]{2,1,0:T(8,128)}, f32[16,128,128]{2,1,0:T(8,128)S(1)}, u32[]{:S(2)}) copy-start(f32[16,128,128]{2,1,0:T(8,128)S(1)} %collective-permute-done.refs_0_) | copy-start | bytes 3145732
  51.7 14.6 %collective-permute-start.5 = (f32[32,16,128]{2,1,0:T(8,128)S(1)}, f32[32,16,128]{2,1,0:T(8,128)S(1)}, u32[]{:S(2)}, u32[]{:S(2)}) collective-permute-start(f32[32,16,128]{2,1,0:T(8,128)S(1)} %pad_maximum_fusion.5), channel_id=1, source_target_pairs={{0,1},{1,2},{2,3},{3,0},{4,5},{5,6},{6,7},{7,4},{8,9},{9,10},{10,1... | collective-permute-start | bytes 786440 | tf_op jit(solution)/shard_map/ppermute | solution.py:367
  54.7 11.6 %collective-permute-start.4 = (f32[32,16,128]{2,1,0:T(8,128)S(1)}, f32[32,16,128]{2,1,0:T(8,128)S(1)}, u32[]{:S(2)}, u32[]{:S(2)}) collective-permute-start(f32[32,16,128]{2,1,0:T(8,128)S(1)} %pad_maximum_fusion.4), channel_id=1, source_target_pairs={{1,0},{2,1},{3,2},{0,3},{5,4},{6,5},{7,6},{4,7},{9,8},{10,9},{11,1... | collective-permute-start | bytes 786440 | tf_op jit(solution)/shard_map/ppermute | solution.py:366
  56.8 11.4 %copy-start.13 = (bf16[768,256]{1,0:T(8,128)(2,1)S(1)}, bf16[768,256]{1,0:T(8,128)(2,1)}, u32[]{:S(2)}) copy-start(bf16[768,256]{1,0:T(8,128)(2,1)} %constant.29.clone.rows_out) | copy-start | bytes 1179652
  56.8 11.4 %copy-start.14 = (bf16[256,480]{1,0:T(8,128)(2,1)S(1)}, bf16[256,480]{1,0:T(8,128)(2,1)}, u32[]{:S(2)}) copy-start(bf16[256,480]{1,0:T(8,128)(2,1)} %constant.30.clone.cols_home) | copy-start | bytes 737284
  56.8 11.4 %copy-start.15 = (bf16[768,128]{1,0:T(8,128)(2,1)S(1)}, bf16[768,128]{1,0:T(8,128)(2,1)}, u32[]{:S(2)}) copy-start(bf16[768,128]{1,0:T(8,128)(2,1)} %constant.31.clone.rows_home) | copy-start | bytes 589828
  68.2 28.5 %copy-start.10 = (bf16[240,256]{1,0:T(8,128)(2,1)S(1)}, bf16[240,256]{1,0:T(8,128)(2,1)}, u32[]{:S(2)}) copy-start(bf16[240,256]{1,0:T(8,128)(2,1)} %constant.32.clone.table_ref) | copy-start | bytes 368644
  111.3 29.4 %collective-permute-start.8 = (f32[64,16,128]{2,1,0:T(8,128)}, f32[64,16,128]{2,1,0:T(8,128)}, u32[]{:S(2)}, u32[]{:S(2)}) collective-permute-start(f32[64,16,128]{2,1,0:T(8,128)} %get-tuple-element.21), channel_id=1, source_target_pairs={{1,0},{2,1},{3,2},{0,3},{5,4},{6,5},{7,6},{4,7},{9,8},{10,9},{11,1... | collective-permute-start | bytes 1572872 | tf_op jit(solution)/shard_map/ppermute | solution.py:366
  112.0 28.7 %collective-permute-start.9 = (f32[64,16,128]{2,1,0:T(8,128)}, f32[64,16,128]{2,1,0:T(8,128)}, u32[]{:S(2)}, u32[]{:S(2)}) collective-permute-start(f32[64,16,128]{2,1,0:T(8,128)} %get-tuple-element.22), channel_id=1, source_target_pairs={{0,1},{1,2},{2,3},{3,0},{4,5},{5,6},{6,7},{7,4},{8,9},{9,10},{10,1... | collective-permute-start | bytes 1572872 | tf_op jit(solution)/shard_map/ppermute | solution.py:367
  113.1 45.6 %collective-permute-start.7 = (f32[16,128,128]{2,1,0:T(8,128)}, f32[16,128,128]{2,1,0:T(8,128)S(1)}, u32[]{:S(2)}, u32[]{:S(2)}) collective-permute-start(f32[16,128,128]{2,1,0:T(8,128)} %get-tuple-element.23), channel_id=1, source_target_pairs={{0,4},{4,8},{8,12},{12,16},{16,20},{20,24},{24,28},{28,0},{1,5},{5... | collective-permute-start | bytes 3145736 | tf_op jit(solution)/shard_map/ppermute | solution.py:367
  113.1 48.2 %collective-permute-start.6 = (f32[16,128,128]{2,1,0:T(8,128)}, f32[16,128,128]{2,1,0:T(8,128)S(1)}, u32[]{:S(2)}, u32[]{:S(2)}) collective-permute-start(f32[16,128,128]{2,1,0:T(8,128)} %get-tuple-element.24), channel_id=1, source_target_pairs={{4,0},{8,4},{12,8},{16,12},{20,16},{24,20},{28,24},{0,28},{5,1},{9... | collective-permute-start | bytes 3145736 | tf_op jit(solution)/shard_map/ppermute | solution.py:366
  117.2 10.0 %copy-start.3 = (f32[64,128,128]{2,1,0:T(8,128)S(1)}, f32[64,128,128]{2,1,0:T(8,128)}, u32[]{:S(2)}) copy-start(f32[64,128,128]{2,1,0:T(8,128)} %refs_0_.1) | copy-start | bytes 12582916
  117.2 10.0 %slice-start.4 = ((f32[16,128,128]{2,1,0:T(8,128)}), f32[1,128,128]{2,1,0:T(8,128)S(1)}, s32[]{:S(2)}) async-start(f32[16,128,128]{2,1,0:T(8,128)} %copy-done.7), calls=%async_computation.4 | async-start | bytes 131072 | tf_op jit(solution)/shard_map/slice | solution.py:432
  117.2 10.0 %slice-start.5 = ((f32[16,128,128]{2,1,0:T(8,128)}), f32[1,128,128]{2,1,0:T(8,128)S(1)}, s32[]{:S(2)}) async-start(f32[16,128,128]{2,1,0:T(8,128)} %copy-done.8), calls=%async_computation.5 | async-start | bytes 131072 | tf_op jit(solution)/shard_map/slice | solution.py:434
  127.2 16.7 %slice-start = ((s8[4259840]{0:T(1024)(128)(4,1)}), s8[65536]{0:T(1024)(128)(4,1)S(1)}, s32[]{:S(2)}) async-start(s8[4259840]{0:T(1024)(128)(4,1)} %bitcast.8), calls=%async_computation | async-start | bytes 131072
  130.8 13.2 %slice-start.1 = ((s8[4259840]{0:T(1024)(128)(4,1)}), s8[4194304]{0:T(1024)(128)(4,1)S(1)}, s32[]{:S(2)}) async-start(s8[4259840]{0:T(1024)(128)(4,1)} %bitcast.8), calls=%async_computation.1 | async-start | bytes 8388608
  161.4 10.5 %collective-permute-start.11 = (f32[32,16,128]{2,1,0:T(8,128)S(1)}, f32[32,16,128]{2,1,0:T(8,128)S(1)}, u32[]{:S(2)}, u32[]{:S(2)}) collective-permute-start(f32[32,16,128]{2,1,0:T(8,128)S(1)} %pad_maximum_fusion.7), channel_id=1, source_target_pairs={{0,1},{1,2},{2,3},{3,0},{4,5},{5,6},{6,7},{7,4},{8,9},{9,10},{10,1... | collective-permute-start | bytes 786440 | tf_op jit(solution)/shard_map/ppermute | solution.py:367
  162.3 11.4 %copy-start.16 = (bf16[768,128]{1,0:T(8,128)(2,1)S(1)}, bf16[768,128]{1,0:T(8,128)(2,1)}, u32[]{:S(2)}) copy-start(bf16[768,128]{1,0:T(8,128)(2,1)} %constant.31.clone.rows_home) | copy-start | bytes 589828
  162.3 9.6 %collective-permute-start.10 = (f32[32,16,128]{2,1,0:T(8,128)S(1)}, f32[32,16,128]{2,1,0:T(8,128)S(1)}, u32[]{:S(2)}, u32[]{:S(2)}) collective-permute-start(f32[32,16,128]{2,1,0:T(8,128)S(1)} %pad_maximum_fusion.6), channel_id=1, source_target_pairs={{1,0},{2,1},{3,2},{0,3},{5,4},{6,5},{7,6},{4,7},{9,8},{10,9},{11,1... | collective-permute-start | bytes 786440 | tf_op jit(solution)/shard_map/ppermute | solution.py:366
  173.7 28.7 %copy-start.5 = (f32[64,128,128]{2,1,0:T(8,128)S(1)}, f32[64,128,128]{2,1,0:T(8,128)}, u32[]{:S(2)}) copy-start(f32[64,128,128]{2,1,0:T(8,128)} %copy-done.4) | copy-start | bytes 12582916
  173.7 41.4 %copy-start.1 = (f32[32,32,32]{2,1,0:T(8,128)S(1)}, f32[32,32,32]{2,1,0:T(8,128)}, u32[]{:S(2)}) copy-start(f32[32,32,32]{2,1,0:T(8,128)} %param.15) | copy-start | bytes 393220
  (7 other events, 29.1 us)
